TPU v7x, 32 devices: a whole 2x2x4 slice. The times are simulated.
32 devices in a mesh: outer: 4 (over y, x), hst: 2 (over core), tp: 4 (over z).
Axes of the slice: x: 2, y: 2, z: 4, core: 2. Of those that a mesh axis runs over, the one named last changes fastest.
Arguments:
- gradient: bfloat16 [8, 2, 8192, 1024], P(('outer', 'hst'), None, None, 'tp'), may hold values from -384 to 384
- error_acc: bfloat16 [8, 2, 8192, 1024], P(('outer', 'hst'), None, None, 'tp'), may hold values from -192 to 192
- q_start: float32 [2, 1024, 32], P(None, 'tp'), may hold values from -6 to 6
Outputs:
- update: bfloat16 [2, 8192, 1024], P(None, None, 'tp')
All inputs are finite; a program needn't handle non-finite values.
Results may differ from a plain program's by a relative error of at most 0.008.
Values may be sent and summed in bfloat16 or wider, within the bound.
No kernel may reach another device: no remote copies, remote signals or barrier semaphores. Data moves between devices by JAX's collectives and lax.ppermute only.
A program may use at most 128 MiB of HBM per device.

v0:
```python
import jax
import jax.numpy as jnp
from jax import lax
from jax.sharding import PartitionSpec as P


def triangular_factor(gram):
    return jnp.linalg.cholesky(gram)


def apply_inverse(left, lower):
    return lax.linalg.triangular_solve(lower, left, left_side=False, lower=True, transpose_a=True)


def local_gram(left):
    return jnp.einsum("mdr,mds->mrs", left, left, precision=lax.Precision.HIGHEST)


def shards(gradient, error_acc, q_start):
    mixed = (gradient[0].astype(jnp.float32) + error_acc[0].astype(jnp.float32)).astype(
        jnp.bfloat16
    )
    q_round = q_start.astype(jnp.bfloat16)
    left_local = jnp.einsum("mdk,mkr->mdr", mixed, q_round, preferred_element_type=jnp.float32)
    left = lax.psum(left_local, ("outer", "hst", "tp"))
    lower = triangular_factor(local_gram(left))
    basis = apply_inverse(left, lower).astype(jnp.bfloat16)
    right_local = jnp.einsum("mdk,mdr->mkr", mixed, basis, preferred_element_type=jnp.float32)
    right = lax.psum(right_local, ("outer", "hst"))
    replicas = lax.axis_size("outer") * lax.axis_size("hst")
    q_mean = (right / replicas).astype(jnp.bfloat16)
    update = jnp.einsum("mdr,mkr->mdk", basis, q_mean, preferred_element_type=jnp.float32)
    return update.astype(jnp.bfloat16)


def solution(mesh):
    in_specs = (
        P(("outer", "hst"), None, None, "tp"),
        P(("outer", "hst"), None, None, "tp"),
        P(None, "tp", None),
    )
    out_specs = P(None, None, "tp")
    return jax.shard_map(shards, mesh=mesh, in_specs=in_specs, out_specs=out_specs, check_vma=False)
```

profile of v0, /device:TPU:0, one launch (start us, length us, event | category | flops | bytes accessed | tf_op | source)
XLA Modules:
  0.0 245.5 jit_solution(5669860562048053723)
XLA Ops:
  6.5 0.0 all-reduce.3.cloned.1.call-start
  6.5 9.7 %fusion.3 = f32[2,8192,32]{1,2,0:T(8,128)} fusion(bf16[1,2,8192,256]{3,2,1,0:T(8,128)(2,1)} %param.4, bf16[1,2,8192,256]{3,2,1,0:T(8,128)(2,1)} %param.3, f32[2,256,32]{1,2,0:T(8,128)} %param.5), kind=kOutput, calls=%fused_computation.5 | convolution fusion | flops 285229056 | bytes 18939904 | tf_op jit(solution)/shard_map/mdk,mkr->mdr/dot_general | solution.py:24
  16.2 0.0 all-reduce.3.cloned.1.call-update
  16.3 0.0 all-reduce.5.cloned.1.call-start
  16.3 136.6 %all-reduce.3.cloned.1.call-done = f32[2,8192,32]{1,2,0:T(8,128)} async-done(((f32[2,8192,32]{1,2,0:T(8,128)}), f32[2,8192,32]{1,2,0:T(8,128)}) %all-reduce.3.cloned.1.call-update) | async-done | bytes 2097168 | tf_op jit(solution)/shard_map/psum | solution.py:25
  153.0 4.2 %fusion.10 = f32[2,32,32]{2,1,0:T(8,128)S(1)} fusion(f32[2,8192,32]{1,2,0:T(8,128)} %all-reduce.3.cloned.1.call-done), kind=kOutput, calls=%fused_computation.18 | convolution fusion | flops 201326592 | bytes 2105344 | tf_op jit(solution)/shard_map/mdr,mds->mrs/dot_general | solution.py:16
  157.2 0.1 copy.6
  157.3 5.9 %custom-call.7 = f32[2,32,32]{2,1,0:T(8,128)S(1)} custom-call(f32[2,32,32]{2,1,0:T(8,128)S(1)} %fusion.6), custom_call_target="Cholesky" | custom-call | tf_op jit(solution)/shard_map/jit(cholesky)/cholesky | solution.py:8
  163.2 0.1 compare_reduce_fusion
  163.3 0.1 select_bitcast_fusion
  163.4 4.9 %custom-call.8 = f32[2,1,32,32]{2,3,1,0:T(8,128)S(1)} custom-call(f32[2,1,32,32]{3,2,1,0:T(8,128)S(1)} %select_bitcast_fusion), custom_call_target="InvertDiagBlocksLowerTriangular" | custom-call | tf_op jit(solution)/shard_map/triangular_solve | solution.py:12
  168.3 3.5 %convolution_convert_fusion.1 = bf16[2,8192,32]{1,2,0:T(8,128)(2,1)S(1)} fusion(f32[2,8192,32]{1,2,0:T(8,128)} %all-reduce.3.cloned.1.call-done, f32[2,1,32,32]{2,3,1,0:T(8,128)S(1)} %custom-call.8), kind=kOutput, calls=%fused_computation.2 | convolution fusion | flops 201850880 | bytes 3153920 | tf_op jit(solution)/shard_map/triangular_solve | solution.py:12
  171.8 8.7 %fusion.1 = f32[2,256,32]{1,2,0:T(8,128)} fusion(bf16[2,8192,32]{1,2,0:T(8,128)(2,1)S(1)} %convolution_convert_fusion.1, bf16[1,2,8192,256]{3,2,1,0:T(8,128)(2,1)} %param.4, bf16[1,2,8192,256]{3,2,1,0:T(8,128)(2,1)} %param.3), kind=kOutput, calls=%fused_computation.4 | convolution fusion | flops 285212672 | bytes 17891328 | tf_op jit(solution)/shard_map/mdk,mdr->mkr/dot_general | solution.py:28
  180.5 0.0 all-reduce.5.cloned.1.call-update
  180.5 51.5 %all-reduce.5.cloned.1.call-done = f32[2,256,32]{1,2,0:T(8,128)} async-done(((f32[2,256,32]{1,2,0:T(8,128)}), f32[2,256,32]{1,2,0:T(8,128)}) %all-reduce.5.cloned.1.call-update) | async-done | bytes 65552 | tf_op jit(solution)/shard_map/psum | solution.py:29
  232.0 6.6 %convolution_convert_fusion = bf16[2,8192,256]{2,1,0:T(8,128)(2,1)} fusion(bf16[2,8192,32]{1,2,0:T(8,128)(2,1)S(1)} %convolution_convert_fusion.1, f32[2,256,32]{1,2,0:T(8,128)} %all-reduce.5.cloned.1.call-done), kind=kOutput, calls=%fused_computation.1 | convolution fusion | flops 272662528 | bytes 9502720 | tf_op jit(solution)/shard_map/mdr,mkr->mdk/dot_general | solution.py:32
  (4 shorter events, 0.1 us)
Async XLA Ops:
  6.5 146.4 %all-reduce.3.cloned.1.call-start = ((), (), s32[]{:S(2)}) async-start(), calls=%async_computation | async-start | bytes 4194304 | tf_op jit(solution)/shard_map/psum | solution.py:25
  16.3 215.8 %all-reduce.5.cloned.1.call-start = ((), (), s32[]{:S(2)}) async-start(), calls=%async_computation.1 | async-start | bytes 131072 | tf_op jit(solution)/shard_map/psum | solution.py:29
Sparse Core Ops, SparseCore 0:
  16.4 136.5 all-reduce.2
  180.6 51.3 all-reduce.4
where the time goes:
time: 246 us; the launch traced here: 245 us
  waiting for transfers between devices  188 us (76%)
  matrix products  32.7 us (13%)
  between operations  13.4 us (5%)
  other arithmetic  11 us (4%)
    psum x1, waiting for transfers between devices, shards(): left = lax.psum(left_local, ('outer', 'hst', 'tp'))  137 us
    psum x1, waiting for transfers between devices, shards(): right = lax.psum(right_local, ('outer', 'hst'))  51.5 us
    dot_general x1, matrix products, shards(): jnp.einsum('mdk,mkr->mdr', mixed, q_round, preferred_element_type=jnp.flo...  9.69 us
    dot_general x1, matrix products, shards(): jnp.einsum('mdk,mdr->mkr', mixed, basis, preferred_element_type=jnp.float32)  8.66 us
    dot_general x1, matrix products, shards(): jnp.einsum('mdr,mkr->mdk', basis, q_mean, preferred_element_type=jnp.floa...  6.62 us
    another operation x4, other arithmetic, triangular_factor(): return jnp.linalg.cholesky(gram)  6.03 us
    another operation x3, other arithmetic, apply_inverse(): lax.linalg.triangular_solve(lower, left, left_side=False, lower=True, tra...  5 us
  transfers between devices with their start and end apart: 2, of which 2 were waited for; matrix products, arithmetic and copies ran while one was open for 0% of the time, Pallas kernels for 0%

commit v1 on v0

v1 whole, which is shorter than its diff:
```python
import jax
import jax.numpy as jnp
from jax import lax
from jax.experimental import pallas as pl
from jax.experimental.pallas import tpu as pltpu
from jax.sharding import PartitionSpec as P

AXES = ("outer", "hst", "tp")
PACK = 4
LANES = 128
F32, BF16 = jnp.float32, jnp.bfloat16
VMEM_LIMIT = 48 * 1024 * 1024


def bits(size):
    return size.bit_length() - 1


def sizes():
    return tuple(lax.axis_size(axis) for axis in AXES)


def coordinates(index):
    _, hst, tp = sizes()
    return index // (hst * tp), index // tp % hst, index % tp


def exchange(x, partner):
    _, hst, tp = sizes()
    pairs = []
    for index in range(sizes()[0] * hst * tp):
        o, h, t = partner(*coordinates(index))
        pairs.append((index, (o * hst + h) * tp + t))
    return lax.ppermute(x, AXES, pairs)


def replica_steps():
    outer, hst, _ = sizes()
    o, h = lax.axis_index("outer"), lax.axis_index("hst")
    steps = []
    for b in range(bits(hst)):
        steps.append((lambda oo, hh, tt, b=b: (oo, hh ^ (1 << b), tt), (h >> b) & 1))
    n = bits(outer)
    for b in range(n):
        def partner(oo, hh, tt, b=b):
            return oo ^ (1 << (b if hh % 2 == 0 else n - 1 - b)), hh, tt
        steps.append((partner, jnp.where(h % 2 == 0, (o >> b) & 1, (o >> (n - 1 - b)) & 1)))
    return steps


def mix_kernel(q_ref, g_hbm, e_hbm, mixed_ref, left_ref):
    m_count, pack, rows, width = mixed_ref.shape
    block = 256

    def body(g_ref, e_ref):
        i = pl.program_id(0)
        where = pl.ds(pl.multiple_of(i * block, block), block)
        total = jnp.zeros((block, m_count * LANES), F32)
        for m in range(m_count):
            for j in range(pack):
                mixed = (g_ref[m, j].astype(F32) + e_ref[m, j].astype(F32)).astype(BF16)
                mixed_ref[m, j, where, :] = mixed
                total += jnp.dot(mixed, q_ref[m, j], preferred_element_type=F32)
        left_ref[where, :] = total

    spec = pl.BlockSpec((m_count, pack, block, width), lambda i: (0, 0, i, 0))
    pltpu.emit_pipeline(body, grid=(rows // block,), in_specs=[spec, spec])(g_hbm, e_hbm)


def mix(gradient, error_acc, q_start):
    m_count, depth, width = gradient.shape
    rank = q_start.shape[-1]
    rows = depth // PACK
    q_round = q_start.astype(BF16)
    m_eye, j_eye = jnp.eye(m_count, dtype=BF16), jnp.eye(PACK, dtype=BF16)
    wide = q_round[:, None, :, None, None, :] * (m_eye[:, None, None, :, None, None] * j_eye[None, :, None, None, :, None])
    wide = wide.reshape(m_count, PACK, width, m_count * PACK * rank)
    shape = (m_count, PACK, rows, width)
    return pl.pallas_call(
        mix_kernel,
        in_specs=[pl.BlockSpec(memory_space=pltpu.VMEM), pl.BlockSpec(memory_space=pl.ANY), pl.BlockSpec(memory_space=pl.ANY)],
        out_specs=[pl.BlockSpec(memory_space=pltpu.VMEM)] * 2,
        out_shape=[pltpu.VMEM(shape, BF16), pltpu.VMEM((rows, m_count * LANES), F32)],
        compiler_params=pltpu.CompilerParams(vmem_limit_bytes=VMEM_LIMIT),
        name="mix",
    )(wide, gradient.reshape(shape), error_acc.reshape(shape))


def project_kernel(left_ref, mixed_ref, right_ref, gram_ref):
    m_count, pack, rows, width = mixed_ref.shape
    rank = LANES // pack
    left = left_ref[...]
    turned = left.T
    every = jnp.dot(turned, left, preferred_element_type=F32)
    for m in range(m_count):
        gram = jnp.zeros((rank, rank), F32)
        right = jnp.zeros((rank, width), F32)
        for j in range(pack):
            at = m * LANES + j * rank
            gram += every[at:at + rank, at:at + rank]
            right += jnp.dot(turned[at:at + rank], mixed_ref[m, j], preferred_element_type=F32)
        gram_ref[m] = gram
        right_ref[m] = right


def project(left, mixed):
    m_count, pack, rows, width = mixed.shape
    rank = LANES // pack
    return pl.pallas_call(
        project_kernel,
        in_specs=[pl.BlockSpec(memory_space=pltpu.VMEM)] * 2,
        out_specs=[pl.BlockSpec(memory_space=pltpu.VMEM)] * 2,
        out_shape=[pltpu.VMEM((m_count, rank, width), F32), pltpu.VMEM((m_count, rank, rank), F32)],
        compiler_params=pltpu.CompilerParams(vmem_limit_bytes=VMEM_LIMIT),
        name="project",
    )(left, mixed)


def invert_kernel(gram_ref, inverse_ref):
    m_count, rank, _ = gram_ref.shape
    row_at = lax.broadcasted_iota(jnp.int32, (rank, rank), 0)
    col_at = lax.broadcasted_iota(jnp.int32, (rank, rank), 1)
    held = [gram_ref[m] for m in range(m_count)]
    for k in range(rank):
        for m in range(m_count):
            a = held[m]
            row, col = a[k:k + 1, :], a[:, k:k + 1]
            inv = 1.0 / a[k:k + 1, k:k + 1]
            scaled = row * inv
            rest = a - col * scaled
            rest = jnp.where(row_at == k, scaled, rest)
            rest = jnp.where(col_at == k, jnp.where(row_at == k, inv, -col * inv), rest)
            held[m] = rest
    for m in range(m_count):
        inverse_ref[m] = held[m]


def invert(gram):
    return pl.pallas_call(
        invert_kernel,
        in_specs=[pl.BlockSpec(memory_space=pltpu.VMEM)],
        out_specs=pl.BlockSpec(memory_space=pltpu.VMEM),
        out_shape=pltpu.VMEM(gram.shape, F32),
        name="invert",
    )(gram)


def expand_kernel(scale, left_ref, inverse_ref, right_ref, update_ref, wide_ref):
    m_count, rank, width = right_ref.shape
    pack = LANES // rank
    m, half = pl.program_id(0), pl.program_id(1)

    @pl.when((m == 0) & (half == 0))
    def _():
        wide_ref[...] = jnp.zeros_like(wide_ref)
        for mm in range(m_count):
            z = jnp.dot(inverse_ref[mm], right_ref[mm], precision=lax.Precision.HIGHEST, preferred_element_type=F32) * scale
            high = z.astype(BF16)
            low = (z - high.astype(F32)).astype(BF16)
            for j in range(pack):
                wide_ref[mm, j, pl.ds(j * rank, rank), :] = high
                wide_ref[mm, j, pl.ds(LANES + j * rank, rank), :] = low

    left = left_ref[...]
    twice = jnp.concatenate([left, left], axis=1)
    for j in range(pack):
        update_ref[0, j] = jnp.dot(twice, wide_ref[m, j], preferred_element_type=F32).astype(BF16)


def expand(left, inverse, right, scale):
    m_count, rank, width = right.shape
    pack = LANES // rank
    rows = left.shape[0]
    block = rows // 4
    out = pl.pallas_call(
        lambda *refs: expand_kernel(scale, *refs),
        grid=(m_count, rows // block),
        in_specs=[
            pl.BlockSpec((block, LANES), lambda m, i: (i, m)),
            pl.BlockSpec(memory_space=pltpu.VMEM),
            pl.BlockSpec(memory_space=pltpu.VMEM),
        ],
        out_specs=pl.BlockSpec((1, pack, block, width), lambda m, i: (m, 0, i, 0)),
        out_shape=jax.ShapeDtypeStruct((m_count, pack, rows, width), BF16),
        scratch_shapes=[pltpu.VMEM((m_count, pack, 2 * LANES, width), BF16)],
        compiler_params=pltpu.CompilerParams(vmem_limit_bytes=VMEM_LIMIT),
        name="expand",
    )(left, inverse, right)
    return out.reshape(m_count, pack * rows, width)


def sum_left(left):
    steps = replica_steps()
    for partner, bit in steps:
        half = left.shape[0] // 2
        low, high = left[:half], left[half:]
        sent = jnp.where(bit == 1, low, high).astype(BF16)
        kept = jnp.where(bit == 1, high, low)
        left = kept + exchange(sent, partner).astype(F32)
    for b in range(bits(lax.axis_size("tp"))):
        sent = left.astype(BF16)
        left = sent.astype(F32) + exchange(sent, lambda o, h, t, b=b: (o, h, t ^ (1 << b))).astype(F32)
    left = left.astype(BF16)
    for partner, bit in reversed(steps):
        other = exchange(left, partner)
        left = jnp.concatenate([jnp.where(bit == 1, other, left), jnp.where(bit == 1, left, other)])
    return left


def sum_right(right):
    outer, hst, _ = sizes()
    for b in range(bits(hst)):
        right = right + exchange(right, lambda o, h, t, b=b: (o, h ^ (1 << b), t))
    for b in range(bits(outer)):
        right = right + exchange(right, lambda o, h, t, b=b: (o ^ (1 << b), h, t))
    return right


def shards(gradient, error_acc, q_start):
    mixed, left = mix(gradient[0], error_acc[0], q_start)
    left = sum_left(left)
    right, gram = project(left, mixed)
    inverse = invert(gram)
    outer, hst, _ = sizes()
    right = sum_right(right)
    return expand(left, inverse, right, 1.0 / (outer * hst))


def solution(mesh):
    in_specs = (
        P(("outer", "hst"), None, None, "tp"),
        P(("outer", "hst"), None, None, "tp"),
        P(None, "tp", None),
    )
    out_specs = P(None, None, "tp")
    return jax.shard_map(shards, mesh=mesh, in_specs=in_specs, out_specs=out_specs, check_vma=False)
```

time: 246 us -> 83.9 us (0.34)
  waiting for transfers between devices: 188 us -> 30.9 us
  matrix products: 32.7 us -> 0 us
  Pallas kernels: 0 us -> 26.7 us
  starting transfers between devices: 0.04 us -> 18.1 us
  between operations: 13.4 us -> 0.16 us
  other arithmetic: 11 us -> 4.03 us
  local copies, waits for them, and re-layouts: 0.08 us -> 3.72 us
    psum x2 -> x0, waiting for transfers between devices: 188 us -> none  [the longest x1 137 us: shards(): left = lax.psum(left_local, ('outer', 'hst', 'tp'))]
    ppermute x0 -> x11, waiting for transfers between devices: none -> 30.9 us  [exchange(): return lax.ppermute(x, AXES, pairs)]
    dot_general x4 -> x0, matrix products: 29.2 us -> none  [the longest x1 9.69 us: shards(): jnp.einsum('mdk,mkr->mdr', mixed, q_round, preferred_element_type=jnp.flo...]
    pallas_call x0 -> x4, Pallas kernels: none -> 26.7 us  [the longest x1 10.2 us: mix(): pl.pallas_call(mix_kernel, in_specs=[pl.BlockSpec(memory_space=pltpu.VMEM...]
    ppermute x0 -> x11, starting transfers between devices: none -> 18.1 us  [exchange(): return lax.ppermute(x, AXES, pairs)]
    another operation x7 -> x0, other arithmetic: 11 us -> none  [the longest x4 6.03 us: triangular_factor(): return jnp.linalg.cholesky(gram)]
    another operation x1 -> x0, matrix products: 3.51 us -> none  [apply_inverse(): lax.linalg.triangular_solve(lower, left, left_side=False, lower=True, tra...]
    unnamed x0 -> x4, local copies, waits for them, and re-layouts: none -> 3.4 us
  transfers between devices with their start and end apart: 2 -> 11, of which waited for: 2 -> 10; matrix products, arithmetic and copies ran while one was open for 0% -> 0% of each run, Pallas kernels for 0% -> 6%
where the time goes in v1:
time: 83.9 us; the launch traced here: 83.5 us
  waiting for transfers between devices  30.9 us (37%)
  Pallas kernels  26.7 us (32%)
  starting transfers between devices  18.1 us (22%)
  other arithmetic  4.03 us (5%)
  local copies, waits for them, and re-layouts  3.72 us (4%)
    ppermute x11, waiting for transfers between devices, exchange(): return lax.ppermute(x, AXES, pairs)  30.9 us
    ppermute x11, starting transfers between devices, exchange(): return lax.ppermute(x, AXES, pairs)  18.1 us
    pallas_call x1, Pallas kernels, mix(): pl.pallas_call(mix_kernel, in_specs=[pl.BlockSpec(memory_space=pltpu.VMEM...  10.2 us
    pallas_call x1, Pallas kernels, expand(): pl.pallas_call(lambda *refs: expand_kernel(scale, *refs), grid=(m_count,...  6.49 us
    pallas_call x1, Pallas kernels, project(): pl.pallas_call(project_kernel, in_specs=[pl.BlockSpec(memory_space=pltpu....  5.26 us
    pallas_call x1, Pallas kernels, invert(): pl.pallas_call(invert_kernel, in_specs=[pl.BlockSpec(memory_space=pltpu.V...  4.73 us
    unnamed x4, local copies, waits for them, and re-layouts  3.4 us
  transfers between devices with their start and end apart: 11, of which 10 were waited for; matrix products, arithmetic and copies ran while one was open for 0% of the time, Pallas kernels for 6%

profile of v1, /device:TPU:0, one launch (start us, length us, event | category | flops | bytes accessed | tf_op | source)
XLA Modules:
  0.0 83.5 jit_solution(6333300478923626918)
XLA Ops:
  0.3 0.8 %convert_element_type.56 = bf16[2,256,32]{1,2,0:T(8,128)(2,1)S(1)} convert(f32[2,256,32]{1,2,0:T(8,128)} %param.5) | non-fusion elementwise | flops 16384 | bytes 98304 | tf_op jit(solution)/shard_map/convert_element_type | solution.py:74
  1.1 0.1 copy.5
  1.3 1.0 %broadcast_multiply_fusion.q_ref = bf16[2,4,256,256]{3,2,1,0:T(8,128)(2,1)} fusion(bf16[2,4,256]{2,1,0:T(4,128)(2,1)S(1)} %mul.47, bf16[2,256,256]{2,1,0:T(8,128)(2,1)S(1)} %copy.5), kind=kLoop, calls=%fused_computation.6 | loop fusion | flops 524288 | bytes 1314816 | tf_op jit(solution)/shard_map/mul | solution.py:76
  2.3 10.2 %mix.1 = (bf16[2,4,2048,256]{3,2,1,0:T(8,128)(2,1)S(1)}, f32[2048,256]{1,0:T(8,128)S(1)}) custom-call(bf16[2,4,256,256]{3,2,1,0:T(8,128)(2,1)} %broadcast_multiply_fusion.q_ref, bf16[2,4,2048,256]{3,2,1,0:T(8,128)(2,1)} %bitcast.4, bf16[2,4,2048,256]{3,2,1,0:T(8,128)(2,1)} %bitcast.5), custom_call_target="tpu_custom_call" | custom-call | tf_op jit(solution)/shard_map/mix/pallas_call | solution.py:79
  12.5 3.4 %copy-done = bf16[2,4,2048,256]{3,2,1,0:T(8,128)(2,1)} copy-done((bf16[2,4,2048,256]{3,2,1,0:T(8,128)(2,1)}, bf16[2,4,2048,256]{3,2,1,0:T(8,128)(2,1)S(1)}, u32[]{:S(2)}) %copy-start) | copy-done | bytes 8388632
  15.9 0.1 select_convert_fusion
  16.0 0.5 collective-permute-start
  16.5 1.7 %collective-permute-done = bf16[1024,256]{1,0:T(8,128)(2,1)} collective-permute-done((bf16[1024,256]{1,0:T(8,128)(2,1)S(1)}, bf16[1024,256]{1,0:T(8,128)(2,1)}, u32[]{:S(2)}, u32[]{:S(2)}) %collective-permute-start) | collective-permute-done | bytes 524320 | tf_op jit(solution)/shard_map/ppermute | solution.py:34
  18.2 1.2 %convert_add_fusion = f32[1024,256]{1,0:T(8,128)S(1)} fusion(bf16[1024,256]{1,0:T(8,128)(2,1)} %collective-permute-done, f32[2048,256]{1,0:T(8,128)S(1)} %get-tuple-element.9, pred[]{:T(512)S(6)} %eq.39), kind=kLoop, calls=%fused_computation.1 | loop fusion | flops 786432 | bytes 3670017 | tf_op jit(solution)/shard_map/add | solution.py:199
  19.5 2.9 %collective-permute-start.1 = (bf16[512,256]{1,0:T(8,128)(2,1)S(1)}, bf16[512,256]{1,0:T(8,128)(2,1)S(1)}, u32[]{:S(2)}, u32[]{:S(2)}) collective-permute-start(bf16[512,256]{1,0:T(8,128)(2,1)S(1)} %select_convert_fusion.1), channel_id=1, source_target_pairs={{0,8},{1,9},{2,10},{3,11},{4,20},{5,21},{6,22},{7,23},{8,0},{9,1},... | collective-permute-start | bytes 786440 | tf_op jit(solution)/shard_map/ppermute | solution.py:34
  22.4 4.4 %collective-permute-done.1 = bf16[512,256]{1,0:T(8,128)(2,1)S(1)} collective-permute-done((bf16[512,256]{1,0:T(8,128)(2,1)S(1)}, bf16[512,256]{1,0:T(8,128)(2,1)S(1)}, u32[]{:S(2)}, u32[]{:S(2)}) %collective-permute-start.1) | collective-permute-done | bytes 262176 | tf_op jit(solution)/shard_map/ppermute | solution.py:34
  26.9 2.1 %collective-permute-start.2 = (bf16[256,256]{1,0:T(8,128)(2,1)S(1)}, bf16[256,256]{1,0:T(8,128)(2,1)S(1)}, u32[]{:S(2)}, u32[]{:S(2)}) collective-permute-start(bf16[256,256]{1,0:T(8,128)(2,1)S(1)} %select_convert_fusion.2), channel_id=1, source_target_pairs={{0,16},{1,17},{2,18},{3,19},{4,12},{5,13},{6,14},{7,15},{8,24},{9,... | collective-permute-start | bytes 393224 | tf_op jit(solution)/shard_map/ppermute | solution.py:34
  29.0 2.9 %collective-permute-done.2 = bf16[256,256]{1,0:T(8,128)(2,1)S(1)} collective-permute-done((bf16[256,256]{1,0:T(8,128)(2,1)S(1)}, bf16[256,256]{1,0:T(8,128)(2,1)S(1)}, u32[]{:S(2)}, u32[]{:S(2)}) %collective-permute-start.2) | collective-permute-done | bytes 131104 | tf_op jit(solution)/shard_map/ppermute | solution.py:34
  32.0 2.1 %collective-permute-start.3 = (bf16[256,256]{1,0:T(8,128)(2,1)S(1)}, bf16[256,256]{1,0:T(8,128)(2,1)S(1)}, u32[]{:S(2)}, u32[]{:S(2)}) collective-permute-start(bf16[256,256]{1,0:T(8,128)(2,1)S(1)} %add_convert_fusion.2), channel_id=1, source_target_pairs={{0,1},{1,0},{2,3},{3,2},{4,5},{5,4},{6,7},{7,6},{8,9},{9,8},{10,11... | collective-permute-start | bytes 393224 | tf_op jit(solution)/shard_map/ppermute | solution.py:34
  34.1 2.9 %collective-permute-done.3 = bf16[256,256]{1,0:T(8,128)(2,1)S(1)} collective-permute-done((bf16[256,256]{1,0:T(8,128)(2,1)S(1)}, bf16[256,256]{1,0:T(8,128)(2,1)S(1)}, u32[]{:S(2)}, u32[]{:S(2)}) %collective-permute-start.3) | collective-permute-done | bytes 131104 | tf_op jit(solution)/shard_map/ppermute | solution.py:34
  37.1 3.5 %collective-permute-start.4 = (bf16[256,256]{1,0:T(8,128)(2,1)S(1)}, bf16[256,256]{1,0:T(8,128)(2,1)S(1)}, u32[]{:S(2)}, u32[]{:S(2)}) collective-permute-start(bf16[256,256]{1,0:T(8,128)(2,1)S(1)} %add_convert_fusion.1), channel_id=1, source_target_pairs={{0,2},{1,3},{2,0},{3,1},{4,6},{5,7},{6,4},{7,5},{8,10},{9,11},{10,... | collective-permute-start | bytes 393224 | tf_op jit(solution)/shard_map/ppermute | solution.py:34
  40.7 4.4 %collective-permute-done.4 = bf16[256,256]{1,0:T(8,128)(2,1)S(1)} collective-permute-done((bf16[256,256]{1,0:T(8,128)(2,1)S(1)}, bf16[256,256]{1,0:T(8,128)(2,1)S(1)}, u32[]{:S(2)}, u32[]{:S(2)}) %collective-permute-start.4) | collective-permute-done | bytes 131104 | tf_op jit(solution)/shard_map/ppermute | solution.py:34
  45.1 1.6 %collective-permute-start.5 = (bf16[256,256]{1,0:T(8,128)(2,1)S(1)}, bf16[256,256]{1,0:T(8,128)(2,1)S(1)}, u32[]{:S(2)}, u32[]{:S(2)}) collective-permute-start(bf16[256,256]{1,0:T(8,128)(2,1)S(1)} %add_convert_fusion), channel_id=1, source_target_pairs={{0,16},{1,17},{2,18},{3,19},{4,12},{5,13},{6,14},{7,15},{8,24},{9,... | collective-permute-start | bytes 393224 | tf_op jit(solution)/shard_map/ppermute | solution.py:34
  46.6 4.1 %collective-permute-done.5 = bf16[256,256]{1,0:T(8,128)(2,1)S(1)} collective-permute-done((bf16[256,256]{1,0:T(8,128)(2,1)S(1)}, bf16[256,256]{1,0:T(8,128)(2,1)S(1)}, u32[]{:S(2)}, u32[]{:S(2)}) %collective-permute-start.5) | collective-permute-done | bytes 131104 | tf_op jit(solution)/shard_map/ppermute | solution.py:34
  50.8 1.7 %collective-permute-start.6 = (bf16[512,256]{1,0:T(8,128)(2,1)S(1)}, bf16[512,256]{1,0:T(8,128)(2,1)S(1)}, u32[]{:S(2)}, u32[]{:S(2)}) collective-permute-start(bf16[512,256]{1,0:T(8,128)(2,1)S(1)} %pad_maximum_fusion.2), channel_id=1, source_target_pairs={{0,8},{1,9},{2,10},{3,11},{4,20},{5,21},{6,22},{7,23},{8,0},{9,1},... | collective-permute-start | bytes 786440 | tf_op jit(solution)/shard_map/ppermute | solution.py:34
  52.5 4.8 %collective-permute-done.6 = bf16[512,256]{1,0:T(8,128)(2,1)S(1)} collective-permute-done((bf16[512,256]{1,0:T(8,128)(2,1)S(1)}, bf16[512,256]{1,0:T(8,128)(2,1)S(1)}, u32[]{:S(2)}, u32[]{:S(2)}) %collective-permute-start.6) | collective-permute-done | bytes 262176 | tf_op jit(solution)/shard_map/ppermute | solution.py:34
  57.3 0.1 broadcast_select_fusion.3
  57.5 1.9 %collective-permute-done.7 = bf16[1024,256]{1,0:T(8,128)(2,1)S(1)} collective-permute-done((bf16[1024,256]{1,0:T(8,128)(2,1)S(1)}, bf16[1024,256]{1,0:T(8,128)(2,1)S(1)}, u32[]{:S(2)}, u32[]{:S(2)}) %collective-permute-start.7) | collective-permute-done | bytes 524320 | tf_op jit(solution)/shard_map/ppermute | solution.py:34
  59.4 0.2 broadcast_select_fusion.1
  59.7 5.3 %project.1 = (f32[2,32,256]{2,1,0:T(8,128)S(1)}, f32[2,32,32]{2,1,0:T(8,128)S(1)}) custom-call(bf16[2048,256]{1,0:T(8,128)(2,1)S(1)} %pad_maximum_fusion.left_ref.refs_0_, bf16[2,4,2048,256]{3,2,1,0:T(8,128)(2,1)} %copy-done), custom_call_target="tpu_custom_call" | custom-call | tf_op jit(solution)/shard_map/project/pallas_call | solution.py:109
  64.9 0.2 collective-permute-start.8
  65.1 1.1 %collective-permute-done.8 = f32[2,32,256]{2,1,0:T(8,128)S(1)} collective-permute-done((f32[2,32,256]{2,1,0:T(8,128)S(1)}, f32[2,32,256]{2,1,0:T(8,128)S(1)}, u32[]{:S(2)}, u32[]{:S(2)}) %collective-permute-start.8) | collective-permute-done | bytes 65568 | tf_op jit(solution)/shard_map/ppermute | solution.py:34
  66.2 1.7 %collective-permute-start.9 = (f32[2,32,256]{2,1,0:T(8,128)S(1)}, f32[2,32,256]{2,1,0:T(8,128)S(1)}, u32[]{:S(2)}, u32[]{:S(2)}) collective-permute-start(f32[2,32,256]{2,1,0:T(8,128)S(1)} %add.35), channel_id=1, source_target_pairs={{0,8},{1,9},{2,10},{3,11},{4,12},{5,13},{6,14},{7,15},{8,0},{9,1},... | collective-permute-start | bytes 196616 | tf_op jit(solution)/shard_map/ppermute | solution.py:34
  67.9 2.7 %collective-permute-done.9 = f32[2,32,256]{2,1,0:T(8,128)S(1)} collective-permute-done((f32[2,32,256]{2,1,0:T(8,128)S(1)}, f32[2,32,256]{2,1,0:T(8,128)S(1)}, u32[]{:S(2)}, u32[]{:S(2)}) %collective-permute-start.9) | collective-permute-done | bytes 65568 | tf_op jit(solution)/shard_map/ppermute | solution.py:34
  70.6 1.7 %collective-permute-start.10 = (f32[2,32,256]{2,1,0:T(8,128)S(1)}, f32[2,32,256]{2,1,0:T(8,128)S(1)}, u32[]{:S(2)}, u32[]{:S(2)}) collective-permute-start(f32[2,32,256]{2,1,0:T(8,128)S(1)} %add.36), channel_id=1, source_target_pairs={{0,16},{1,17},{2,18},{3,19},{4,20},{5,21},{6,22},{7,23},{8,24},{9,... | collective-permute-start | bytes 196616 | tf_op jit(solution)/shard_map/ppermute | solution.py:34
  72.3 4.7 %invert.1.refs_1_ = f32[2,32,32]{2,1,0:T(8,128)S(1)} custom-call(f32[2,32,32]{2,1,0:T(8,128)} %copy-done.1), custom_call_target="tpu_custom_call" | custom-call | tf_op jit(solution)/shard_map/invert/pallas_call | solution.py:139
  77.0 6.5 %expand.1 = bf16[2,4,2048,256]{3,2,1,0:T(8,128)(2,1)} custom-call(bf16[2048,256]{1,0:T(8,128)(2,1)S(1)} %pad_maximum_fusion.left_ref.refs_0_, f32[2,32,32]{2,1,0:T(8,128)S(1)} %invert.1.refs_1_, f32[2,32,256]{2,1,0:T(8,128)S(1)} %add.37.refs_2_), custom_call_target="tpu_custom_call" | custom-call | tf_op jit(solution)/shard_map/expand/pallas_call | solution.py:175
  (24 shorter events, 0.8 us)
Async XLA Ops:
  12.5 3.4 %copy-start = (bf16[2,4,2048,256]{3,2,1,0:T(8,128)(2,1)}, bf16[2,4,2048,256]{3,2,1,0:T(8,128)(2,1)S(1)}, u32[]{:S(2)}) copy-start(bf16[2,4,2048,256]{3,2,1,0:T(8,128)(2,1)S(1)} %get-tuple-element.10.mixed_ref) | copy-start | bytes 25165828
  16.0 2.2 %collective-permute-start = (bf16[1024,256]{1,0:T(8,128)(2,1)S(1)}, bf16[1024,256]{1,0:T(8,128)(2,1)}, u32[]{:S(2)}, u32[]{:S(2)}) collective-permute-start(bf16[1024,256]{1,0:T(8,128)(2,1)S(1)} %select_convert_fusion), channel_id=1, source_target_pairs={{0,4},{1,5},{2,6},{3,7},{4,0},{5,1},{6,2},{7,3},{8,12},{9,13},{10,... | collective-permute-start | bytes 1572872 | tf_op jit(solution)/shard_map/ppermute | solution.py:34
  19.5 7.3 %collective-permute-start.1 = (bf16[512,256]{1,0:T(8,128)(2,1)S(1)}, bf16[512,256]{1,0:T(8,128)(2,1)S(1)}, u32[]{:S(2)}, u32[]{:S(2)}) collective-permute-start(bf16[512,256]{1,0:T(8,128)(2,1)S(1)} %select_convert_fusion.1), channel_id=1, source_target_pairs={{0,8},{1,9},{2,10},{3,11},{4,20},{5,21},{6,22},{7,23},{8,0},{9,1},... | collective-permute-start | bytes 786440 | tf_op jit(solution)/shard_map/ppermute | solution.py:34
  26.9 5.1 %collective-permute-start.2 = (bf16[256,256]{1,0:T(8,128)(2,1)S(1)}, bf16[256,256]{1,0:T(8,128)(2,1)S(1)}, u32[]{:S(2)}, u32[]{:S(2)}) collective-permute-start(bf16[256,256]{1,0:T(8,128)(2,1)S(1)} %select_convert_fusion.2), channel_id=1, source_target_pairs={{0,16},{1,17},{2,18},{3,19},{4,12},{5,13},{6,14},{7,15},{8,24},{9,... | collective-permute-start | bytes 393224 | tf_op jit(solution)/shard_map/ppermute | solution.py:34
  32.0 5.1 %collective-permute-start.3 = (bf16[256,256]{1,0:T(8,128)(2,1)S(1)}, bf16[256,256]{1,0:T(8,128)(2,1)S(1)}, u32[]{:S(2)}, u32[]{:S(2)}) collective-permute-start(bf16[256,256]{1,0:T(8,128)(2,1)S(1)} %add_convert_fusion.2), channel_id=1, source_target_pairs={{0,1},{1,0},{2,3},{3,2},{4,5},{5,4},{6,7},{7,6},{8,9},{9,8},{10,11... | collective-permute-start | bytes 393224 | tf_op jit(solution)/shard_map/ppermute | solution.py:34
  37.1 7.9 %collective-permute-start.4 = (bf16[256,256]{1,0:T(8,128)(2,1)S(1)}, bf16[256,256]{1,0:T(8,128)(2,1)S(1)}, u32[]{:S(2)}, u32[]{:S(2)}) collective-permute-start(bf16[256,256]{1,0:T(8,128)(2,1)S(1)} %add_convert_fusion.1), channel_id=1, source_target_pairs={{0,2},{1,3},{2,0},{3,1},{4,6},{5,7},{6,4},{7,5},{8,10},{9,11},{10,... | collective-permute-start | bytes 393224 | tf_op jit(solution)/shard_map/ppermute | solution.py:34
  45.1 5.7 %collective-permute-start.5 = (bf16[256,256]{1,0:T(8,128)(2,1)S(1)}, bf16[256,256]{1,0:T(8,128)(2,1)S(1)}, u32[]{:S(2)}, u32[]{:S(2)}) collective-permute-start(bf16[256,256]{1,0:T(8,128)(2,1)S(1)} %add_convert_fusion), channel_id=1, source_target_pairs={{0,16},{1,17},{2,18},{3,19},{4,12},{5,13},{6,14},{7,15},{8,24},{9,... | collective-permute-start | bytes 393224 | tf_op jit(solution)/shard_map/ppermute | solution.py:34
  50.8 6.4 %collective-permute-start.6 = (bf16[512,256]{1,0:T(8,128)(2,1)S(1)}, bf16[512,256]{1,0:T(8,128)(2,1)S(1)}, u32[]{:S(2)}, u32[]{:S(2)}) collective-permute-start(bf16[512,256]{1,0:T(8,128)(2,1)S(1)} %pad_maximum_fusion.2), channel_id=1, source_target_pairs={{0,8},{1,9},{2,10},{3,11},{4,20},{5,21},{6,22},{7,23},{8,0},{9,1},... | collective-permute-start | bytes 786440 | tf_op jit(solution)/shard_map/ppermute | solution.py:34
  57.4 2.0 %collective-permute-start.7 = (bf16[1024,256]{1,0:T(8,128)(2,1)S(1)}, bf16[1024,256]{1,0:T(8,128)(2,1)S(1)}, u32[]{:S(2)}, u32[]{:S(2)}) collective-permute-start(bf16[1024,256]{1,0:T(8,128)(2,1)S(1)} %pad_maximum_fusion.1), channel_id=1, source_target_pairs={{0,4},{1,5},{2,6},{3,7},{4,0},{5,1},{6,2},{7,3},{8,12},{9,13},{10,... | collective-permute-start | bytes 1572872 | tf_op jit(solution)/shard_map/ppermute | solution.py:34
  64.9 7.3 %copy-start.1 = (f32[2,32,32]{2,1,0:T(8,128)}, f32[2,32,32]{2,1,0:T(8,128)S(1)}, u32[]{:S(2)}) copy-start(f32[2,32,32]{2,1,0:T(8,128)S(1)} %get-tuple-element.11.gram_ref) | copy-start | bytes 24580
  64.9 1.3 %collective-permute-start.8 = (f32[2,32,256]{2,1,0:T(8,128)S(1)}, f32[2,32,256]{2,1,0:T(8,128)S(1)}, u32[]{:S(2)}, u32[]{:S(2)}) collective-permute-start(f32[2,32,256]{2,1,0:T(8,128)S(1)} %get-tuple-element.12), channel_id=1, source_target_pairs={{0,4},{1,5},{2,6},{3,7},{4,0},{5,1},{6,2},{7,3},{8,12},{9,13},{10,... | collective-permute-start | bytes 196616 | tf_op jit(solution)/shard_map/ppermute | solution.py:34
  66.2 4.3 %collective-permute-start.9 = (f32[2,32,256]{2,1,0:T(8,128)S(1)}, f32[2,32,256]{2,1,0:T(8,128)S(1)}, u32[]{:S(2)}, u32[]{:S(2)}) collective-permute-start(f32[2,32,256]{2,1,0:T(8,128)S(1)} %add.35), channel_id=1, source_target_pairs={{0,8},{1,9},{2,10},{3,11},{4,12},{5,13},{6,14},{7,15},{8,0},{9,1},... | collective-permute-start | bytes 196616 | tf_op jit(solution)/shard_map/ppermute | solution.py:34
  70.6 6.4 %collective-permute-start.10 = (f32[2,32,256]{2,1,0:T(8,128)S(1)}, f32[2,32,256]{2,1,0:T(8,128)S(1)}, u32[]{:S(2)}, u32[]{:S(2)}) collective-permute-start(f32[2,32,256]{2,1,0:T(8,128)S(1)} %add.36), channel_id=1, source_target_pairs={{0,16},{1,17},{2,18},{3,19},{4,20},{5,21},{6,22},{7,23},{8,24},{9,... | collective-permute-start | bytes 196616 | tf_op jit(solution)/shard_map/ppermute | solution.py:34

commit v2 on v0

v2 whole, which is shorter than its diff:
```python
import jax
import jax.numpy as jnp
from jax import lax
from jax.experimental import pallas as pl
from jax.experimental.pallas import tpu as pltpu
from jax.sharding import PartitionSpec as P

AXES = ("outer", "hst", "tp")
PACK = 4
LANES = 128
F32, BF16 = jnp.float32, jnp.bfloat16
MIB = 1024 * 1024


def bits(size):
    return size.bit_length() - 1


def sizes():
    return tuple(lax.axis_size(axis) for axis in AXES)


def coordinates(index):
    _, hst, tp = sizes()
    return index // (hst * tp), index // tp % hst, index % tp


def exchange(x, partner):
    _, hst, tp = sizes()
    pairs = []
    for index in range(sizes()[0] * hst * tp):
        o, h, t = partner(*coordinates(index))
        pairs.append((index, (o * hst + h) * tp + t))
    return lax.ppermute(x, AXES, pairs)


def replica_steps():
    outer, hst, _ = sizes()
    steps = []
    for b in range(bits(hst)):
        steps.append((lambda o, h, t, b=b: (o, h ^ (1 << b), t), lambda o, h, b=b: (h >> b) & 1))
    n = bits(outer)
    for b in range(n):
        def partner(o, h, t, b=b):
            return o ^ (1 << (b if h % 2 == 0 else n - 1 - b)), h, t

        def bit(o, h, b=b):
            return jnp.where(h % 2 == 0, (o >> b) & 1, (o >> (n - 1 - b)) & 1)

        steps.append((partner, bit))
    return steps


def pick(x, index):
    half = x.shape[0] // 2
    return jnp.where(index == 1, x[half:], x[:half])


def params(mib):
    return pltpu.CompilerParams(vmem_limit_bytes=mib * MIB)


def whole():
    return pl.BlockSpec(memory_space=pltpu.VMEM)


def in_hbm(x):
    return pltpu.with_memory_space_constraint(x, pltpu.HBM)


def scalar():
    return pl.BlockSpec(memory_space=pltpu.SMEM)


MIX_CHUNKS = 2


def mix_kernel(start_ref, q_hbm, g_hbm, e_hbm, mixed_hbm, left_ref, q_ref, g_ref, e_ref, mixed_ref, wide_ref, q_sem, sems, out_sems):
    m_count, pack, rows, width = mixed_ref.shape
    rank = q_ref.shape[1]
    block = rows // MIX_CHUNKS
    q_copy = pltpu.make_async_copy(q_hbm, q_ref, q_sem)
    q_copy.start()
    start = start_ref[0]

    def copies(c):
        source = pl.ds(pl.multiple_of(start * rows + c * block, block), block)
        where = pl.ds(c * block, block)
        return [
            pltpu.make_async_copy(hbm.at[:, :, source, :], ref.at[:, :, where, :], sems.at[k, c])
            for k, (hbm, ref) in enumerate(((g_hbm, g_ref), (e_hbm, e_ref)))
        ]

    for c in range(MIX_CHUNKS):
        for copy in copies(c):
            copy.start()
    lane_group = lax.broadcasted_iota(jnp.int32, (width, LANES), 1) // rank
    q_copy.wait()
    for m in range(m_count):
        turned = jnp.concatenate([q_ref[m]] * pack, axis=0).T
        for j in range(pack):
            wide_ref[m, pl.ds(j * width, width), :] = jnp.where(lane_group == j, turned, 0.0).astype(BF16)
    outgoing = []
    for c in range(MIX_CHUNKS):
        for copy in copies(c):
            copy.wait()
        where = pl.ds(c * block, block)
        for m in range(m_count):
            parts = []
            for j in range(pack):
                mixed = g_ref[m, j, where, :] + e_ref[m, j, where, :]
                mixed_ref[m, j, where, :] = mixed
                parts.append(mixed)
            total = jnp.dot(jnp.concatenate(parts, axis=1), wide_ref[m], preferred_element_type=F32)
            left_ref[where, m * LANES:(m + 1) * LANES] = total.astype(left_ref.dtype)
        copy = pltpu.make_async_copy(mixed_ref.at[:, :, where, :], mixed_hbm.at[:, :, where, :], out_sems.at[c])
        copy.start()
        outgoing.append(copy)
    for copy in outgoing:
        copy.wait()


def mix(gradient, error_acc, q_turned, start, rows, dtype):
    m_count, pack, _, width = gradient.shape
    elements = m_count * pack * rows * width
    shape = (m_count, pack, rows, width)
    return pl.pallas_call(
        mix_kernel,
        in_specs=[scalar()] + [pl.BlockSpec(memory_space=pltpu.HBM)] * 3,
        out_specs=[pl.BlockSpec(memory_space=pltpu.HBM), whole()],
        out_shape=[pltpu.HBM(shape, BF16), pltpu.VMEM((rows, m_count * LANES), dtype)],
        scratch_shapes=[
            pltpu.VMEM(q_turned.shape, F32),
            pltpu.VMEM(shape, BF16),
            pltpu.VMEM(shape, BF16),
            pltpu.VMEM(shape, BF16),
            pltpu.VMEM((m_count, pack * width, LANES), BF16),
            pltpu.SemaphoreType.DMA,
            pltpu.SemaphoreType.DMA((2, MIX_CHUNKS)),
            pltpu.SemaphoreType.DMA((MIX_CHUNKS,)),
        ],
        compiler_params=params(16),
        cost_estimate=pl.CostEstimate(flops=2 * elements * LANES, bytes_accessed=4 * elements, transcendentals=0),
        name="mix",
    )(start.astype(jnp.int32).reshape(1), q_turned, gradient, error_acc)


def project_kernel(left_ref, mixed_ref, *refs):
    right_ref, gram_ref = refs[-2:]
    m_count, pack, _, width = mixed_ref.shape
    rank = LANES // pack
    left = left_ref[...]
    turned = left.T
    every = jnp.dot(turned, left, preferred_element_type=F32)
    for m in range(m_count):
        gram = jnp.zeros((rank, rank), F32)
        right = refs[0][m] if len(refs) == 3 else jnp.zeros((rank, width), F32)
        for j in range(pack):
            at = m * LANES + j * rank
            gram += every[at:at + rank, at:at + rank]
            right += jnp.dot(turned[at:at + rank], mixed_ref[m, j], preferred_element_type=F32)
        gram_ref[m] = gram
        right_ref[m] = right


def project(left, mixed, *before):
    m_count, pack, rows, width = mixed.shape
    rank = LANES // pack
    elements = m_count * pack * rows * width
    mixed = pltpu.with_memory_space_constraint(mixed, pltpu.VMEM)
    return pl.pallas_call(
        project_kernel,
        in_specs=[whole()] * (2 + len(before)),
        out_specs=[whole()] * 2,
        out_shape=[pltpu.VMEM((m_count, rank, width), F32), pltpu.VMEM((m_count, rank, rank), F32)],
        compiler_params=params(8),
        cost_estimate=pl.CostEstimate(flops=2 * elements * LANES * 4, bytes_accessed=0, transcendentals=0),
        name="project",
    )(left, mixed, *before)


def invert_kernel(steps, *refs):
    grams, held_ref = refs[:-1], refs[-1]
    m_count, rank, _ = held_ref.shape
    row_at = lax.broadcasted_iota(jnp.int32, (rank, rank), 0)
    col_at = lax.broadcasted_iota(jnp.int32, (rank, rank), 1)
    held = [grams[0][m] for m in range(m_count)]
    if len(grams) == 4:
        held = [(grams[0][m] + grams[1][m]) + (grams[2][m] + grams[3][m]) for m in range(m_count)]
    for k in steps:
        for m in range(m_count):
            a = held[m]
            row, col = a[k:k + 1, :], a[:, k:k + 1]
            inv = 1.0 / a[k:k + 1, k:k + 1]
            scaled = row * inv
            rest = a - col * scaled
            rest = jnp.where(row_at == k, scaled, rest)
            held[m] = jnp.where(col_at == k, jnp.where(row_at == k, inv, -col * inv), rest)
    for m in range(m_count):
        held_ref[m] = held[m]


def invert(steps, *grams):
    return pl.pallas_call(
        lambda *refs: invert_kernel(steps, *refs),
        in_specs=[whole()] * len(grams),
        out_specs=whole(),
        out_shape=pltpu.VMEM(grams[0].shape, F32),
        compiler_params=params(4),
        cost_estimate=pl.CostEstimate(flops=2 * 10**9, bytes_accessed=0, transcendentals=0),
        name="invert",
    )(*grams)


def expand_kernel(scale, place_ref, left_ref, inverse_ref, right_ref, update_ref, wide_ref, held_ref, sems):
    m_count, rank, width = right_ref.shape
    pack = LANES // rank
    count, block, _ = left_ref.shape
    wide_ref[...] = jnp.zeros_like(wide_ref)
    copies = []
    for m in range(m_count):
        z = jnp.dot(inverse_ref[m], right_ref[m], precision=lax.Precision.HIGHEST, preferred_element_type=F32) * scale
        high = z.astype(BF16)
        low = (z - high.astype(F32)).astype(BF16)
        for j in range(pack):
            wide_ref[m, j, pl.ds(j * rank, rank), :] = high
            wide_ref[m, j, pl.ds(LANES + j * rank, rank), :] = low
            for p in range(count):
                left = left_ref[p, :, m * LANES:(m + 1) * LANES]
                rows = jnp.dot(jnp.concatenate([left, left], axis=1), wide_ref[m, j], preferred_element_type=F32)
                held_ref[m, j, p] = rows.astype(BF16)
                where = pl.ds(pl.multiple_of(place_ref[p] * block, block), block)
                copy = pltpu.make_async_copy(held_ref.at[m, j, p], update_ref.at[m, j, where, :], sems.at[m, j, p])
                copy.start()
                copies.append(copy)
    for copy in copies:
        copy.wait()


def expand(pieces, places, inverse, right, scale):
    m_count, rank, width = right.shape
    pack = LANES // rank
    count, block, _ = pieces.shape
    out = pl.pallas_call(
        lambda *refs: expand_kernel(scale, *refs),
        in_specs=[scalar(), whole(), whole(), whole()],
        out_specs=pl.BlockSpec(memory_space=pl.ANY),
        out_shape=jax.ShapeDtypeStruct((m_count, pack, count * block, width), BF16),
        scratch_shapes=[
            pltpu.VMEM((m_count, pack, 2 * LANES, width), BF16),
            pltpu.VMEM((m_count, pack, count, block, width), BF16),
            pltpu.SemaphoreType.DMA((m_count, pack, count)),
        ],
        compiler_params=params(20),
        name="expand",
    )(places, pieces, inverse, right)
    return out.reshape(m_count, pack * count * block, width)


def sum_right(right, grams):
    outer, hst, _ = sizes()
    rank = right.shape[1]
    for b in range(bits(hst)):
        right = right + exchange(right, lambda o, h, t, b=b: (o, h ^ (1 << b), t))
    right, grams = lax.optimization_barrier((right, grams))
    inverse = invert(range(rank // 2), *grams)
    for b in range(bits(outer)):
        right = right + exchange(right, lambda o, h, t, b=b: (o ^ (1 << b), h, t))
        if b == 0:
            right, inverse = lax.optimization_barrier((right, inverse))
    return right, invert(range(rank // 2, rank), inverse)


def shards(gradient, error_acc, q_start):
    _, m_count, depth, width = gradient.shape
    rows = depth // PACK
    quarter = rows // 4
    shape = (m_count, PACK, rows, width)
    gradient, error_acc = in_hbm(gradient.reshape(shape)), in_hbm(error_acc.reshape(shape))
    q_turned = in_hbm(jnp.swapaxes(q_start, 1, 2))
    steps = replica_steps()
    o, h = lax.axis_index("outer"), lax.axis_index("hst")
    (partner0, bit0), (partner1, bit1) = steps[:2]
    b0, b1, beyond = bit0(o, h), bit1(o, h), bit1(o, h ^ 1)
    at_own, at_side = 2 * b0 + b1, 2 * b0 + 1 - b1
    at_far, at_far_side = 2 * (1 - b0) + beyond, 2 * (1 - b0) + 1 - beyond

    def mixed_left(at, dtype):
        return mix(gradient, error_acc, q_turned, at, quarter, dtype)

    mixed_far_side, left_far_side = mixed_left(at_far_side, BF16)
    came_side = exchange(left_far_side, partner0)
    mixed_side, left_side = mixed_left(at_side, F32)
    sent, at_far_late = lax.optimization_barrier(((left_side + came_side.astype(F32)).astype(BF16), at_far))
    side = exchange(sent, partner1)
    mixed_far, left_far = mixed_left(at_far_late, BF16)
    came_own = exchange(left_far, partner0)
    mixed_own, left = mixed_left(at_own, F32)
    left = left + came_own.astype(F32) + side.astype(F32)
    for partner, bit in steps[2:]:
        b = bit(o, h)
        left = pick(left, b) + exchange(pick(left, 1 - b).astype(BF16), partner).astype(F32)
    for b in range(bits(lax.axis_size("tp"))):
        sent = left.astype(BF16)
        left = sent.astype(F32) + exchange(sent, lambda o, h, t, b=b: (o, h, t ^ (1 << b))).astype(F32)
    own = left.astype(BF16)

    for partner, bit in reversed(steps[2:]):
        b = bit(o, h)
        other = exchange(own, partner)
        own = jnp.concatenate([jnp.where(b == 1, other, own), jnp.where(b == 1, own, other)])
    far = exchange(own, partner0)
    side = exchange(own, partner1)
    right, gram_own = project(own, mixed_own)
    right, gram_far = project(far, mixed_far, right)
    side, right = lax.optimization_barrier((side, right))
    far_side = exchange(side, partner0)
    right, gram_side = project(side, mixed_side, right)
    right, gram_far_side = project(far_side, mixed_far_side, right)

    near, beyond = (gram_own, gram_side), (gram_far, gram_far_side)
    right, inverse = sum_right(right, near + beyond)
    outer, hst, _ = sizes()
    pieces = jnp.stack([own, far, side, far_side])
    places = jnp.stack([at_own, at_far, at_side, at_far_side]).astype(jnp.int32)
    return expand(pieces, places, inverse, right, 1.0 / (outer * hst))


def solution(mesh):
    in_specs = (
        P(("outer", "hst"), None, None, "tp"),
        P(("outer", "hst"), None, None, "tp"),
        P(None, "tp", None),
    )
    out_specs = P(None, None, "tp")
    return jax.shard_map(shards, mesh=mesh, in_specs=in_specs, out_specs=out_specs, check_vma=False)
```

time: 246 us -> 64.5 us (0.26)
  waiting for transfers between devices: 188 us -> 22.1 us
  matrix products: 32.7 us -> 0 us
  Pallas kernels: 0 us -> 25.6 us
  starting transfers between devices: 0.04 us -> 15.9 us
  between operations: 13.4 us -> 0.18 us
  other arithmetic: 11 us -> 0.58 us
    psum x2 -> x0, waiting for transfers between devices: 188 us -> none  [the longest x1 137 us: shards(): left = lax.psum(left_local, ('outer', 'hst', 'tp'))]
    dot_general x4 -> x0, matrix products: 29.2 us -> none  [the longest x1 9.69 us: shards(): jnp.einsum('mdk,mkr->mdr', mixed, q_round, preferred_element_type=jnp.flo...]
    pallas_call x0 -> x11, Pallas kernels: none -> 25.6 us  [the longest x4 14.7 us: mix(): pl.pallas_call(mix_kernel, in_specs=[scalar()] + [pl.BlockSpec(memory_spa...]
    ppermute x0 -> x13, waiting for transfers between devices: none -> 22.1 us  [exchange(): return lax.ppermute(x, AXES, pairs)]
    ppermute x0 -> x13, starting transfers between devices: none -> 15.9 us  [exchange(): return lax.ppermute(x, AXES, pairs)]
    another operation x7 -> x3, other arithmetic: 11 us -> 0.24 us  [the longest x2 0.17 us: shards(): pieces = jnp.stack([own, far, side, far_side])]
    another operation x1 -> x0, matrix products: 3.51 us -> none  [apply_inverse(): lax.linalg.triangular_solve(lower, left, left_side=False, lower=True, tra...]
  transfers between devices with their start and end apart: 2 -> 13, of which waited for: 2 -> 9; matrix products, arithmetic and copies ran while one was open for 0% -> 0% of each run, Pallas kernels for 0% -> 26%
where the time goes in v2:
time: 64.5 us; the launch traced here: 64.3 us
  Pallas kernels  25.6 us (40%)
  waiting for transfers between devices  22.1 us (34%)
  starting transfers between devices  15.9 us (25%)
    ppermute x13, waiting for transfers between devices, exchange(): return lax.ppermute(x, AXES, pairs)  22.1 us
    ppermute x13, starting transfers between devices, exchange(): return lax.ppermute(x, AXES, pairs)  15.9 us
    pallas_call x4, Pallas kernels, mix(): pl.pallas_call(mix_kernel, in_specs=[scalar()] + [pl.BlockSpec(memory_spa...  14.7 us
    pallas_call x1, Pallas kernels, expand(): pl.pallas_call(lambda *refs: expand_kernel(scale, *refs), in_specs=[scala...  4.64 us
    pallas_call x2, Pallas kernels, invert(): pl.pallas_call(lambda *refs: invert_kernel(steps, *refs), in_specs=[whole...  3.92 us
    pallas_call x4, Pallas kernels, project(): pl.pallas_call(project_kernel, in_specs=[whole()] * (2 + len(before)), ou...  2.32 us
  transfers between devices with their start and end apart: 13, of which 9 were waited for; matrix products, arithmetic and copies ran while one was open for 0% of the time, Pallas kernels for 26%

profile of v2, /device:TPU:0, one launch (start us, length us, event | category | flops | bytes accessed | tf_op | source)
XLA Modules:
  0.0 64.3 jit_solution(3830369914285540704)
XLA Ops:
  0.0 3.7 %mix.6 = (bf16[2,4,512,256]{3,2,1,0:T(8,128)(2,1)}, bf16[512,256]{1,0:T(8,128)(2,1)S(1)}) custom-call(s32[1]{0:T(128)} %bitcast.3.start_ref, f32[2,32,256]{2,1,0:T(8,128)} %bitcast.25, bf16[2,4,2048,256]{3,2,1,0:T(8,128)(2,1)} %bitcast.17, bf16[2,4,2048,256]{3,2,1,0:T(8,128)(2,1)} %bitcast.21), custom_call_target="tpu_custom_call" | custom-call | flops 268435456 | bytes 4194304 | tf_op jit(solution)/shard_map/mix/pallas_call | solution.py:127
  3.7 0.5 collective-permute-start
  4.2 3.6 %mix.5 = (bf16[2,4,512,256]{3,2,1,0:T(8,128)(2,1)}, f32[512,256]{1,0:T(8,128)S(1)}) custom-call(s32[1]{0:T(128)} %bitcast.2.start_ref, f32[2,32,256]{2,1,0:T(8,128)} %bitcast.26, bf16[2,4,2048,256]{3,2,1,0:T(8,128)(2,1)} %bitcast.18, bf16[2,4,2048,256]{3,2,1,0:T(8,128)(2,1)} %bitcast.22), custom_call_target="tpu_custom_call" | custom-call | flops 268435456 | bytes 4194304 | tf_op jit(solution)/shard_map/mix/pallas_call | solution.py:127
  7.9 2.6 %collective-permute-start.2 = (bf16[512,256]{1,0:T(8,128)(2,1)S(1)}, bf16[512,256]{1,0:T(8,128)(2,1)S(1)}, u32[]{:S(2)}, u32[]{:S(2)}) collective-permute-start(bf16[512,256]{1,0:T(8,128)(2,1)S(1)} %add_convert_fusion), channel_id=1, source_target_pairs={{0,8},{1,9},{2,10},{3,11},{4,20},{5,21},{6,22},{7,23},{8,0},{9,1},... | collective-permute-start | bytes 786440 | tf_op jit(solution)/shard_map/ppermute | solution.py:34
  10.5 3.6 %mix.7 = (bf16[2,4,512,256]{3,2,1,0:T(8,128)(2,1)}, bf16[512,256]{1,0:T(8,128)(2,1)S(1)}) custom-call(s32[1]{0:T(128)} %bitcast.7.start_ref, f32[2,32,256]{2,1,0:T(8,128)} %bitcast.27, bf16[2,4,2048,256]{3,2,1,0:T(8,128)(2,1)} %bitcast.19, bf16[2,4,2048,256]{3,2,1,0:T(8,128)(2,1)} %bitcast.23), custom_call_target="tpu_custom_call" | custom-call | flops 268435456 | bytes 4194304 | tf_op jit(solution)/shard_map/mix/pallas_call | solution.py:127
  14.2 0.3 collective-permute-start.1
  14.5 3.7 %mix.4 = (bf16[2,4,512,256]{3,2,1,0:T(8,128)(2,1)}, f32[512,256]{1,0:T(8,128)S(1)}) custom-call(s32[1]{0:T(128)} %bitcast.start_ref, f32[2,32,256]{2,1,0:T(8,128)} %bitcast.28, bf16[2,4,2048,256]{3,2,1,0:T(8,128)(2,1)} %bitcast.20, bf16[2,4,2048,256]{3,2,1,0:T(8,128)(2,1)} %bitcast.24), custom_call_target="tpu_custom_call" | custom-call | flops 268435456 | bytes 4194304 | tf_op jit(solution)/shard_map/mix/pallas_call | solution.py:127
  18.3 1.4 %collective-permute-start.3 = (bf16[256,256]{1,0:T(8,128)(2,1)S(1)}, bf16[256,256]{1,0:T(8,128)(2,1)S(1)}, u32[]{:S(2)}, u32[]{:S(2)}) collective-permute-start(bf16[256,256]{1,0:T(8,128)(2,1)S(1)} %select_convert_fusion), channel_id=1, source_target_pairs={{0,16},{1,17},{2,18},{3,19},{4,12},{5,13},{6,14},{7,15},{8,24},{9,... | collective-permute-start | bytes 393224 | tf_op jit(solution)/shard_map/ppermute | solution.py:34
  19.7 3.6 %collective-permute-done.3 = bf16[256,256]{1,0:T(8,128)(2,1)S(1)} collective-permute-done((bf16[256,256]{1,0:T(8,128)(2,1)S(1)}, bf16[256,256]{1,0:T(8,128)(2,1)S(1)}, u32[]{:S(2)}, u32[]{:S(2)}) %collective-permute-start.3) | collective-permute-done | bytes 131104 | tf_op jit(solution)/shard_map/ppermute | solution.py:34
  23.4 1.6 %collective-permute-start.4 = (bf16[256,256]{1,0:T(8,128)(2,1)S(1)}, bf16[256,256]{1,0:T(8,128)(2,1)S(1)}, u32[]{:S(2)}, u32[]{:S(2)}) collective-permute-start(bf16[256,256]{1,0:T(8,128)(2,1)S(1)} %add_convert_fusion.3), channel_id=1, source_target_pairs={{0,1},{1,0},{2,3},{3,2},{4,5},{5,4},{6,7},{7,6},{8,9},{9,8},{10,11... | collective-permute-start | bytes 393224 | tf_op jit(solution)/shard_map/ppermute | solution.py:34
  25.0 3.4 %collective-permute-done.4 = bf16[256,256]{1,0:T(8,128)(2,1)S(1)} collective-permute-done((bf16[256,256]{1,0:T(8,128)(2,1)S(1)}, bf16[256,256]{1,0:T(8,128)(2,1)S(1)}, u32[]{:S(2)}, u32[]{:S(2)}) %collective-permute-start.4) | collective-permute-done | bytes 131104 | tf_op jit(solution)/shard_map/ppermute | solution.py:34
  28.5 2.7 %collective-permute-start.5 = (bf16[256,256]{1,0:T(8,128)(2,1)S(1)}, bf16[256,256]{1,0:T(8,128)(2,1)S(1)}, u32[]{:S(2)}, u32[]{:S(2)}) collective-permute-start(bf16[256,256]{1,0:T(8,128)(2,1)S(1)} %add_convert_fusion.2), channel_id=1, source_target_pairs={{0,2},{1,3},{2,0},{3,1},{4,6},{5,7},{6,4},{7,5},{8,10},{9,11},{10,... | collective-permute-start | bytes 393224 | tf_op jit(solution)/shard_map/ppermute | solution.py:34
  31.1 4.8 %collective-permute-done.5 = bf16[256,256]{1,0:T(8,128)(2,1)S(1)} collective-permute-done((bf16[256,256]{1,0:T(8,128)(2,1)S(1)}, bf16[256,256]{1,0:T(8,128)(2,1)S(1)}, u32[]{:S(2)}, u32[]{:S(2)}) %collective-permute-start.5) | collective-permute-done | bytes 131104 | tf_op jit(solution)/shard_map/ppermute | solution.py:34
  36.0 1.9 %collective-permute-start.6 = (bf16[256,256]{1,0:T(8,128)(2,1)S(1)}, bf16[256,256]{1,0:T(8,128)(2,1)S(1)}, u32[]{:S(2)}, u32[]{:S(2)}) collective-permute-start(bf16[256,256]{1,0:T(8,128)(2,1)S(1)} %add_convert_fusion.1), channel_id=1, source_target_pairs={{0,16},{1,17},{2,18},{3,19},{4,12},{5,13},{6,14},{7,15},{8,24},{9,... | collective-permute-start | bytes 393224 | tf_op jit(solution)/shard_map/ppermute | solution.py:34
  37.9 3.1 %collective-permute-done.6 = bf16[256,256]{1,0:T(8,128)(2,1)S(1)} collective-permute-done((bf16[256,256]{1,0:T(8,128)(2,1)S(1)}, bf16[256,256]{1,0:T(8,128)(2,1)S(1)}, u32[]{:S(2)}, u32[]{:S(2)}) %collective-permute-start.6) | collective-permute-done | bytes 131104 | tf_op jit(solution)/shard_map/ppermute | solution.py:34
  41.2 1.4 %collective-permute-start.8 = (bf16[512,256]{1,0:T(8,128)(2,1)S(1)}, bf16[512,256]{1,0:T(8,128)(2,1)S(1)}, u32[]{:S(2)}, u32[]{:S(2)}) collective-permute-start(bf16[512,256]{1,0:T(8,128)(2,1)S(1)} %get-tuple-element.60.left_ref), channel_id=1, source_target_pairs={{0,8},{1,9},{2,10},{3,11},{4,20},{5,21},{6,22},{7,23},{8,0},{9,1},... | collective-permute-start | bytes 786440 | tf_op jit(solution)/shard_map/ppermute | solution.py:34
  42.6 0.6 project.4
  43.2 0.6 project.5
  43.8 3.8 %collective-permute-done.8.left_ref = bf16[512,256]{1,0:T(8,128)(2,1)S(1)} collective-permute-done((bf16[512,256]{1,0:T(8,128)(2,1)S(1)}, bf16[512,256]{1,0:T(8,128)(2,1)S(1)}, u32[]{:S(2)}, u32[]{:S(2)}) %collective-permute-start.8) | collective-permute-done | bytes 262176 | tf_op jit(solution)/shard_map/ppermute | solution.py:34
  47.7 0.6 project.6
  48.3 0.9 %collective-permute-done.9.left_ref = bf16[512,256]{1,0:T(8,128)(2,1)S(1)} collective-permute-done((bf16[512,256]{1,0:T(8,128)(2,1)S(1)}, bf16[512,256]{1,0:T(8,128)(2,1)S(1)}, u32[]{:S(2)}, u32[]{:S(2)}) %collective-permute-start.9) | collective-permute-done | bytes 262176 | tf_op jit(solution)/shard_map/ppermute | solution.py:34
  49.1 0.6 project.7
  49.7 0.2 collective-permute-start.10
  49.9 0.1 pad_maximum_fusion.refs_1_
  50.0 1.0 %collective-permute-done.10 = f32[2,32,256]{2,1,0:T(8,128)S(1)} collective-permute-done((f32[2,32,256]{2,1,0:T(8,128)S(1)}, f32[2,32,256]{2,1,0:T(8,128)S(1)}, u32[]{:S(2)}, u32[]{:S(2)}) %collective-permute-start.10) | collective-permute-done | bytes 65568 | tf_op jit(solution)/shard_map/ppermute | solution.py:34
  51.0 1.4 %collective-permute-start.11 = (f32[2,32,256]{2,1,0:T(8,128)S(1)}, f32[2,32,256]{2,1,0:T(8,128)S(1)}, u32[]{:S(2)}, u32[]{:S(2)}) collective-permute-start(f32[2,32,256]{2,1,0:T(8,128)S(1)} %add.60), channel_id=1, source_target_pairs={{0,8},{1,9},{2,10},{3,11},{4,12},{5,13},{6,14},{7,15},{8,0},{9,1},... | collective-permute-start | bytes 196616 | tf_op jit(solution)/shard_map/ppermute | solution.py:34
  52.4 1.9 %invert.2.refs_0_ = f32[2,32,32]{2,1,0:T(8,128)S(1)} custom-call(f32[2,32,32]{2,1,0:T(8,128)S(1)} %get-tuple-element.53.refs_0_, f32[2,32,32]{2,1,0:T(8,128)S(1)} %get-tuple-element.54.refs_1_, f32[2,32,32]{2,1,0:T(8,128)S(1)} %get-tuple-element.55.refs_2_, f32[2,32,32]{2,1,0:T(8,128)S(1)} %get-tuple-element.56.refs_3_), custom_call_target="tpu_custom_call" | custom-call | flops 2000000000 | tf_op jit(solution)/shard_map/invert/pallas_call | solution.py:204
  54.4 1.0 %collective-permute-done.11 = f32[2,32,256]{2,1,0:T(8,128)S(1)} collective-permute-done((f32[2,32,256]{2,1,0:T(8,128)S(1)}, f32[2,32,256]{2,1,0:T(8,128)S(1)}, u32[]{:S(2)}, u32[]{:S(2)}) %collective-permute-start.11) | collective-permute-done | bytes 65568 | tf_op jit(solution)/shard_map/ppermute | solution.py:34
  55.4 1.9 %collective-permute-start.12 = (f32[2,32,256]{2,1,0:T(8,128)S(1)}, f32[2,32,256]{2,1,0:T(8,128)S(1)}, u32[]{:S(2)}, u32[]{:S(2)}) collective-permute-start(f32[2,32,256]{2,1,0:T(8,128)S(1)} %add.61), channel_id=1, source_target_pairs={{0,16},{1,17},{2,18},{3,19},{4,20},{5,21},{6,22},{7,23},{8,24},{9,... | collective-permute-start | bytes 196616 | tf_op jit(solution)/shard_map/ppermute | solution.py:34
  57.2 2.0 %invert.3.refs_2_ = f32[2,32,32]{2,1,0:T(8,128)S(1)} custom-call(f32[2,32,32]{2,1,0:T(8,128)S(1)} %invert.2.refs_0_), custom_call_target="tpu_custom_call" | custom-call | flops 2000000000 | tf_op jit(solution)/shard_map/invert/pallas_call | solution.py:204
  59.2 0.5 collective-permute-done.12
  59.7 4.6 %expand.1 = bf16[2,4,2048,256]{3,2,1,0:T(8,128)(2,1)} custom-call(s32[4]{0:T(128)S(1)} %pad_add_fusion.refs_0_, bf16[4,512,256]{2,1,0:T(8,128)(2,1)S(1)} %pad_maximum_fusion.refs_1_, f32[2,32,32]{2,1,0:T(8,128)S(1)} %invert.3.refs_2_, f32[2,32,256]{2,1,0:T(8,128)S(1)} %add.62.refs_3_), custom_call_target="tpu_custom_call" | custom-call | tf_op jit(solution)/shard_map/expand/pallas_call | solution.py:244
  (26 shorter events, 0.6 us)
Async XLA Ops:
  3.7 4.2 %collective-permute-start = (bf16[512,256]{1,0:T(8,128)(2,1)S(1)}, bf16[512,256]{1,0:T(8,128)(2,1)S(1)}, u32[]{:S(2)}, u32[]{:S(2)}) collective-permute-start(bf16[512,256]{1,0:T(8,128)(2,1)S(1)} %get-tuple-element.34), channel_id=1, source_target_pairs={{0,4},{1,5},{2,6},{3,7},{4,0},{5,1},{6,2},{7,3},{8,12},{9,13},{10,... | collective-permute-start | bytes 786440 | tf_op jit(solution)/shard_map/ppermute | solution.py:34
  7.9 10.2 %collective-permute-start.2 = (bf16[512,256]{1,0:T(8,128)(2,1)S(1)}, bf16[512,256]{1,0:T(8,128)(2,1)S(1)}, u32[]{:S(2)}, u32[]{:S(2)}) collective-permute-start(bf16[512,256]{1,0:T(8,128)(2,1)S(1)} %add_convert_fusion), channel_id=1, source_target_pairs={{0,8},{1,9},{2,10},{3,11},{4,20},{5,21},{6,22},{7,23},{8,0},{9,1},... | collective-permute-start | bytes 786440 | tf_op jit(solution)/shard_map/ppermute | solution.py:34
  14.2 4.0 %collective-permute-start.1 = (bf16[512,256]{1,0:T(8,128)(2,1)S(1)}, bf16[512,256]{1,0:T(8,128)(2,1)S(1)}, u32[]{:S(2)}, u32[]{:S(2)}) collective-permute-start(bf16[512,256]{1,0:T(8,128)(2,1)S(1)} %get-tuple-element.36), channel_id=1, source_target_pairs={{0,4},{1,5},{2,6},{3,7},{4,0},{5,1},{6,2},{7,3},{8,12},{9,13},{10,... | collective-permute-start | bytes 786440 | tf_op jit(solution)/shard_map/ppermute | solution.py:34
  18.2 24.4 %copy-start.3 = (bf16[2,4,512,256]{3,2,1,0:T(8,128)(2,1)S(1)}, bf16[2,4,512,256]{3,2,1,0:T(8,128)(2,1)}, u32[]{:S(2)}) copy-start(bf16[2,4,512,256]{3,2,1,0:T(8,128)(2,1)} %get-tuple-element.39.mixed_ref) | copy-start | bytes 6291460
  18.3 5.0 %collective-permute-start.3 = (bf16[256,256]{1,0:T(8,128)(2,1)S(1)}, bf16[256,256]{1,0:T(8,128)(2,1)S(1)}, u32[]{:S(2)}, u32[]{:S(2)}) collective-permute-start(bf16[256,256]{1,0:T(8,128)(2,1)S(1)} %select_convert_fusion), channel_id=1, source_target_pairs={{0,16},{1,17},{2,18},{3,19},{4,12},{5,13},{6,14},{7,15},{8,24},{9,... | collective-permute-start | bytes 393224 | tf_op jit(solution)/shard_map/ppermute | solution.py:34
  23.4 5.0 %collective-permute-start.4 = (bf16[256,256]{1,0:T(8,128)(2,1)S(1)}, bf16[256,256]{1,0:T(8,128)(2,1)S(1)}, u32[]{:S(2)}, u32[]{:S(2)}) collective-permute-start(bf16[256,256]{1,0:T(8,128)(2,1)S(1)} %add_convert_fusion.3), channel_id=1, source_target_pairs={{0,1},{1,0},{2,3},{3,2},{4,5},{5,4},{6,7},{7,6},{8,9},{9,8},{10,11... | collective-permute-start | bytes 393224 | tf_op jit(solution)/shard_map/ppermute | solution.py:34
  28.5 7.5 %collective-permute-start.5 = (bf16[256,256]{1,0:T(8,128)(2,1)S(1)}, bf16[256,256]{1,0:T(8,128)(2,1)S(1)}, u32[]{:S(2)}, u32[]{:S(2)}) collective-permute-start(bf16[256,256]{1,0:T(8,128)(2,1)S(1)} %add_convert_fusion.2), channel_id=1, source_target_pairs={{0,2},{1,3},{2,0},{3,1},{4,6},{5,7},{6,4},{7,5},{8,10},{9,11},{10,... | collective-permute-start | bytes 393224 | tf_op jit(solution)/shard_map/ppermute | solution.py:34
  36.0 5.0 %collective-permute-start.6 = (bf16[256,256]{1,0:T(8,128)(2,1)S(1)}, bf16[256,256]{1,0:T(8,128)(2,1)S(1)}, u32[]{:S(2)}, u32[]{:S(2)}) collective-permute-start(bf16[256,256]{1,0:T(8,128)(2,1)S(1)} %add_convert_fusion.1), channel_id=1, source_target_pairs={{0,16},{1,17},{2,18},{3,19},{4,12},{5,13},{6,14},{7,15},{8,24},{9,... | collective-permute-start | bytes 393224 | tf_op jit(solution)/shard_map/ppermute | solution.py:34
  41.1 2.1 %copy-start.2 = (bf16[2,4,512,256]{3,2,1,0:T(8,128)(2,1)S(1)}, bf16[2,4,512,256]{3,2,1,0:T(8,128)(2,1)}, u32[]{:S(2)}) copy-start(bf16[2,4,512,256]{3,2,1,0:T(8,128)(2,1)} %get-tuple-element.38.mixed_ref) | copy-start | bytes 6291460
  41.1 2.1 %collective-permute-start.7 = (bf16[512,256]{1,0:T(8,128)(2,1)S(1)}, bf16[512,256]{1,0:T(8,128)(2,1)S(1)}, u32[]{:S(2)}, u32[]{:S(2)}) collective-permute-start(bf16[512,256]{1,0:T(8,128)(2,1)S(1)} %get-tuple-element.60.left_ref), channel_id=1, source_target_pairs={{0,4},{1,5},{2,6},{3,7},{4,0},{5,1},{6,2},{7,3},{8,12},{9,13},{10,... | collective-permute-start | bytes 786440 | tf_op jit(solution)/shard_map/ppermute | solution.py:34
  41.2 6.4 %collective-permute-start.8 = (bf16[512,256]{1,0:T(8,128)(2,1)S(1)}, bf16[512,256]{1,0:T(8,128)(2,1)S(1)}, u32[]{:S(2)}, u32[]{:S(2)}) collective-permute-start(bf16[512,256]{1,0:T(8,128)(2,1)S(1)} %get-tuple-element.60.left_ref), channel_id=1, source_target_pairs={{0,8},{1,9},{2,10},{3,11},{4,20},{5,21},{6,22},{7,23},{8,0},{9,1},... | collective-permute-start | bytes 786440 | tf_op jit(solution)/shard_map/ppermute | solution.py:34
  43.2 4.5 %copy-start.1 = (bf16[2,4,512,256]{3,2,1,0:T(8,128)(2,1)S(1)}, bf16[2,4,512,256]{3,2,1,0:T(8,128)(2,1)}, u32[]{:S(2)}) copy-start(bf16[2,4,512,256]{3,2,1,0:T(8,128)(2,1)} %get-tuple-element.44.mixed_ref) | copy-start | bytes 6291460
  43.8 5.4 %copy-start = (bf16[2,4,512,256]{3,2,1,0:T(8,128)(2,1)S(1)}, bf16[2,4,512,256]{3,2,1,0:T(8,128)(2,1)}, u32[]{:S(2)}) copy-start(bf16[2,4,512,256]{3,2,1,0:T(8,128)(2,1)} %get-tuple-element.43.mixed_ref) | copy-start | bytes 6291460
  47.6 1.5 %collective-permute-start.9 = (bf16[512,256]{1,0:T(8,128)(2,1)S(1)}, bf16[512,256]{1,0:T(8,128)(2,1)S(1)}, u32[]{:S(2)}, u32[]{:S(2)}) collective-permute-start(bf16[512,256]{1,0:T(8,128)(2,1)S(1)} %collective-permute-done.8.left_ref), channel_id=1, source_target_pairs={{0,4},{1,5},{2,6},{3,7},{4,0},{5,1},{6,2},{7,3},{8,12},{9,13},{10,... | collective-permute-start | bytes 786440 | tf_op jit(solution)/shard_map/ppermute | solution.py:34
  49.7 1.3 %collective-permute-start.10 = (f32[2,32,256]{2,1,0:T(8,128)S(1)}, f32[2,32,256]{2,1,0:T(8,128)S(1)}, u32[]{:S(2)}, u32[]{:S(2)}) collective-permute-start(f32[2,32,256]{2,1,0:T(8,128)S(1)} %get-tuple-element.47), channel_id=1, source_target_pairs={{0,4},{1,5},{2,6},{3,7},{4,0},{5,1},{6,2},{7,3},{8,12},{9,13},{10,... | collective-permute-start | bytes 196616 | tf_op jit(solution)/shard_map/ppermute | solution.py:34
  51.0 4.3 %collective-permute-start.11 = (f32[2,32,256]{2,1,0:T(8,128)S(1)}, f32[2,32,256]{2,1,0:T(8,128)S(1)}, u32[]{:S(2)}, u32[]{:S(2)}) collective-permute-start(f32[2,32,256]{2,1,0:T(8,128)S(1)} %add.60), channel_id=1, source_target_pairs={{0,8},{1,9},{2,10},{3,11},{4,12},{5,13},{6,14},{7,15},{8,0},{9,1},... | collective-permute-start | bytes 196616 | tf_op jit(solution)/shard_map/ppermute | solution.py:34
  55.4 4.3 %collective-permute-start.12 = (f32[2,32,256]{2,1,0:T(8,128)S(1)}, f32[2,32,256]{2,1,0:T(8,128)S(1)}, u32[]{:S(2)}, u32[]{:S(2)}) collective-permute-start(f32[2,32,256]{2,1,0:T(8,128)S(1)} %add.61), channel_id=1, source_target_pairs={{0,16},{1,17},{2,18},{3,19},{4,20},{5,21},{6,22},{7,23},{8,24},{9,... | collective-permute-start | bytes 196616 | tf_op jit(solution)/shard_map/ppermute | solution.py:34

commit v3 on v2

--- a/solution.py
+++ b/solution.py
@@ -60,6 +60,10 @@
     return pltpu.CompilerParams(vmem_limit_bytes=mib * MIB)
 
 
+def cost():
+    return pl.CostEstimate(flops=10**6, bytes_accessed=0, transcendentals=0)
+
+
 def whole():
     return pl.BlockSpec(memory_space=pltpu.VMEM)
 
@@ -72,77 +76,104 @@
     return pl.BlockSpec(memory_space=pltpu.SMEM)
 
 
-MIX_CHUNKS = 2
-
-
-def mix_kernel(start_ref, q_hbm, g_hbm, e_hbm, mixed_hbm, left_ref, q_ref, g_ref, e_ref, mixed_ref, wide_ref, q_sem, sems, out_sems):
-    m_count, pack, rows, width = mixed_ref.shape
-    rank = q_ref.shape[1]
-    block = rows // MIX_CHUNKS
-    q_copy = pltpu.make_async_copy(q_hbm, q_ref, q_sem)
-    q_copy.start()
-    start = start_ref[0]
-
-    def copies(c):
-        source = pl.ds(pl.multiple_of(start * rows + c * block, block), block)
-        where = pl.ds(c * block, block)
-        return [
+MIX_CHUNK, KEEP_CHUNK = 512, 256
+
+
+def load(starts, chunk, g_hbm, e_hbm, g_ref, e_ref, sems):
+    chunks = []
+    for c, start in enumerate(starts):
+        source = pl.ds(pl.multiple_of(start, chunk), chunk)
+        where = pl.ds(c * chunk, chunk)
+        copies = [
             pltpu.make_async_copy(hbm.at[:, :, source, :], ref.at[:, :, where, :], sems.at[k, c])
             for k, (hbm, ref) in enumerate(((g_hbm, g_ref), (e_hbm, e_ref)))
         ]
-
-    for c in range(MIX_CHUNKS):
-        for copy in copies(c):
+        for copy in copies:
             copy.start()
+        chunks.append((where, copies))
+    return chunks
+
+
+def mix_kernel(place_ref, q_hbm, g_hbm, e_hbm, first_ref, second_ref, q_ref, g_ref, e_ref, wide_ref, q_sem, sems):
+    m_count, pack, _, width = g_ref.shape
+    rank = q_ref.shape[1]
+    rows = first_ref.shape[0]
+    outs = (first_ref, second_ref)
+    starts = [place_ref[k] * rows + c * MIX_CHUNK for k in range(2) for c in range(rows // MIX_CHUNK)]
+    q_copy = pltpu.make_async_copy(q_hbm, q_ref, q_sem)
+    q_copy.start()
+    chunks = load(starts, MIX_CHUNK, g_hbm, e_hbm, g_ref, e_ref, sems)
     lane_group = lax.broadcasted_iota(jnp.int32, (width, LANES), 1) // rank
     q_copy.wait()
     for m in range(m_count):
         turned = jnp.concatenate([q_ref[m]] * pack, axis=0).T
         for j in range(pack):
             wide_ref[m, pl.ds(j * width, width), :] = jnp.where(lane_group == j, turned, 0.0).astype(BF16)
+    for c, (where, copies) in enumerate(chunks):
+        for copy in copies:
+            copy.wait()
+        left_ref = outs[c * MIX_CHUNK // rows]
+        for m in range(m_count):
+            mixed = [g_ref[m, j, where, :] + e_ref[m, j, where, :] for j in range(pack)]
+            total = jnp.dot(jnp.concatenate(mixed, axis=1), wide_ref[m], preferred_element_type=F32)
+            left_ref[pl.ds(c * MIX_CHUNK % rows, MIX_CHUNK), m * LANES:(m + 1) * LANES] = total.astype(left_ref.dtype)
+
+
+def mix(gradient, error_acc, q_turned, first, second, rows):
+    m_count, pack, _, width = gradient.shape
+    shape = (m_count, pack, 2 * rows, width)
+    return pl.pallas_call(
+        mix_kernel,
+        in_specs=[scalar()] + [pl.BlockSpec(memory_space=pltpu.HBM)] * 3,
+        out_specs=[whole()] * 2,
+        out_shape=[pltpu.VMEM((rows, m_count * LANES), dtype) for dtype in (BF16, F32)],
+        scratch_shapes=[
+            pltpu.VMEM(q_turned.shape, F32),
+            pltpu.VMEM(shape, BF16),
+            pltpu.VMEM(shape, BF16),
+            pltpu.VMEM((m_count, pack * width, LANES), BF16),
+            pltpu.SemaphoreType.DMA,
+            pltpu.SemaphoreType.DMA((2, 2 * rows // MIX_CHUNK)),
+        ],
+        compiler_params=params(16),
+        cost_estimate=cost(),
+        name="mix",
+    )(jnp.stack([first, second]).astype(jnp.int32), q_turned, gradient, error_acc)
+
+
+def keep_kernel(place_ref, g_hbm, e_hbm, mixed_hbm, g_ref, e_ref, sems, out_sems):
+    rows = g_ref.shape[2]
+    starts = [place_ref[0] * rows + c * KEEP_CHUNK for c in range(rows // KEEP_CHUNK)]
     outgoing = []
-    for c in range(MIX_CHUNKS):
-        for copy in copies(c):
+    for c, (where, copies) in enumerate(load(starts, KEEP_CHUNK, g_hbm, e_hbm, g_ref, e_ref, sems)):
+        for copy in copies:
             copy.wait()
-        where = pl.ds(c * block, block)
-        for m in range(m_count):
-            parts = []
-            for j in range(pack):
-                mixed = g_ref[m, j, where, :] + e_ref[m, j, where, :]
-                mixed_ref[m, j, where, :] = mixed
-                parts.append(mixed)
-            total = jnp.dot(jnp.concatenate(parts, axis=1), wide_ref[m], preferred_element_type=F32)
-            left_ref[where, m * LANES:(m + 1) * LANES] = total.astype(left_ref.dtype)
-        copy = pltpu.make_async_copy(mixed_ref.at[:, :, where, :], mixed_hbm.at[:, :, where, :], out_sems.at[c])
+        g_ref[:, :, where, :] = g_ref[:, :, where, :] + e_ref[:, :, where, :]
+        copy = pltpu.make_async_copy(g_ref.at[:, :, where, :], mixed_hbm.at[:, :, where, :], out_sems.at[c])
         copy.start()
         outgoing.append(copy)
     for copy in outgoing:
         copy.wait()
 
 
-def mix(gradient, error_acc, q_turned, start, rows, dtype):
+def keep(gradient, error_acc, place, rows):
     m_count, pack, _, width = gradient.shape
-    elements = m_count * pack * rows * width
     shape = (m_count, pack, rows, width)
     return pl.pallas_call(
-        mix_kernel,
-        in_specs=[scalar()] + [pl.BlockSpec(memory_space=pltpu.HBM)] * 3,
-        out_specs=[pl.BlockSpec(memory_space=pltpu.HBM), whole()],
-        out_shape=[pltpu.HBM(shape, BF16), pltpu.VMEM((rows, m_count * LANES), dtype)],
+        keep_kernel,
+        in_specs=[scalar()] + [pl.BlockSpec(memory_space=pltpu.HBM)] * 2,
+        out_specs=pl.BlockSpec(memory_space=pltpu.HBM),
+        out_shape=pltpu.HBM(shape, BF16),
         scratch_shapes=[
-            pltpu.VMEM(q_turned.shape, F32),
             pltpu.VMEM(shape, BF16),
             pltpu.VMEM(shape, BF16),
-            pltpu.VMEM(shape, BF16),
-            pltpu.VMEM((m_count, pack * width, LANES), BF16),
-            pltpu.SemaphoreType.DMA,
-            pltpu.SemaphoreType.DMA((2, MIX_CHUNKS)),
-            pltpu.SemaphoreType.DMA((MIX_CHUNKS,)),
+            pltpu.SemaphoreType.DMA((2, rows // KEEP_CHUNK)),
+            pltpu.SemaphoreType.DMA((rows // KEEP_CHUNK,)),
         ],
-        compiler_params=params(16),
-        cost_estimate=pl.CostEstimate(flops=2 * elements * LANES, bytes_accessed=4 * elements, transcendentals=0),
-        name="mix",
-    )(start.astype(jnp.int32).reshape(1), q_turned, gradient, error_acc)
+        compiler_params=params(12),
+        cost_estimate=cost(),
+        name="keep",
+    )(place.astype(jnp.int32).reshape(1), gradient, error_acc)
 
 
 def project_kernel(left_ref, mixed_ref, *refs):
@@ -166,7 +197,6 @@
 def project(left, mixed, *before):
     m_count, pack, rows, width = mixed.shape
     rank = LANES // pack
-    elements = m_count * pack * rows * width
     mixed = pltpu.with_memory_space_constraint(mixed, pltpu.VMEM)
     return pl.pallas_call(
         project_kernel,
@@ -174,7 +204,7 @@
         out_specs=[whole()] * 2,
         out_shape=[pltpu.VMEM((m_count, rank, width), F32), pltpu.VMEM((m_count, rank, rank), F32)],
         compiler_params=params(8),
-        cost_estimate=pl.CostEstimate(flops=2 * elements * LANES * 4, bytes_accessed=0, transcendentals=0),
+        cost_estimate=cost(),
         name="project",
     )(left, mixed, *before)
 
@@ -207,9 +237,24 @@
         out_specs=whole(),
         out_shape=pltpu.VMEM(grams[0].shape, F32),
         compiler_params=params(4),
-        cost_estimate=pl.CostEstimate(flops=2 * 10**9, bytes_accessed=0, transcendentals=0),
+        cost_estimate=cost(),
         name="invert",
     )(*grams)
+
+
+def three_parts(x):
+    high = x.astype(BF16)
+    rest = x - high.astype(F32)
+    middle = rest.astype(BF16)
+    return high, middle, (rest - middle.astype(F32)).astype(BF16)
+
+
+def small_dot(a, b):
+    a0, a1, a2 = three_parts(a)
+    b0, b1, b2 = three_parts(b)
+    wide = jnp.concatenate([a0, a0, a1, a1, a0, a2], axis=1)
+    tall = jnp.concatenate([b0, b1, b0, b1, b2, b0], axis=0)
+    return jnp.dot(wide, tall, preferred_element_type=F32)
 
 
 def expand_kernel(scale, place_ref, left_ref, inverse_ref, right_ref, update_ref, wide_ref, held_ref, sems):
@@ -219,7 +264,7 @@
     wide_ref[...] = jnp.zeros_like(wide_ref)
     copies = []
     for m in range(m_count):
-        z = jnp.dot(inverse_ref[m], right_ref[m], precision=lax.Precision.HIGHEST, preferred_element_type=F32) * scale
+        z = small_dot(inverse_ref[m], right_ref[m]) * scale
         high = z.astype(BF16)
         low = (z - high.astype(F32)).astype(BF16)
         for j in range(pack):
@@ -262,13 +307,17 @@
     rank = right.shape[1]
     for b in range(bits(hst)):
         right = right + exchange(right, lambda o, h, t, b=b: (o, h ^ (1 << b), t))
-    right, grams = lax.optimization_barrier((right, grams))
-    inverse = invert(range(rank // 2), *grams)
-    for b in range(bits(outer)):
-        right = right + exchange(right, lambda o, h, t, b=b: (o ^ (1 << b), h, t))
-        if b == 0:
-            right, inverse = lax.optimization_barrier((right, inverse))
-    return right, invert(range(rank // 2, rank), inverse)
+    early = rank * 3 // 8
+    right, inverse = after(right, invert(range(early), *grams))
+    parts = [right] + [exchange(right, lambda o, h, t, k=k: (o ^ k, h, t)) for k in range(1, outer)]
+    inverse = invert(range(early, rank), inverse)
+    while len(parts) > 1:
+        parts = [parts[k] + parts[k + 1] for k in range(0, len(parts), 2)]
+    return parts[0], inverse
+
+
+def after(value, *others):
+    return lax.optimization_barrier((value, *others))
 
 
 def shards(gradient, error_acc, q_start):
@@ -284,42 +333,45 @@
     b0, b1, beyond = bit0(o, h), bit1(o, h), bit1(o, h ^ 1)
     at_own, at_side = 2 * b0 + b1, 2 * b0 + 1 - b1
     at_far, at_far_side = 2 * (1 - b0) + beyond, 2 * (1 - b0) + 1 - beyond
-
-    def mixed_left(at, dtype):
-        return mix(gradient, error_acc, q_turned, at, quarter, dtype)
-
-    mixed_far_side, left_far_side = mixed_left(at_far_side, BF16)
-    came_side = exchange(left_far_side, partner0)
-    mixed_side, left_side = mixed_left(at_side, F32)
-    sent, at_far_late = lax.optimization_barrier(((left_side + came_side.astype(F32)).astype(BF16), at_far))
+    waiting, mixed = [at_own, at_far, at_side, at_far_side], []
+
+    def swap(x, partner):
+        if not waiting:
+            return exchange(x, partner)
+        x, at = after(x, waiting.pop(0))
+        kept = keep(gradient, error_acc, at, quarter)
+        came, kept = after(exchange(x, partner), kept)
+        mixed.append(kept)
+        return came
+
+    left_far_side, left = mix(gradient, error_acc, q_turned, at_far_side, at_side, quarter)
+    left = left + exchange(left_far_side, partner0).astype(F32)
+    sent, at = after(left.astype(BF16), at_far)
     side = exchange(sent, partner1)
-    mixed_far, left_far = mixed_left(at_far_late, BF16)
-    came_own = exchange(left_far, partner0)
-    mixed_own, left = mixed_left(at_own, F32)
-    left = left + came_own.astype(F32) + side.astype(F32)
+    left_far, left = mix(gradient, error_acc, q_turned, at, at_own, quarter)
+    left = left + exchange(left_far, partner0).astype(F32) + side.astype(F32)
     for partner, bit in steps[2:]:
         b = bit(o, h)
-        left = pick(left, b) + exchange(pick(left, 1 - b).astype(BF16), partner).astype(F32)
+        left = pick(left, b) + swap(pick(left, 1 - b).astype(BF16), partner).astype(F32)
     for b in range(bits(lax.axis_size("tp"))):
         sent = left.astype(BF16)
-        left = sent.astype(F32) + exchange(sent, lambda o, h, t, b=b: (o, h, t ^ (1 << b))).astype(F32)
+        left = sent.astype(F32) + swap(sent, lambda o, h, t, b=b: (o, h, t ^ (1 << b))).astype(F32)
     own = left.astype(BF16)
 
     for partner, bit in reversed(steps[2:]):
         b = bit(o, h)
-        other = exchange(own, partner)
+        other = swap(own, partner)
         own = jnp.concatenate([jnp.where(b == 1, other, own), jnp.where(b == 1, own, other)])
     far = exchange(own, partner0)
     side = exchange(own, partner1)
-    right, gram_own = project(own, mixed_own)
-    right, gram_far = project(far, mixed_far, right)
-    side, right = lax.optimization_barrier((side, right))
+    right, gram_own = project(own, mixed[0])
+    right, gram_far = project(far, mixed[1], right)
+    side, right = after(side, right)
     far_side = exchange(side, partner0)
-    right, gram_side = project(side, mixed_side, right)
-    right, gram_far_side = project(far_side, mixed_far_side, right)
-
-    near, beyond = (gram_own, gram_side), (gram_far, gram_far_side)
-    right, inverse = sum_right(right, near + beyond)
+    right, gram_side = project(side, mixed[2], right)
+    right, gram_far_side = project(far_side, mixed[3], right)
+
+    right, inverse = sum_right(right, (gram_own, gram_side, gram_far, gram_far_side))
     outer, hst, _ = sizes()
     pieces = jnp.stack([own, far, side, far_side])
     places = jnp.stack([at_own, at_far, at_side, at_far_side]).astype(jnp.int32)

time: 64.5 us -> 61.9 us (0.960)
  waiting for transfers between devices: 22.1 us -> 11.1 us
  Pallas kernels: 25.6 us -> 34 us
    pallas_call x0 -> x4, Pallas kernels: none -> 13.4 us  [keep(): pl.pallas_call(keep_kernel, in_specs=[scalar()] + [pl.BlockSpec(memory_sp...]
    ppermute x13 -> x14, waiting for transfers between devices: 22.1 us -> 11.1 us  [exchange(): return lax.ppermute(x, AXES, pairs)]
    pallas_call x4 -> x2, Pallas kernels: 14.7 us -> 9.74 us  [mix(): pl.pallas_call(mix_kernel, in_specs=[scalar()] + [pl.BlockSpec(memory_spa...]
    ppermute x13 -> x14, starting transfers between devices: 15.9 us -> 15.8 us  [exchange(): return lax.ppermute(x, AXES, pairs)]
  transfers between devices with their start and end apart: 13 -> 14, of which waited for: 9 -> 10; matrix products, arithmetic and copies ran while one was open for 0% -> 0% of each run, Pallas kernels for 26% -> 39%
where the time goes in v3:
time: 61.9 us; the launch traced here: 61.7 us
  Pallas kernels  34 us (55%)
  starting transfers between devices  15.8 us (26%)
  waiting for transfers between devices  11.1 us (18%)
  other arithmetic  0.71 us (1%)
    ppermute x14, starting transfers between devices, exchange(): return lax.ppermute(x, AXES, pairs)  15.8 us
    pallas_call x4, Pallas kernels, keep(): pl.pallas_call(keep_kernel, in_specs=[scalar()] + [pl.BlockSpec(memory_sp...  13.4 us
    ppermute x14, waiting for transfers between devices, exchange(): return lax.ppermute(x, AXES, pairs)  11.1 us
    pallas_call x2, Pallas kernels, mix(): pl.pallas_call(mix_kernel, in_specs=[scalar()] + [pl.BlockSpec(memory_spa...  9.74 us
    pallas_call x1, Pallas kernels, expand(): pl.pallas_call(lambda *refs: expand_kernel(scale, *refs), in_specs=[scala...  4.63 us
    pallas_call x2, Pallas kernels, invert(): pl.pallas_call(lambda *refs: invert_kernel(steps, *refs), in_specs=[whole...  3.9 us
    pallas_call x4, Pallas kernels, project(): pl.pallas_call(project_kernel, in_specs=[whole()] * (2 + len(before)), ou...  2.32 us
  transfers between devices with their start and end apart: 14, of which 10 were waited for; matrix products, arithmetic and copies ran while one was open for 0% of the time, Pallas kernels for 39%

profile of v3, /device:TPU:0, one launch (start us, length us, event | category | flops | bytes accessed | tf_op | source)
XLA Modules:
  0.0 61.7 jit_solution(11023999170260434628)
XLA Ops:
  0.1 4.9 %mix.2 = (bf16[512,256]{1,0:T(8,128)(2,1)S(1)}, f32[512,256]{1,0:T(8,128)S(1)}) custom-call(s32[2]{0:T(128)S(1)} %pad_add_fusion.1.place_ref, f32[2,32,256]{2,1,0:T(8,128)} %bitcast.33, bf16[2,4,2048,256]{3,2,1,0:T(8,128)(2,1)} %bitcast.21, bf16[2,4,2048,256]{3,2,1,0:T(8,128)(2,1)} %bitcast.27), custom_call_target="tpu_custom_call" | custom-call | flops 1000000 | tf_op jit(solution)/shard_map/mix/pallas_call | solution.py:125
  5.0 0.5 collective-permute-start
  5.5 1.2 %collective-permute-done = bf16[512,256]{1,0:T(8,128)(2,1)S(1)} collective-permute-done((bf16[512,256]{1,0:T(8,128)(2,1)S(1)}, bf16[512,256]{1,0:T(8,128)(2,1)S(1)}, u32[]{:S(2)}, u32[]{:S(2)}) %collective-permute-start) | collective-permute-done | bytes 262176 | tf_op jit(solution)/shard_map/ppermute | solution.py:34
  6.7 2.9 %collective-permute-start.2 = (bf16[512,256]{1,0:T(8,128)(2,1)S(1)}, bf16[512,256]{1,0:T(8,128)(2,1)S(1)}, u32[]{:S(2)}, u32[]{:S(2)}) collective-permute-start(bf16[512,256]{1,0:T(8,128)(2,1)S(1)} %add_convert_fusion), channel_id=1, source_target_pairs={{0,8},{1,9},{2,10},{3,11},{4,20},{5,21},{6,22},{7,23},{8,0},{9,1},... | collective-permute-start | bytes 786440 | tf_op jit(solution)/shard_map/ppermute | solution.py:34
  9.7 4.9 %mix.3 = (bf16[512,256]{1,0:T(8,128)(2,1)S(1)}, f32[512,256]{1,0:T(8,128)S(1)}) custom-call(s32[2]{0:T(128)S(1)} %pad_add_fusion.2.place_ref, f32[2,32,256]{2,1,0:T(8,128)} %bitcast.34, bf16[2,4,2048,256]{3,2,1,0:T(8,128)(2,1)} %bitcast.22, bf16[2,4,2048,256]{3,2,1,0:T(8,128)(2,1)} %bitcast.28), custom_call_target="tpu_custom_call" | custom-call | flops 1000000 | tf_op jit(solution)/shard_map/mix/pallas_call | solution.py:125
  14.7 1.5 %collective-permute-done.1 = bf16[512,256]{1,0:T(8,128)(2,1)S(1)} collective-permute-done((bf16[512,256]{1,0:T(8,128)(2,1)S(1)}, bf16[512,256]{1,0:T(8,128)(2,1)S(1)}, u32[]{:S(2)}, u32[]{:S(2)}) %collective-permute-start.1) | collective-permute-done | bytes 262176 | tf_op jit(solution)/shard_map/ppermute | solution.py:34
  16.3 1.6 %collective-permute-start.3 = (bf16[256,256]{1,0:T(8,128)(2,1)S(1)}, bf16[256,256]{1,0:T(8,128)(2,1)S(1)}, u32[]{:S(2)}, u32[]{:S(2)}) collective-permute-start(bf16[256,256]{1,0:T(8,128)(2,1)S(1)} %select_convert_fusion), channel_id=1, source_target_pairs={{0,16},{1,17},{2,18},{3,19},{4,12},{5,13},{6,14},{7,15},{8,24},{9,... | collective-permute-start | bytes 393224 | tf_op jit(solution)/shard_map/ppermute | solution.py:34
  17.9 3.3 %keep.4.mixed_ref = bf16[2,4,512,256]{3,2,1,0:T(8,128)(2,1)} custom-call(s32[1]{0:T(128)} %bitcast.8.place_ref, bf16[2,4,2048,256]{3,2,1,0:T(8,128)(2,1)} %bitcast.23, bf16[2,4,2048,256]{3,2,1,0:T(8,128)(2,1)} %bitcast.29), custom_call_target="tpu_custom_call" | custom-call | flops 1000000 | tf_op jit(solution)/shard_map/keep/pallas_call | solution.py:162
  21.2 0.1 collective-permute-done.3
  21.4 1.6 %collective-permute-start.4 = (bf16[256,256]{1,0:T(8,128)(2,1)S(1)}, bf16[256,256]{1,0:T(8,128)(2,1)S(1)}, u32[]{:S(2)}, u32[]{:S(2)}) collective-permute-start(bf16[256,256]{1,0:T(8,128)(2,1)S(1)} %add_convert_fusion.3), channel_id=1, source_target_pairs={{0,1},{1,0},{2,3},{3,2},{4,5},{5,4},{6,7},{7,6},{8,9},{9,8},{10,11... | collective-permute-start | bytes 393224 | tf_op jit(solution)/shard_map/ppermute | solution.py:34
  23.0 3.3 %keep.5.mixed_ref = bf16[2,4,512,256]{3,2,1,0:T(8,128)(2,1)} custom-call(s32[1]{0:T(128)} %bitcast.9.place_ref, bf16[2,4,2048,256]{3,2,1,0:T(8,128)(2,1)} %bitcast.24, bf16[2,4,2048,256]{3,2,1,0:T(8,128)(2,1)} %bitcast.30), custom_call_target="tpu_custom_call" | custom-call | flops 1000000 | tf_op jit(solution)/shard_map/keep/pallas_call | solution.py:162
  26.4 2.7 %collective-permute-start.5 = (bf16[256,256]{1,0:T(8,128)(2,1)S(1)}, bf16[256,256]{1,0:T(8,128)(2,1)S(1)}, u32[]{:S(2)}, u32[]{:S(2)}) collective-permute-start(bf16[256,256]{1,0:T(8,128)(2,1)S(1)} %add_convert_fusion.2), channel_id=1, source_target_pairs={{0,2},{1,3},{2,0},{3,1},{4,6},{5,7},{6,4},{7,5},{8,10},{9,11},{10,... | collective-permute-start | bytes 393224 | tf_op jit(solution)/shard_map/ppermute | solution.py:34
  29.1 3.3 %keep.6.mixed_ref = bf16[2,4,512,256]{3,2,1,0:T(8,128)(2,1)} custom-call(s32[1]{0:T(128)} %bitcast.10.place_ref, bf16[2,4,2048,256]{3,2,1,0:T(8,128)(2,1)} %bitcast.25, bf16[2,4,2048,256]{3,2,1,0:T(8,128)(2,1)} %bitcast.31), custom_call_target="tpu_custom_call" | custom-call | flops 1000000 | tf_op jit(solution)/shard_map/keep/pallas_call | solution.py:162
  32.4 2.3 %collective-permute-done.5 = bf16[256,256]{1,0:T(8,128)(2,1)S(1)} collective-permute-done((bf16[256,256]{1,0:T(8,128)(2,1)S(1)}, bf16[256,256]{1,0:T(8,128)(2,1)S(1)}, u32[]{:S(2)}, u32[]{:S(2)}) %collective-permute-start.5) | collective-permute-done | bytes 131104 | tf_op jit(solution)/shard_map/ppermute | solution.py:34
  34.7 1.4 %collective-permute-start.6 = (bf16[256,256]{1,0:T(8,128)(2,1)S(1)}, bf16[256,256]{1,0:T(8,128)(2,1)S(1)}, u32[]{:S(2)}, u32[]{:S(2)}) collective-permute-start(bf16[256,256]{1,0:T(8,128)(2,1)S(1)} %add_convert_fusion.1), channel_id=1, source_target_pairs={{0,16},{1,17},{2,18},{3,19},{4,12},{5,13},{6,14},{7,15},{8,24},{9,... | collective-permute-start | bytes 393224 | tf_op jit(solution)/shard_map/ppermute | solution.py:34
  36.2 3.5 %keep.7.mixed_ref = bf16[2,4,512,256]{3,2,1,0:T(8,128)(2,1)} custom-call(s32[1]{0:T(128)} %bitcast.11.place_ref, bf16[2,4,2048,256]{3,2,1,0:T(8,128)(2,1)} %bitcast.26, bf16[2,4,2048,256]{3,2,1,0:T(8,128)(2,1)} %bitcast.32), custom_call_target="tpu_custom_call" | custom-call | flops 1000000 | tf_op jit(solution)/shard_map/keep/pallas_call | solution.py:162
  39.9 1.1 %collective-permute-start.8 = (bf16[512,256]{1,0:T(8,128)(2,1)S(1)}, bf16[512,256]{1,0:T(8,128)(2,1)S(1)}, u32[]{:S(2)}, u32[]{:S(2)}) collective-permute-start(bf16[512,256]{1,0:T(8,128)(2,1)S(1)} %get-tuple-element.74.left_ref), channel_id=1, source_target_pairs={{0,8},{1,9},{2,10},{3,11},{4,20},{5,21},{6,22},{7,23},{8,0},{9,1},... | collective-permute-start | bytes 786440 | tf_op jit(solution)/shard_map/ppermute | solution.py:34
  41.1 0.6 project.4
  41.7 0.6 project.5
  42.3 4.1 %collective-permute-done.8.left_ref = bf16[512,256]{1,0:T(8,128)(2,1)S(1)} collective-permute-done((bf16[512,256]{1,0:T(8,128)(2,1)S(1)}, bf16[512,256]{1,0:T(8,128)(2,1)S(1)}, u32[]{:S(2)}, u32[]{:S(2)}) %collective-permute-start.8) | collective-permute-done | bytes 262176 | tf_op jit(solution)/shard_map/ppermute | solution.py:34
  46.4 0.6 project.6
  46.9 0.9 %collective-permute-done.9.left_ref = bf16[512,256]{1,0:T(8,128)(2,1)S(1)} collective-permute-done((bf16[512,256]{1,0:T(8,128)(2,1)S(1)}, bf16[512,256]{1,0:T(8,128)(2,1)S(1)}, u32[]{:S(2)}, u32[]{:S(2)}) %collective-permute-start.9) | collective-permute-done | bytes 262176 | tf_op jit(solution)/shard_map/ppermute | solution.py:34
  47.9 0.6 project.7
  48.5 0.2 collective-permute-start.10
  48.7 1.4 %invert.2.refs_0_ = f32[2,32,32]{2,1,0:T(8,128)S(1)} custom-call(f32[2,32,32]{2,1,0:T(8,128)S(1)} %get-tuple-element.67.refs_0_, f32[2,32,32]{2,1,0:T(8,128)S(1)} %get-tuple-element.68.refs_1_, f32[2,32,32]{2,1,0:T(8,128)S(1)} %get-tuple-element.69.refs_2_, f32[2,32,32]{2,1,0:T(8,128)S(1)} %get-tuple-element.70.refs_3_), custom_call_target="tpu_custom_call" | custom-call | flops 1000000 | tf_op jit(solution)/shard_map/invert/pallas_call | solution.py:234
  50.2 1.8 %collective-permute-start.13 = (f32[2,32,256]{2,1,0:T(8,128)S(1)}, f32[2,32,256]{2,1,0:T(8,128)S(1)}, u32[]{:S(2)}, u32[]{:S(2)}) collective-permute-start(f32[2,32,256]{2,1,0:T(8,128)S(1)} %add.63), channel_id=1, source_target_pairs={{0,24},{1,25},{2,26},{3,27},{4,28},{5,29},{6,30},{7,31},{8,16},{9,... | collective-permute-start | bytes 196616 | tf_op jit(solution)/shard_map/ppermute | solution.py:34
  52.0 0.8 %collective-permute-start.12 = (f32[2,32,256]{2,1,0:T(8,128)S(1)}, f32[2,32,256]{2,1,0:T(8,128)S(1)}, u32[]{:S(2)}, u32[]{:S(2)}) collective-permute-start(f32[2,32,256]{2,1,0:T(8,128)S(1)} %add.63), channel_id=1, source_target_pairs={{0,16},{1,17},{2,18},{3,19},{4,20},{5,21},{6,22},{7,23},{8,24},{9,... | collective-permute-start | bytes 196616 | tf_op jit(solution)/shard_map/ppermute | solution.py:34
  52.8 1.0 %collective-permute-start.11 = (f32[2,32,256]{2,1,0:T(8,128)S(1)}, f32[2,32,256]{2,1,0:T(8,128)S(1)}, u32[]{:S(2)}, u32[]{:S(2)}) collective-permute-start(f32[2,32,256]{2,1,0:T(8,128)S(1)} %add.63), channel_id=1, source_target_pairs={{0,8},{1,9},{2,10},{3,11},{4,12},{5,13},{6,14},{7,15},{8,0},{9,1},... | collective-permute-start | bytes 196616 | tf_op jit(solution)/shard_map/ppermute | solution.py:34
  53.9 2.5 %invert.3.refs_2_ = f32[2,32,32]{2,1,0:T(8,128)S(1)} custom-call(f32[2,32,32]{2,1,0:T(8,128)S(1)} %invert.2.refs_0_), custom_call_target="tpu_custom_call" | custom-call | flops 1000000 | tf_op jit(solution)/shard_map/invert/pallas_call | solution.py:234
  56.4 0.6 collective-permute-done.12
  56.9 0.1 collective-permute-done.11
  57.1 4.6 %expand.1 = bf16[2,4,2048,256]{3,2,1,0:T(8,128)(2,1)} custom-call(s32[4]{0:T(128)S(1)} %pad_add_fusion.refs_0_, bf16[4,512,256]{2,1,0:T(8,128)(2,1)S(1)} %pad_maximum_fusion.refs_1_, f32[2,32,32]{2,1,0:T(8,128)S(1)} %invert.3.refs_2_, f32[2,32,256]{2,1,0:T(8,128)S(1)} %add_add_fusion.refs_3_), custom_call_target="tpu_custom_call" | custom-call | tf_op jit(solution)/shard_map/expand/pallas_call | solution.py:289
  (31 shorter events, 1.1 us)
Async XLA Ops:
  5.0 1.7 %collective-permute-start = (bf16[512,256]{1,0:T(8,128)(2,1)S(1)}, bf16[512,256]{1,0:T(8,128)(2,1)S(1)}, u32[]{:S(2)}, u32[]{:S(2)}) collective-permute-start(bf16[512,256]{1,0:T(8,128)(2,1)S(1)} %get-tuple-element.40), channel_id=1, source_target_pairs={{0,4},{1,5},{2,6},{3,7},{4,0},{5,1},{6,2},{7,3},{8,12},{9,13},{10,... | collective-permute-start | bytes 786440 | tf_op jit(solution)/shard_map/ppermute | solution.py:34
  6.7 8.0 %collective-permute-start.2 = (bf16[512,256]{1,0:T(8,128)(2,1)S(1)}, bf16[512,256]{1,0:T(8,128)(2,1)S(1)}, u32[]{:S(2)}, u32[]{:S(2)}) collective-permute-start(bf16[512,256]{1,0:T(8,128)(2,1)S(1)} %add_convert_fusion), channel_id=1, source_target_pairs={{0,8},{1,9},{2,10},{3,11},{4,20},{5,21},{6,22},{7,23},{8,0},{9,1},... | collective-permute-start | bytes 786440 | tf_op jit(solution)/shard_map/ppermute | solution.py:34
  14.6 1.6 %collective-permute-start.1 = (bf16[512,256]{1,0:T(8,128)(2,1)S(1)}, bf16[512,256]{1,0:T(8,128)(2,1)S(1)}, u32[]{:S(2)}, u32[]{:S(2)}) collective-permute-start(bf16[512,256]{1,0:T(8,128)(2,1)S(1)} %get-tuple-element.43), channel_id=1, source_target_pairs={{0,4},{1,5},{2,6},{3,7},{4,0},{5,1},{6,2},{7,3},{8,12},{9,13},{10,... | collective-permute-start | bytes 786440 | tf_op jit(solution)/shard_map/ppermute | solution.py:34
  16.3 5.0 %collective-permute-start.3 = (bf16[256,256]{1,0:T(8,128)(2,1)S(1)}, bf16[256,256]{1,0:T(8,128)(2,1)S(1)}, u32[]{:S(2)}, u32[]{:S(2)}) collective-permute-start(bf16[256,256]{1,0:T(8,128)(2,1)S(1)} %select_convert_fusion), channel_id=1, source_target_pairs={{0,16},{1,17},{2,18},{3,19},{4,12},{5,13},{6,14},{7,15},{8,24},{9,... | collective-permute-start | bytes 393224 | tf_op jit(solution)/shard_map/ppermute | solution.py:34
  21.4 5.0 %collective-permute-start.4 = (bf16[256,256]{1,0:T(8,128)(2,1)S(1)}, bf16[256,256]{1,0:T(8,128)(2,1)S(1)}, u32[]{:S(2)}, u32[]{:S(2)}) collective-permute-start(bf16[256,256]{1,0:T(8,128)(2,1)S(1)} %add_convert_fusion.3), channel_id=1, source_target_pairs={{0,1},{1,0},{2,3},{3,2},{4,5},{5,4},{6,7},{7,6},{8,9},{9,8},{10,11... | collective-permute-start | bytes 393224 | tf_op jit(solution)/shard_map/ppermute | solution.py:34
  26.4 8.3 %collective-permute-start.5 = (bf16[256,256]{1,0:T(8,128)(2,1)S(1)}, bf16[256,256]{1,0:T(8,128)(2,1)S(1)}, u32[]{:S(2)}, u32[]{:S(2)}) collective-permute-start(bf16[256,256]{1,0:T(8,128)(2,1)S(1)} %add_convert_fusion.2), channel_id=1, source_target_pairs={{0,2},{1,3},{2,0},{3,1},{4,6},{5,7},{6,4},{7,5},{8,10},{9,11},{10,... | collective-permute-start | bytes 393224 | tf_op jit(solution)/shard_map/ppermute | solution.py:34
  34.7 5.0 %collective-permute-start.6 = (bf16[256,256]{1,0:T(8,128)(2,1)S(1)}, bf16[256,256]{1,0:T(8,128)(2,1)S(1)}, u32[]{:S(2)}, u32[]{:S(2)}) collective-permute-start(bf16[256,256]{1,0:T(8,128)(2,1)S(1)} %add_convert_fusion.1), channel_id=1, source_target_pairs={{0,16},{1,17},{2,18},{3,19},{4,12},{5,13},{6,14},{7,15},{8,24},{9,... | collective-permute-start | bytes 393224 | tf_op jit(solution)/shard_map/ppermute | solution.py:34
  36.1 4.9 %copy-start = (bf16[2,4,512,256]{3,2,1,0:T(8,128)(2,1)S(1)}, bf16[2,4,512,256]{3,2,1,0:T(8,128)(2,1)}, u32[]{:S(2)}) copy-start(bf16[2,4,512,256]{3,2,1,0:T(8,128)(2,1)} %keep.4.mixed_ref) | copy-start | bytes 6291460
  39.6 2.0 %copy-start.2 = (bf16[2,4,512,256]{3,2,1,0:T(8,128)(2,1)S(1)}, bf16[2,4,512,256]{3,2,1,0:T(8,128)(2,1)}, u32[]{:S(2)}) copy-start(bf16[2,4,512,256]{3,2,1,0:T(8,128)(2,1)} %keep.5.mixed_ref) | copy-start | bytes 6291460
  39.8 6.5 %copy-start.1 = (bf16[2,4,512,256]{3,2,1,0:T(8,128)(2,1)S(1)}, bf16[2,4,512,256]{3,2,1,0:T(8,128)(2,1)}, u32[]{:S(2)}) copy-start(bf16[2,4,512,256]{3,2,1,0:T(8,128)(2,1)} %keep.6.mixed_ref) | copy-start | bytes 6291460
  39.8 1.8 %collective-permute-start.7 = (bf16[512,256]{1,0:T(8,128)(2,1)S(1)}, bf16[512,256]{1,0:T(8,128)(2,1)S(1)}, u32[]{:S(2)}, u32[]{:S(2)}) collective-permute-start(bf16[512,256]{1,0:T(8,128)(2,1)S(1)} %get-tuple-element.74.left_ref), channel_id=1, source_target_pairs={{0,4},{1,5},{2,6},{3,7},{4,0},{5,1},{6,2},{7,3},{8,12},{9,13},{10,... | collective-permute-start | bytes 786440 | tf_op jit(solution)/shard_map/ppermute | solution.py:34
  39.9 6.4 %collective-permute-start.8 = (bf16[512,256]{1,0:T(8,128)(2,1)S(1)}, bf16[512,256]{1,0:T(8,128)(2,1)S(1)}, u32[]{:S(2)}, u32[]{:S(2)}) collective-permute-start(bf16[512,256]{1,0:T(8,128)(2,1)S(1)} %get-tuple-element.74.left_ref), channel_id=1, source_target_pairs={{0,8},{1,9},{2,10},{3,11},{4,20},{5,21},{6,22},{7,23},{8,0},{9,1},... | collective-permute-start | bytes 786440 | tf_op jit(solution)/shard_map/ppermute | solution.py:34
  41.7 6.2 %copy-start.3 = (bf16[2,4,512,256]{3,2,1,0:T(8,128)(2,1)S(1)}, bf16[2,4,512,256]{3,2,1,0:T(8,128)(2,1)}, u32[]{:S(2)}) copy-start(bf16[2,4,512,256]{3,2,1,0:T(8,128)(2,1)} %keep.7.mixed_ref) | copy-start | bytes 6291460
  46.4 1.5 %collective-permute-start.9 = (bf16[512,256]{1,0:T(8,128)(2,1)S(1)}, bf16[512,256]{1,0:T(8,128)(2,1)S(1)}, u32[]{:S(2)}, u32[]{:S(2)}) collective-permute-start(bf16[512,256]{1,0:T(8,128)(2,1)S(1)} %collective-permute-done.8.left_ref), channel_id=1, source_target_pairs={{0,4},{1,5},{2,6},{3,7},{4,0},{5,1},{6,2},{7,3},{8,12},{9,13},{10,... | collective-permute-start | bytes 786440 | tf_op jit(solution)/shard_map/ppermute | solution.py:34
  48.5 1.7 %collective-permute-start.10 = (f32[2,32,256]{2,1,0:T(8,128)S(1)}, f32[2,32,256]{2,1,0:T(8,128)S(1)}, u32[]{:S(2)}, u32[]{:S(2)}) collective-permute-start(f32[2,32,256]{2,1,0:T(8,128)S(1)} %get-tuple-element.66), channel_id=1, source_target_pairs={{0,4},{1,5},{2,6},{3,7},{4,0},{5,1},{6,2},{7,3},{8,12},{9,13},{10,... | collective-permute-start | bytes 196616 | tf_op jit(solution)/shard_map/ppermute | solution.py:34
  50.2 6.2 %collective-permute-start.13 = (f32[2,32,256]{2,1,0:T(8,128)S(1)}, f32[2,32,256]{2,1,0:T(8,128)S(1)}, u32[]{:S(2)}, u32[]{:S(2)}) collective-permute-start(f32[2,32,256]{2,1,0:T(8,128)S(1)} %add.63), channel_id=1, source_target_pairs={{0,24},{1,25},{2,26},{3,27},{4,28},{5,29},{6,30},{7,31},{8,16},{9,... | collective-permute-start | bytes 196616 | tf_op jit(solution)/shard_map/ppermute | solution.py:34
  52.0 4.9 %collective-permute-start.12 = (f32[2,32,256]{2,1,0:T(8,128)S(1)}, f32[2,32,256]{2,1,0:T(8,128)S(1)}, u32[]{:S(2)}, u32[]{:S(2)}) collective-permute-start(f32[2,32,256]{2,1,0:T(8,128)S(1)} %add.63), channel_id=1, source_target_pairs={{0,16},{1,17},{2,18},{3,19},{4,20},{5,21},{6,22},{7,23},{8,24},{9,... | collective-permute-start | bytes 196616 | tf_op jit(solution)/shard_map/ppermute | solution.py:34
  52.8 4.3 %collective-permute-start.11 = (f32[2,32,256]{2,1,0:T(8,128)S(1)}, f32[2,32,256]{2,1,0:T(8,128)S(1)}, u32[]{:S(2)}, u32[]{:S(2)}) collective-permute-start(f32[2,32,256]{2,1,0:T(8,128)S(1)} %add.63), channel_id=1, source_target_pairs={{0,8},{1,9},{2,10},{3,11},{4,12},{5,13},{6,14},{7,15},{8,0},{9,1},... | collective-permute-start | bytes 196616 | tf_op jit(solution)/shard_map/ppermute | solution.py:34

commit v4 on v3

v4 whole, which is shorter than its diff:
```python
import jax
import jax.numpy as jnp
from jax import lax
from jax.experimental import pallas as pl
from jax.experimental.pallas import tpu as pltpu
from jax.sharding import PartitionSpec as P

AXES = ("outer", "hst", "tp")
PACK = 4
LANES = 128
F32, BF16 = jnp.float32, jnp.bfloat16
MIB = 1024 * 1024


def bits(size):
    return size.bit_length() - 1


def sizes():
    return tuple(lax.axis_size(axis) for axis in AXES)


def coordinates(index):
    _, hst, tp = sizes()
    return index // (hst * tp), index // tp % hst, index % tp


def exchange(x, partner):
    _, hst, tp = sizes()
    pairs = []
    for index in range(sizes()[0] * hst * tp):
        o, h, t = partner(*coordinates(index))
        pairs.append((index, (o * hst + h) * tp + t))
    return lax.ppermute(x, AXES, pairs)


def pick(x, index):
    half = x.shape[0] // 2
    return jnp.where(index == 1, x[half:], x[:half])


def params(mib):
    return pltpu.CompilerParams(vmem_limit_bytes=mib * MIB)


def cost():
    return pl.CostEstimate(flops=10**6, bytes_accessed=0, transcendentals=0)


def whole():
    return pl.BlockSpec(memory_space=pltpu.VMEM)


def in_hbm(x):
    return pltpu.with_memory_space_constraint(x, pltpu.HBM)


def scalar():
    return pl.BlockSpec(memory_space=pltpu.SMEM)


def load(starts, rows, g_hbm, e_hbm, g_ref, e_ref, sems):
    chunks = []
    for c, start in enumerate(starts):
        source = pl.ds(pl.multiple_of(start, rows), rows)
        where = pl.ds(c * rows, rows)
        copies = [
            pltpu.make_async_copy(hbm.at[:, :, source, :], ref.at[:, :, where, :], sems.at[k, c])
            for k, (hbm, ref) in enumerate(((g_hbm, g_ref), (e_hbm, e_ref)))
        ]
        chunks.append((where, copies))
    return chunks


def start_all(copies):
    for k, copy in enumerate(copies):
        copy.start(priority=1)


def wait_all(copies):
    for copy in copies:
        copy.wait()


FETCHES = 4


def mix_kernel(place_ref, q_hbm, g_hbm, e_hbm, *refs):
    mixed_hbm = refs[2] if len(refs) == 10 else None
    first_ref, second_ref = refs[:2]
    q_ref, g_ref, e_ref, wide_ref, q_sem, sems, out_sems = refs[-7:]
    m_count, pack, total_rows, width = g_ref.shape
    rank = q_ref.shape[1]
    count = place_ref.shape[0]
    rows = total_rows // count
    q_copy = pltpu.make_async_copy(q_hbm, q_ref, q_sem)
    q_copy.start()
    chunks = load([place_ref[c] * rows for c in range(count)], rows, g_hbm, e_hbm, g_ref, e_ref, sems)
    for _, copies in chunks[:FETCHES]:
        start_all(copies)
    lane_group = lax.broadcasted_iota(jnp.int32, (width, LANES), 1) // rank
    q_copy.wait()
    for m in range(m_count):
        turned = jnp.concatenate([q_ref[m]] * pack, axis=0).T
        for j in range(pack):
            wide_ref[m, pl.ds(j * width, width), :] = jnp.where(lane_group == j, turned, 0.0).astype(BF16)
    outgoing = []
    for c, (where, copies) in enumerate(chunks):
        wait_all(copies)
        if c + FETCHES < count:
            start_all(chunks[c + FETCHES][1])
        left_ref = first_ref if c < count // 2 else second_ref
        at = pl.ds(c % (count // 2) * rows, rows)
        for m in range(m_count):
            mixed = [g_ref[m, j, where, :] + e_ref[m, j, where, :] for j in range(pack)]
            total = jnp.dot(jnp.concatenate(mixed, axis=1), wide_ref[m], preferred_element_type=F32)
            left_ref[at, m * LANES:(m + 1) * LANES] = total.astype(left_ref.dtype)
            if mixed_hbm is not None:
                for j in range(pack):
                    g_ref[m, j, where, :] = mixed[j]
        if mixed_hbm is not None:
            copy = pltpu.make_async_copy(g_ref.at[:, :, where, :], mixed_hbm.at[:, :, where, :], out_sems.at[c])
            copy.start()
            outgoing.append(copy)
    wait_all(outgoing)


def mix(gradient, error_acc, q_turned, first, second, rows, kept=False):
    m_count, pack, _, width = gradient.shape
    places = jnp.stack(first + second).astype(jnp.int32)
    count = len(first + second)
    shape = (m_count, pack, count * rows, width)
    hbm = pl.BlockSpec(memory_space=pltpu.HBM)
    return pl.pallas_call(
        mix_kernel,
        in_specs=[scalar()] + [hbm] * 3,
        out_specs=[whole()] * 2 + [hbm] * kept,
        out_shape=[pltpu.VMEM((len(first) * rows, m_count * LANES), dtype) for dtype in (BF16, F32)] + [pltpu.HBM(shape, BF16)] * kept,
        scratch_shapes=[
            pltpu.VMEM(q_turned.shape, F32),
            pltpu.VMEM(shape, BF16),
            pltpu.VMEM(shape, BF16),
            pltpu.VMEM((m_count, pack * width, LANES), BF16),
            pltpu.SemaphoreType.DMA,
            pltpu.SemaphoreType.DMA((2, count)),
            pltpu.SemaphoreType.DMA((count,)),
        ],
        compiler_params=params(20),
        cost_estimate=cost(),
        name="mix",
    )(places, q_turned, gradient, error_acc)


def keep_kernel(place_ref, g_hbm, e_hbm, mixed_hbm, g_ref, e_ref, sems, out_sems):
    count = place_ref.shape[0]
    rows = g_ref.shape[2] // count
    outgoing = []
    chunks = load([place_ref[c] * rows for c in range(count)], rows, g_hbm, e_hbm, g_ref, e_ref, sems)
    for _, copies in chunks:
        start_all(copies)
    for c, (where, copies) in enumerate(chunks):
        wait_all(copies)
        g_ref[:, :, where, :] = g_ref[:, :, where, :] + e_ref[:, :, where, :]
        copy = pltpu.make_async_copy(g_ref.at[:, :, where, :], mixed_hbm.at[:, :, where, :], out_sems.at[c])
        copy.start()
        outgoing.append(copy)
    wait_all(outgoing)


def keep(gradient, error_acc, places, rows):
    m_count, pack, _, width = gradient.shape
    count = len(places)
    shape = (m_count, pack, count * rows, width)
    return pl.pallas_call(
        keep_kernel,
        in_specs=[scalar()] + [pl.BlockSpec(memory_space=pltpu.HBM)] * 2,
        out_specs=pl.BlockSpec(memory_space=pltpu.HBM),
        out_shape=pltpu.HBM(shape, BF16),
        scratch_shapes=[
            pltpu.VMEM(shape, BF16),
            pltpu.VMEM(shape, BF16),
            pltpu.SemaphoreType.DMA((2, count)),
            pltpu.SemaphoreType.DMA((count,)),
        ],
        compiler_params=params(16),
        cost_estimate=cost(),
        name="keep",
    )(jnp.stack(places).astype(jnp.int32), gradient, error_acc)


def project_kernel(chunks, *refs):
    count = len(chunks)
    lefts, right_ref, gram_ref = refs[:count], refs[-2], refs[-1]
    stores = 1 + max(store for store, _ in chunks)
    mixed = refs[count:count + stores]
    before = refs[count + stores:-2]
    m_count, pack, _, width = mixed[0].shape
    rank = LANES // pack
    right = [before[0][m] if before else jnp.zeros((rank, width), F32) for m in range(m_count)]
    for c, (store, place) in enumerate(chunks):
        left = lefts[c][...]
        rows = left.shape[0]
        turned = left.T
        every = jnp.dot(turned, left, preferred_element_type=F32)
        for m in range(m_count):
            gram = jnp.zeros((rank, rank), F32)
            for j in range(pack):
                at = m * LANES + j * rank
                gram += every[at:at + rank, at:at + rank]
                block = mixed[store][m, j, pl.ds(place * rows, rows), :]
                right[m] += jnp.dot(turned[at:at + rank], block, preferred_element_type=F32)
            gram_ref[c, m] = gram
    for m in range(m_count):
        right_ref[m] = right[m]


def project(lefts, mixed, chunks, *before):
    m_count, pack, _, width = mixed[0].shape
    rank = LANES // pack
    mixed = [pltpu.with_memory_space_constraint(x, pltpu.VMEM) for x in mixed]
    return pl.pallas_call(
        lambda *refs: project_kernel(chunks, *refs),
        in_specs=[whole()] * (len(lefts) + len(mixed) + len(before)),
        out_specs=[whole()] * 2,
        out_shape=[pltpu.VMEM((m_count, rank, width), F32), pltpu.VMEM((len(lefts), m_count, rank, rank), F32)],
        compiler_params=params(8),
        cost_estimate=cost(),
        name="project",
    )(*lefts, *mixed, *before)


def tree_sum(parts):
    while len(parts) > 1:
        parts = [parts[k] + parts[k + 1] for k in range(0, len(parts), 2)]
    return parts[0]


def invert_kernel(steps, *refs):
    grams, held_ref = refs[:-1], refs[-1]
    m_count, rank, _ = held_ref.shape
    row_at = lax.broadcasted_iota(jnp.int32, (rank, rank), 0)
    col_at = lax.broadcasted_iota(jnp.int32, (rank, rank), 1)
    held = [grams[0][m] for m in range(m_count)] if len(grams) == 1 else [
        tree_sum([grams[0][0, m]] + [grams[1][c, m] for c in range(grams[1].shape[0])])
        + tree_sum([grams[0][1, m]] + [grams[2][c, m] for c in range(grams[2].shape[0])])
        for m in range(m_count)
    ]
    for k in steps:
        for m in range(m_count):
            a = held[m]
            row, col = a[k:k + 1, :], a[:, k:k + 1]
            inv = 1.0 / a[k:k + 1, k:k + 1]
            scaled = row * inv
            rest = a - col * scaled
            rest = jnp.where(row_at == k, scaled, rest)
            held[m] = jnp.where(col_at == k, jnp.where(row_at == k, inv, -col * inv), rest)
    for m in range(m_count):
        held_ref[m] = held[m]


def invert(steps, *grams):
    return pl.pallas_call(
        lambda *refs: invert_kernel(steps, *refs),
        in_specs=[whole()] * len(grams),
        out_specs=whole(),
        out_shape=pltpu.VMEM(grams[0].shape[-3:], F32),
        compiler_params=params(4),
        cost_estimate=cost(),
        name="invert",
    )(*grams)


def three_parts(x):
    high = x.astype(BF16)
    rest = x - high.astype(F32)
    middle = rest.astype(BF16)
    return high, middle, (rest - middle.astype(F32)).astype(BF16)


def small_dot(a, b):
    a0, a1, a2 = three_parts(a)
    b0, b1, b2 = three_parts(b)
    wide = jnp.concatenate([a0, a0, a1, a1, a0, a2], axis=1)
    tall = jnp.concatenate([b0, b1, b0, b1, b2, b0], axis=0)
    return jnp.dot(wide, tall, preferred_element_type=F32)


def expand_kernel(scale, place_ref, left_ref, inverse_ref, right_ref, update_ref, wide_ref, held_ref, sems):
    m_count, rank, width = right_ref.shape
    pack = LANES // rank
    count, block, _ = left_ref.shape
    wide_ref[...] = jnp.zeros_like(wide_ref)
    copies = []
    for m in range(m_count):
        z = small_dot(inverse_ref[m], right_ref[m]) * scale
        high = z.astype(BF16)
        low = (z - high.astype(F32)).astype(BF16)
        for j in range(pack):
            wide_ref[m, j, pl.ds(j * rank, rank), :] = high
            wide_ref[m, j, pl.ds(LANES + j * rank, rank), :] = low
            for p in range(count):
                left = left_ref[p, :, m * LANES:(m + 1) * LANES]
                rows = jnp.dot(jnp.concatenate([left, left], axis=1), wide_ref[m, j], preferred_element_type=F32)
                held_ref[m, j, p] = rows.astype(BF16)
                where = pl.ds(pl.multiple_of(place_ref[p] * block, block), block)
                copy = pltpu.make_async_copy(held_ref.at[m, j, p], update_ref.at[m, j, where, :], sems.at[m, j, p])
                copy.start(priority=p % 2)
                copies.append(copy)
    for copy in copies:
        copy.wait()


def expand(pieces, places, inverse, right, scale):
    m_count, rank, width = right.shape
    pack = LANES // rank
    count, block, _ = pieces.shape
    out = pl.pallas_call(
        lambda *refs: expand_kernel(scale, *refs),
        in_specs=[scalar(), whole(), whole(), whole()],
        out_specs=pl.BlockSpec(memory_space=pl.ANY),
        out_shape=jax.ShapeDtypeStruct((m_count, pack, count * block, width), BF16),
        scratch_shapes=[
            pltpu.VMEM((m_count, pack, 2 * LANES, width), BF16),
            pltpu.VMEM((m_count, pack, count, block, width), BF16),
            pltpu.SemaphoreType.DMA((m_count, pack, count)),
        ],
        compiler_params=params(20),
        name="expand",
    )(places, pieces, inverse, right)
    return out.reshape(m_count, pack * count * block, width)


def sum_right(right, grams):
    outer, hst, _ = sizes()
    rank = right.shape[1]
    for b in range(bits(hst)):
        right = right + exchange(right, lambda o, h, t, b=b: (o, h ^ (1 << b), t))
    early = rank * 3 // 8
    right, inverse = after(right, invert(range(early), *grams))
    parts = [right] + [exchange(right, lambda o, h, t, k=k: (o ^ k, h, t)) for k in range(1, outer)]
    inverse = invert(range(early, rank), inverse)
    return tree_sum(parts), inverse


def after(value, *others):
    return lax.optimization_barrier((value, *others))


def shards(gradient, error_acc, q_start):
    _, m_count, depth, width = gradient.shape
    outer, hst, tp = sizes()
    rows = depth // PACK
    chunk = rows // (2 * outer)
    shape = (m_count, PACK, rows, width)
    gradient, error_acc = in_hbm(gradient.reshape(shape)), in_hbm(error_acc.reshape(shape))
    q_turned = in_hbm(jnp.swapaxes(q_start, 1, 2))
    o, h = lax.axis_index("outer"), lax.axis_index("hst")
    near = [(h & 1) * outer + (o ^ k) for k in range(outer)]
    far = [(1 - (h & 1)) * outer + (o ^ k) for k in range(outer)]

    def core(x):
        return exchange(x, lambda o, h, t: (o, h ^ 1, t))

    def chip(x, k):
        return exchange(x, lambda o, h, t: (o ^ k, h, t))

    def after_all(value, places):
        value, *places = after(value, *places)
        return value, places

    left_far, left = mix(gradient, error_acc, q_turned, far[1:], near[1:], chunk)
    sent = (left + core(left_far).astype(F32)).astype(BF16)
    sent, (at_far, at_near) = after_all(sent, [far[0], near[0]])
    came = [chip(sent[(k - 1) * chunk:k * chunk], k) for k in range(1, outer)]
    left_far, left, mixed_own = mix(gradient, error_acc, q_turned, [at_far], [at_near], chunk, True)
    left = left + core(left_far).astype(F32)
    for part in came:
        left = left + part.astype(F32)
    for b in range(1, bits(hst)):
        bit = (h >> b) & 1
        sent = pick(left, 1 - bit).astype(BF16)
        left = pick(left, bit) + exchange(sent, lambda o, h, t, b=b: (o, h ^ (1 << b), t)).astype(F32)
    others = near[1:] + far[1:]
    early, late = len(others) // 6, len(others) * 2 // 3
    waiting, mixed = [others[:early], others[early:late]], []
    for b in range(bits(tp)):
        sent = left.astype(BF16)
        places = waiting.pop(0) if waiting else None
        if places:
            sent, places = after_all(sent, places)
            kept = keep(gradient, error_acc, places, chunk)
        got = exchange(sent, lambda o, h, t, b=b: (o, h, t ^ (1 << b)))
        if places:
            got, kept = after(got, kept)
            mixed.append(kept)
        left = sent.astype(F32) + got.astype(F32)
    mixed += [keep(gradient, error_acc, places, chunk) for places in waiting]
    own = left.astype(BF16)

    for b in reversed(range(1, bits(hst))):
        bit = (h >> b) & 1
        got = exchange(own, lambda o, h, t, b=b: (o, h ^ (1 << b), t))
        own = jnp.concatenate([jnp.where(bit == 1, got, own), jnp.where(bit == 1, own, got)])
    own, places = after_all(own, others[late:])
    near_left, far_left = [own], [core(own)]
    came = [chip(own, k) for k in range(1, outer)]
    right, gram_own = project([own, far_left[0]], [mixed_own], [(0, 1), (0, 0)])
    mixed.append(keep(gradient, error_acc, places, chunk))
    came[-1], right, mixed[2] = after(came[-1], right, mixed[2])
    near_left += came
    far_left += [core(part) for part in came]
    where = [(0, k) for k in range(early)] + [(1, k) for k in range(late - early)] + [(2, k) for k in range(len(others) - late)]
    n = outer - 1

    def project_others(lefts, chunks, right):
        used = sorted({store for store, _ in chunks})
        chunks = [(used.index(store), place) for store, place in chunks]
        return project(lefts, [mixed[store] for store in used], chunks, right)

    right, gram_near = project_others(near_left[1:], where[:n], right)
    right, gram_far = project_others(far_left[1:], where[n:], right)

    right, inverse = sum_right(right, (gram_own, gram_near, gram_far))
    pieces = jnp.stack(near_left + far_left)
    places = jnp.stack(near + far).astype(jnp.int32)
    return expand(pieces, places, inverse, right, 1.0 / (outer * hst))


def solution(mesh):
    in_specs = (
        P(("outer", "hst"), None, None, "tp"),
        P(("outer", "hst"), None, None, "tp"),
        P(None, "tp", None),
    )
    out_specs = P(None, None, "tp")
    return jax.shard_map(shards, mesh=mesh, in_specs=in_specs, out_specs=out_specs, check_vma=False)
```

time: 61.9 us -> 58.7 us (0.948)
  waiting for transfers between devices: 11.1 us -> 7.54 us
  starting transfers between devices: 15.8 us -> 17.5 us
  Pallas kernels: 34 us -> 32.5 us
    ppermute x14 -> x18, waiting for transfers between devices: 11.1 us -> 7.54 us  [exchange(): return lax.ppermute(x, AXES, pairs)]
    ppermute x14 -> x18, starting transfers between devices: 15.8 us -> 17.5 us  [exchange(): return lax.ppermute(x, AXES, pairs)]
    pallas_call x4 -> x3, Pallas kernels: 13.4 us -> 11.7 us  [keep(): pl.pallas_call(keep_kernel, in_specs=[scalar()] + [pl.BlockSpec(memory_sp...]
    pallas_call x6 -> x5, Pallas kernels: 12.1 us -> 12.1 us  [the longest x2 10 us: mix(): pl.pallas_call(mix_kernel, in_specs=[scalar()] + [hbm] * 3, out_specs=[wh...]
  transfers between devices with their start and end apart: 14 -> 18, of which waited for: 10 -> 8; matrix products, arithmetic and copies ran while one was open for 0% -> 1% of each run, Pallas kernels for 39% -> 36%
where the time goes in v4:
time: 58.7 us; the launch traced here: 58.6 us
  Pallas kernels  32.5 us (55%)
  starting transfers between devices  17.5 us (30%)
  waiting for transfers between devices  7.54 us (13%)
    ppermute x18, starting transfers between devices, exchange(): return lax.ppermute(x, AXES, pairs)  17.5 us
    pallas_call x3, Pallas kernels, keep(): pl.pallas_call(keep_kernel, in_specs=[scalar()] + [pl.BlockSpec(memory_sp...  11.7 us
    pallas_call x2, Pallas kernels, mix(): pl.pallas_call(mix_kernel, in_specs=[scalar()] + [hbm] * 3, out_specs=[wh...  10 us
    ppermute x18, waiting for transfers between devices, exchange(): return lax.ppermute(x, AXES, pairs)  7.54 us
    pallas_call x1, Pallas kernels, expand(): pl.pallas_call(lambda *refs: expand_kernel(scale, *refs), in_specs=[scala...  4.77 us
    pallas_call x2, Pallas kernels, invert(): pl.pallas_call(lambda *refs: invert_kernel(steps, *refs), in_specs=[whole...  3.91 us
    pallas_call x3, Pallas kernels, project(): pl.pallas_call(lambda *refs: project_kernel(chunks, *refs), in_specs=[who...  2.07 us
  transfers between devices with their start and end apart: 18, of which 8 were waited for; matrix products, arithmetic and copies ran while one was open for 1% of the time, Pallas kernels for 36%

profile of v4, /device:TPU:0, one launch (start us, length us, event | category | flops | bytes accessed | tf_op | source)
XLA Modules:
  0.0 58.6 jit_solution(17492459680423942518)
XLA Ops:
  0.1 6.0 %mix.2 = (bf16[768,256]{1,0:T(8,128)(2,1)S(1)}, f32[768,256]{1,0:T(8,128)S(1)}) custom-call(s32[6]{0:T(128)S(1)} %stack.105.place_ref, f32[2,32,256]{2,1,0:T(8,128)} %bitcast.46, bf16[2,4,2048,256]{3,2,1,0:T(8,128)(2,1)} %bitcast.36, bf16[2,4,2048,256]{3,2,1,0:T(8,128)(2,1)} %bitcast.41), custom_call_target="tpu_custom_call" | custom-call | flops 1000000 | tf_op jit(solution)/shard_map/mix/pallas_call | solution.py:134
  6.1 0.5 collective-permute-start
  6.6 1.3 %collective-permute-done = bf16[768,256]{1,0:T(8,128)(2,1)S(1)} collective-permute-done((bf16[768,256]{1,0:T(8,128)(2,1)S(1)}, bf16[768,256]{1,0:T(8,128)(2,1)S(1)}, u32[]{:S(2)}, u32[]{:S(2)}) %collective-permute-start) | collective-permute-done | bytes 393248 | tf_op jit(solution)/shard_map/ppermute | solution.py:34
  8.1 2.9 %collective-permute-start.2 = (bf16[256,256]{1,0:T(8,128)(2,1)S(1)}, bf16[256,256]{1,0:T(8,128)(2,1)S(1)}, u32[]{:S(2)}, u32[]{:S(2)}) collective-permute-start(bf16[256,256]{1,0:T(8,128)(2,1)S(1)} %get-tuple-element.69), channel_id=1, source_target_pairs={{0,8},{1,9},{2,10},{3,11},{4,12},{5,13},{6,14},{7,15},{8,0},{9,1},... | collective-permute-start | bytes 393224 | tf_op jit(solution)/shard_map/ppermute | solution.py:34
  11.0 1.5 %collective-permute-start.4 = (bf16[256,256]{1,0:T(8,128)(2,1)S(1)}, bf16[256,256]{1,0:T(8,128)(2,1)S(1)}, u32[]{:S(2)}, u32[]{:S(2)}) collective-permute-start(bf16[256,256]{1,0:T(8,128)(2,1)S(1)} %get-tuple-element.70), channel_id=1, source_target_pairs={{0,24},{1,25},{2,26},{3,27},{4,28},{5,29},{6,30},{7,31},{8,16},{9,... | collective-permute-start | bytes 393224 | tf_op jit(solution)/shard_map/ppermute | solution.py:34
  12.6 4.1 %mix.3 = (bf16[256,256]{1,0:T(8,128)(2,1)S(1)}, f32[256,256]{1,0:T(8,128)S(1)}, bf16[2,4,512,256]{3,2,1,0:T(8,128)(2,1)}) custom-call(s32[2]{0:T(128)S(1)} %pad_add_fusion.place_ref, f32[2,32,256]{2,1,0:T(8,128)} %bitcast.47, bf16[2,4,2048,256]{3,2,1,0:T(8,128)(2,1)} %bitcast.37, bf16[2,4,2048,256]{3,2,1,0:T(8,128)(2,1)} %bitcast.42), custom_call_target="tpu_custom_call" | custom-call | flops 1000000 | tf_op jit(solution)/shard_map/mix/pallas_call | solution.py:134
  16.8 2.1 %collective-permute-done.4 = bf16[256,256]{1,0:T(8,128)(2,1)S(1)} collective-permute-done((bf16[256,256]{1,0:T(8,128)(2,1)S(1)}, bf16[256,256]{1,0:T(8,128)(2,1)S(1)}, u32[]{:S(2)}, u32[]{:S(2)}) %collective-permute-start.4) | collective-permute-done | bytes 131104 | tf_op jit(solution)/shard_map/ppermute | solution.py:34
  18.9 1.4 %collective-permute-done.3 = bf16[256,256]{1,0:T(8,128)(2,1)S(1)} collective-permute-done((bf16[256,256]{1,0:T(8,128)(2,1)S(1)}, bf16[256,256]{1,0:T(8,128)(2,1)S(1)}, u32[]{:S(2)}, u32[]{:S(2)}) %collective-permute-start.3) | collective-permute-done | bytes 131104 | tf_op jit(solution)/shard_map/ppermute | solution.py:34
  20.4 1.6 %collective-permute-start.5 = (bf16[256,256]{1,0:T(8,128)(2,1)S(1)}, bf16[256,256]{1,0:T(8,128)(2,1)S(1)}, u32[]{:S(2)}, u32[]{:S(2)}) collective-permute-start(bf16[256,256]{1,0:T(8,128)(2,1)S(1)} %add_convert_fusion.3), channel_id=1, source_target_pairs={{0,1},{1,0},{2,3},{3,2},{4,5},{5,4},{6,7},{7,6},{8,9},{9,8},{10,11... | collective-permute-start | bytes 393224 | tf_op jit(solution)/shard_map/ppermute | solution.py:34
  22.0 2.7 %keep.3.refs_3_ = bf16[2,4,256,256]{3,2,1,0:T(8,128)(2,1)} custom-call(s32[1]{0:T(128)} %bitcast.13.place_ref, bf16[2,4,2048,256]{3,2,1,0:T(8,128)(2,1)} %bitcast.38, bf16[2,4,2048,256]{3,2,1,0:T(8,128)(2,1)} %bitcast.43), custom_call_target="tpu_custom_call" | custom-call | flops 1000000 | tf_op jit(solution)/shard_map/keep/pallas_call | solution.py:174
  24.7 0.7 %collective-permute-done.5 = bf16[256,256]{1,0:T(8,128)(2,1)S(1)} collective-permute-done((bf16[256,256]{1,0:T(8,128)(2,1)S(1)}, bf16[256,256]{1,0:T(8,128)(2,1)S(1)}, u32[]{:S(2)}, u32[]{:S(2)}) %collective-permute-start.5) | collective-permute-done | bytes 131104 | tf_op jit(solution)/shard_map/ppermute | solution.py:34
  25.5 2.7 %collective-permute-start.6 = (bf16[256,256]{1,0:T(8,128)(2,1)S(1)}, bf16[256,256]{1,0:T(8,128)(2,1)S(1)}, u32[]{:S(2)}, u32[]{:S(2)}) collective-permute-start(bf16[256,256]{1,0:T(8,128)(2,1)S(1)} %add_convert_fusion.2), channel_id=1, source_target_pairs={{0,2},{1,3},{2,0},{3,1},{4,6},{5,7},{6,4},{7,5},{8,10},{9,11},{10,... | collective-permute-start | bytes 393224 | tf_op jit(solution)/shard_map/ppermute | solution.py:34
  28.3 4.9 %keep.4.refs_4_.refs_3_ = bf16[2,4,768,256]{3,2,1,0:T(8,128)(2,1)} custom-call(s32[3]{0:T(128)S(1)} %pad_add_fusion.1.place_ref, bf16[2,4,2048,256]{3,2,1,0:T(8,128)(2,1)} %bitcast.39, bf16[2,4,2048,256]{3,2,1,0:T(8,128)(2,1)} %bitcast.44), custom_call_target="tpu_custom_call" | custom-call | flops 1000000 | tf_op jit(solution)/shard_map/keep/pallas_call | solution.py:174
  33.3 1.5 %collective-permute-start.9 = (bf16[256,256]{1,0:T(8,128)(2,1)S(1)}, bf16[256,256]{1,0:T(8,128)(2,1)S(1)}, u32[]{:S(2)}, u32[]{:S(2)}) collective-permute-start(bf16[256,256]{1,0:T(8,128)(2,1)S(1)} %add_convert_fusion.1.refs_0_), channel_id=1, source_target_pairs={{0,24},{1,25},{2,26},{3,27},{4,28},{5,29},{6,30},{7,31},{8,16},{9,... | collective-permute-start | bytes 393224 | tf_op jit(solution)/shard_map/ppermute | solution.py:34
  34.8 1.5 %collective-permute-start.8 = (bf16[256,256]{1,0:T(8,128)(2,1)S(1)}, bf16[256,256]{1,0:T(8,128)(2,1)S(1)}, u32[]{:S(2)}, u32[]{:S(2)}) collective-permute-start(bf16[256,256]{1,0:T(8,128)(2,1)S(1)} %add_convert_fusion.1.refs_0_), channel_id=1, source_target_pairs={{0,16},{1,17},{2,18},{3,19},{4,20},{5,21},{6,22},{7,23},{8,24},{9,... | collective-permute-start | bytes 393224 | tf_op jit(solution)/shard_map/ppermute | solution.py:34
  36.3 0.5 collective-permute-start.7
  36.9 4.1 %keep.5.refs_4_ = bf16[2,4,512,256]{3,2,1,0:T(8,128)(2,1)} custom-call(s32[2]{0:T(128)S(1)} %pad_add_fusion.2.place_ref, bf16[2,4,2048,256]{3,2,1,0:T(8,128)(2,1)} %bitcast.40, bf16[2,4,2048,256]{3,2,1,0:T(8,128)(2,1)} %bitcast.45), custom_call_target="tpu_custom_call" | custom-call | flops 1000000 | tf_op jit(solution)/shard_map/keep/pallas_call | solution.py:174
  41.1 0.5 project.3
  41.7 0.3 collective-permute-done.7.refs_0_
  42.0 0.9 %collective-permute-done.8.refs_1_ = bf16[256,256]{1,0:T(8,128)(2,1)S(1)} collective-permute-done((bf16[256,256]{1,0:T(8,128)(2,1)S(1)}, bf16[256,256]{1,0:T(8,128)(2,1)S(1)}, u32[]{:S(2)}, u32[]{:S(2)}) %collective-permute-start.8) | collective-permute-done | bytes 131104 | tf_op jit(solution)/shard_map/ppermute | solution.py:34
  43.0 0.5 collective-permute-start.11
  43.5 0.8 %project.4 = (f32[2,32,256]{2,1,0:T(8,128)S(1)}, f32[3,2,32,32]{3,2,1,0:T(8,128)S(1)}) custom-call(bf16[256,256]{1,0:T(8,128)(2,1)S(1)} %collective-permute-done.7.refs_0_, bf16[256,256]{1,0:T(8,128)(2,1)S(1)} %collective-permute-done.8.refs_1_, bf16[256,256]{1,0:T(8,128)(2,1)S(1)} %collective-permute-done.9.refs_2_, bf16[2,4,256,256]{3,2,1,0:T(8,128)(2,1)S(1)} %copy-done.2, ...), custom_call_target="tpu_custom_call" | custom-call | flops 1000000 | tf_op jit(solution)/shard_map/project/pallas_call | solution.py:221
  44.4 0.2 collective-permute-done.11.refs_0_
  44.5 0.8 %project.5 = (f32[2,32,256]{2,1,0:T(8,128)S(1)}, f32[3,2,32,32]{3,2,1,0:T(8,128)S(1)}) custom-call(bf16[256,256]{1,0:T(8,128)(2,1)S(1)} %collective-permute-done.11.refs_0_, bf16[256,256]{1,0:T(8,128)(2,1)S(1)} %collective-permute-done.12.refs_1_, bf16[256,256]{1,0:T(8,128)(2,1)S(1)} %collective-permute-done.13.refs_2_, ...), custom_call_target="tpu_custom_call" | custom-call | flops 1000000 | tf_op jit(solution)/shard_map/project/pallas_call | solution.py:221
  45.3 0.4 collective-permute-start.14
  45.7 1.4 %invert.2.refs_0_ = f32[2,32,32]{2,1,0:T(8,128)S(1)} custom-call(f32[2,2,32,32]{3,2,1,0:T(8,128)S(1)} %get-tuple-element.64.refs_0_, f32[3,2,32,32]{3,2,1,0:T(8,128)S(1)} %get-tuple-element.65.refs_1_, f32[3,2,32,32]{3,2,1,0:T(8,128)S(1)} %get-tuple-element.66.refs_2_), custom_call_target="tpu_custom_call" | custom-call | flops 1000000 | tf_op jit(solution)/shard_map/invert/pallas_call | solution.py:262
  47.2 1.6 %collective-permute-start.17 = (f32[2,32,256]{2,1,0:T(8,128)S(1)}, f32[2,32,256]{2,1,0:T(8,128)S(1)}, u32[]{:S(2)}, u32[]{:S(2)}) collective-permute-start(f32[2,32,256]{2,1,0:T(8,128)S(1)} %add.72), channel_id=1, source_target_pairs={{0,24},{1,25},{2,26},{3,27},{4,28},{5,29},{6,30},{7,31},{8,16},{9,... | collective-permute-start | bytes 196616 | tf_op jit(solution)/shard_map/ppermute | solution.py:34
  48.8 0.7 %collective-permute-start.16 = (f32[2,32,256]{2,1,0:T(8,128)S(1)}, f32[2,32,256]{2,1,0:T(8,128)S(1)}, u32[]{:S(2)}, u32[]{:S(2)}) collective-permute-start(f32[2,32,256]{2,1,0:T(8,128)S(1)} %add.72), channel_id=1, source_target_pairs={{0,16},{1,17},{2,18},{3,19},{4,20},{5,21},{6,22},{7,23},{8,24},{9,... | collective-permute-start | bytes 196616 | tf_op jit(solution)/shard_map/ppermute | solution.py:34
  49.5 1.2 %collective-permute-start.15 = (f32[2,32,256]{2,1,0:T(8,128)S(1)}, f32[2,32,256]{2,1,0:T(8,128)S(1)}, u32[]{:S(2)}, u32[]{:S(2)}) collective-permute-start(f32[2,32,256]{2,1,0:T(8,128)S(1)} %add.72), channel_id=1, source_target_pairs={{0,8},{1,9},{2,10},{3,11},{4,12},{5,13},{6,14},{7,15},{8,0},{9,1},... | collective-permute-start | bytes 196616 | tf_op jit(solution)/shard_map/ppermute | solution.py:34
  50.8 2.5 %invert.3.refs_2_ = f32[2,32,32]{2,1,0:T(8,128)S(1)} custom-call(f32[2,32,32]{2,1,0:T(8,128)S(1)} %invert.2.refs_0_), custom_call_target="tpu_custom_call" | custom-call | flops 1000000 | tf_op jit(solution)/shard_map/invert/pallas_call | solution.py:262
  53.2 0.5 collective-permute-done.16
  53.8 4.8 %expand.1 = bf16[2,4,2048,256]{3,2,1,0:T(8,128)(2,1)} custom-call(s32[8]{0:T(128)S(1)} %stack.104.refs_0_, bf16[8,256,256]{2,1,0:T(8,128)(2,1)S(1)} %bitcast_dynamic-update-slice_fusion.refs_1_, f32[2,32,32]{2,1,0:T(8,128)S(1)} %invert.3.refs_2_, f32[2,32,256]{2,1,0:T(8,128)S(1)} %add_add_fusion.refs_3_), custom_call_target="tpu_custom_call" | custom-call | tf_op jit(solution)/shard_map/expand/pallas_call | solution.py:317
  (43 shorter events, 1.3 us)
Async XLA Ops:
  6.1 1.9 %collective-permute-start = (bf16[768,256]{1,0:T(8,128)(2,1)S(1)}, bf16[768,256]{1,0:T(8,128)(2,1)S(1)}, u32[]{:S(2)}, u32[]{:S(2)}) collective-permute-start(bf16[768,256]{1,0:T(8,128)(2,1)S(1)} %get-tuple-element.38), channel_id=1, source_target_pairs={{0,4},{1,5},{2,6},{3,7},{4,0},{5,1},{6,2},{7,3},{8,12},{9,13},{10,... | collective-permute-start | bytes 1179656 | tf_op jit(solution)/shard_map/ppermute | solution.py:34
  8.1 8.7 %collective-permute-start.2 = (bf16[256,256]{1,0:T(8,128)(2,1)S(1)}, bf16[256,256]{1,0:T(8,128)(2,1)S(1)}, u32[]{:S(2)}, u32[]{:S(2)}) collective-permute-start(bf16[256,256]{1,0:T(8,128)(2,1)S(1)} %get-tuple-element.69), channel_id=1, source_target_pairs={{0,8},{1,9},{2,10},{3,11},{4,12},{5,13},{6,14},{7,15},{8,0},{9,1},... | collective-permute-start | bytes 393224 | tf_op jit(solution)/shard_map/ppermute | solution.py:34
  11.0 7.9 %collective-permute-start.4 = (bf16[256,256]{1,0:T(8,128)(2,1)S(1)}, bf16[256,256]{1,0:T(8,128)(2,1)S(1)}, u32[]{:S(2)}, u32[]{:S(2)}) collective-permute-start(bf16[256,256]{1,0:T(8,128)(2,1)S(1)} %get-tuple-element.70), channel_id=1, source_target_pairs={{0,24},{1,25},{2,26},{3,27},{4,28},{5,29},{6,30},{7,31},{8,16},{9,... | collective-permute-start | bytes 393224 | tf_op jit(solution)/shard_map/ppermute | solution.py:34
  12.5 7.8 %collective-permute-start.3 = (bf16[256,256]{1,0:T(8,128)(2,1)S(1)}, bf16[256,256]{1,0:T(8,128)(2,1)S(1)}, u32[]{:S(2)}, u32[]{:S(2)}) collective-permute-start(bf16[256,256]{1,0:T(8,128)(2,1)S(1)} %get-tuple-element.71), channel_id=1, source_target_pairs={{0,16},{1,17},{2,18},{3,19},{4,20},{5,21},{6,22},{7,23},{8,24},{9,... | collective-permute-start | bytes 393224 | tf_op jit(solution)/shard_map/ppermute | solution.py:34
  16.7 3.6 %collective-permute-start.1 = (bf16[256,256]{1,0:T(8,128)(2,1)S(1)}, bf16[256,256]{1,0:T(8,128)(2,1)S(1)}, u32[]{:S(2)}, u32[]{:S(2)}) collective-permute-start(bf16[256,256]{1,0:T(8,128)(2,1)S(1)} %get-tuple-element.42), channel_id=1, source_target_pairs={{0,4},{1,5},{2,6},{3,7},{4,0},{5,1},{6,2},{7,3},{8,12},{9,13},{10,... | collective-permute-start | bytes 393224 | tf_op jit(solution)/shard_map/ppermute | solution.py:34
  20.4 5.0 %collective-permute-start.5 = (bf16[256,256]{1,0:T(8,128)(2,1)S(1)}, bf16[256,256]{1,0:T(8,128)(2,1)S(1)}, u32[]{:S(2)}, u32[]{:S(2)}) collective-permute-start(bf16[256,256]{1,0:T(8,128)(2,1)S(1)} %add_convert_fusion.3), channel_id=1, source_target_pairs={{0,1},{1,0},{2,3},{3,2},{4,5},{5,4},{6,7},{7,6},{8,9},{9,8},{10,11... | collective-permute-start | bytes 393224 | tf_op jit(solution)/shard_map/ppermute | solution.py:34
  25.5 7.7 %collective-permute-start.6 = (bf16[256,256]{1,0:T(8,128)(2,1)S(1)}, bf16[256,256]{1,0:T(8,128)(2,1)S(1)}, u32[]{:S(2)}, u32[]{:S(2)}) collective-permute-start(bf16[256,256]{1,0:T(8,128)(2,1)S(1)} %add_convert_fusion.2), channel_id=1, source_target_pairs={{0,2},{1,3},{2,0},{3,1},{4,6},{5,7},{6,4},{7,5},{8,10},{9,11},{10,... | collective-permute-start | bytes 393224 | tf_op jit(solution)/shard_map/ppermute | solution.py:34
  33.2 7.9 %collective-permute-start.10 = (bf16[256,256]{1,0:T(8,128)(2,1)S(1)}, bf16[256,256]{1,0:T(8,128)(2,1)S(1)}, u32[]{:S(2)}, u32[]{:S(2)}) collective-permute-start(bf16[256,256]{1,0:T(8,128)(2,1)S(1)} %add_convert_fusion.1.refs_0_), channel_id=1, source_target_pairs={{0,4},{1,5},{2,6},{3,7},{4,0},{5,1},{6,2},{7,3},{8,12},{9,13},{10,... | collective-permute-start | bytes 393224 | tf_op jit(solution)/shard_map/ppermute | solution.py:34
  33.3 8.3 %collective-permute-start.9 = (bf16[256,256]{1,0:T(8,128)(2,1)S(1)}, bf16[256,256]{1,0:T(8,128)(2,1)S(1)}, u32[]{:S(2)}, u32[]{:S(2)}) collective-permute-start(bf16[256,256]{1,0:T(8,128)(2,1)S(1)} %add_convert_fusion.1.refs_0_), channel_id=1, source_target_pairs={{0,24},{1,25},{2,26},{3,27},{4,28},{5,29},{6,30},{7,31},{8,16},{9,... | collective-permute-start | bytes 393224 | tf_op jit(solution)/shard_map/ppermute | solution.py:34
  34.8 8.1 %collective-permute-start.8 = (bf16[256,256]{1,0:T(8,128)(2,1)S(1)}, bf16[256,256]{1,0:T(8,128)(2,1)S(1)}, u32[]{:S(2)}, u32[]{:S(2)}) collective-permute-start(bf16[256,256]{1,0:T(8,128)(2,1)S(1)} %add_convert_fusion.1.refs_0_), channel_id=1, source_target_pairs={{0,16},{1,17},{2,18},{3,19},{4,20},{5,21},{6,22},{7,23},{8,24},{9,... | collective-permute-start | bytes 393224 | tf_op jit(solution)/shard_map/ppermute | solution.py:34
  36.3 5.6 %collective-permute-start.7 = (bf16[256,256]{1,0:T(8,128)(2,1)S(1)}, bf16[256,256]{1,0:T(8,128)(2,1)S(1)}, u32[]{:S(2)}, u32[]{:S(2)}) collective-permute-start(bf16[256,256]{1,0:T(8,128)(2,1)S(1)} %add_convert_fusion.1.refs_0_), channel_id=1, source_target_pairs={{0,8},{1,9},{2,10},{3,11},{4,12},{5,13},{6,14},{7,15},{8,0},{9,1},... | collective-permute-start | bytes 393224 | tf_op jit(solution)/shard_map/ppermute | solution.py:34
  36.9 4.2 %copy-start.3 = (bf16[2,4,512,256]{3,2,1,0:T(8,128)(2,1)S(1)}, bf16[2,4,512,256]{3,2,1,0:T(8,128)(2,1)}, u32[]{:S(2)}) copy-start(bf16[2,4,512,256]{3,2,1,0:T(8,128)(2,1)} %get-tuple-element.53.refs_2_) | copy-start | bytes 6291460
  36.9 6.6 %copy-start = (bf16[2,4,768,256]{3,2,1,0:T(8,128)(2,1)S(1)}, bf16[2,4,768,256]{3,2,1,0:T(8,128)(2,1)}, u32[]{:S(2)}) copy-start(bf16[2,4,768,256]{3,2,1,0:T(8,128)(2,1)} %keep.4.refs_4_.refs_3_) | copy-start | bytes 9437188
  36.9 6.6 %copy-start.2 = (bf16[2,4,256,256]{3,2,1,0:T(8,128)(2,1)S(1)}, bf16[2,4,256,256]{3,2,1,0:T(8,128)(2,1)}, u32[]{:S(2)}) copy-start(bf16[2,4,256,256]{3,2,1,0:T(8,128)(2,1)} %keep.3.refs_3_) | copy-start | bytes 3145732
  41.0 3.5 %copy-start.1 = (bf16[2,4,512,256]{3,2,1,0:T(8,128)(2,1)S(1)}, bf16[2,4,512,256]{3,2,1,0:T(8,128)(2,1)}, u32[]{:S(2)}) copy-start(bf16[2,4,512,256]{3,2,1,0:T(8,128)(2,1)} %keep.5.refs_4_) | copy-start | bytes 6291460
  41.6 2.9 %collective-permute-start.13 = (bf16[256,256]{1,0:T(8,128)(2,1)S(1)}, bf16[256,256]{1,0:T(8,128)(2,1)S(1)}, u32[]{:S(2)}, u32[]{:S(2)}) collective-permute-start(bf16[256,256]{1,0:T(8,128)(2,1)S(1)} %collective-permute-done.9.refs_2_), channel_id=1, source_target_pairs={{0,4},{1,5},{2,6},{3,7},{4,0},{5,1},{6,2},{7,3},{8,12},{9,13},{10,... | collective-permute-start | bytes 393224 | tf_op jit(solution)/shard_map/ppermute | solution.py:34
  42.9 1.4 %collective-permute-start.12 = (bf16[256,256]{1,0:T(8,128)(2,1)S(1)}, bf16[256,256]{1,0:T(8,128)(2,1)S(1)}, u32[]{:S(2)}, u32[]{:S(2)}) collective-permute-start(bf16[256,256]{1,0:T(8,128)(2,1)S(1)} %collective-permute-done.8.refs_1_), channel_id=1, source_target_pairs={{0,4},{1,5},{2,6},{3,7},{4,0},{5,1},{6,2},{7,3},{8,12},{9,13},{10,... | collective-permute-start | bytes 393224 | tf_op jit(solution)/shard_map/ppermute | solution.py:34
  43.0 1.5 %collective-permute-start.11 = (bf16[256,256]{1,0:T(8,128)(2,1)S(1)}, bf16[256,256]{1,0:T(8,128)(2,1)S(1)}, u32[]{:S(2)}, u32[]{:S(2)}) collective-permute-start(bf16[256,256]{1,0:T(8,128)(2,1)S(1)} %collective-permute-done.7.refs_0_), channel_id=1, source_target_pairs={{0,4},{1,5},{2,6},{3,7},{4,0},{5,1},{6,2},{7,3},{8,12},{9,13},{10,... | collective-permute-start | bytes 393224 | tf_op jit(solution)/shard_map/ppermute | solution.py:34
  45.3 1.9 %collective-permute-start.14 = (f32[2,32,256]{2,1,0:T(8,128)S(1)}, f32[2,32,256]{2,1,0:T(8,128)S(1)}, u32[]{:S(2)}, u32[]{:S(2)}) collective-permute-start(f32[2,32,256]{2,1,0:T(8,128)S(1)} %get-tuple-element.63), channel_id=1, source_target_pairs={{0,4},{1,5},{2,6},{3,7},{4,0},{5,1},{6,2},{7,3},{8,12},{9,13},{10,... | collective-permute-start | bytes 196616 | tf_op jit(solution)/shard_map/ppermute | solution.py:34
  47.2 6.0 %collective-permute-start.17 = (f32[2,32,256]{2,1,0:T(8,128)S(1)}, f32[2,32,256]{2,1,0:T(8,128)S(1)}, u32[]{:S(2)}, u32[]{:S(2)}) collective-permute-start(f32[2,32,256]{2,1,0:T(8,128)S(1)} %add.72), channel_id=1, source_target_pairs={{0,24},{1,25},{2,26},{3,27},{4,28},{5,29},{6,30},{7,31},{8,16},{9,... | collective-permute-start | bytes 196616 | tf_op jit(solution)/shard_map/ppermute | solution.py:34
  48.8 4.9 %collective-permute-start.16 = (f32[2,32,256]{2,1,0:T(8,128)S(1)}, f32[2,32,256]{2,1,0:T(8,128)S(1)}, u32[]{:S(2)}, u32[]{:S(2)}) collective-permute-start(f32[2,32,256]{2,1,0:T(8,128)S(1)} %add.72), channel_id=1, source_target_pairs={{0,16},{1,17},{2,18},{3,19},{4,20},{5,21},{6,22},{7,23},{8,24},{9,... | collective-permute-start | bytes 196616 | tf_op jit(solution)/shard_map/ppermute | solution.py:34
  49.5 4.3 %collective-permute-start.15 = (f32[2,32,256]{2,1,0:T(8,128)S(1)}, f32[2,32,256]{2,1,0:T(8,128)S(1)}, u32[]{:S(2)}, u32[]{:S(2)}) collective-permute-start(f32[2,32,256]{2,1,0:T(8,128)S(1)} %add.72), channel_id=1, source_target_pairs={{0,8},{1,9},{2,10},{3,11},{4,12},{5,13},{6,14},{7,15},{8,0},{9,1},... | collective-permute-start | bytes 196616 | tf_op jit(solution)/shard_map/ppermute | solution.py:34

commit v5 on v4

--- a/solution.py
+++ b/solution.py
@@ -73,7 +73,7 @@
 
 
 def start_all(copies):
-    for k, copy in enumerate(copies):
+    for copy in copies:
         copy.start(priority=1)
 
 
@@ -86,9 +86,9 @@
 
 
 def mix_kernel(place_ref, q_hbm, g_hbm, e_hbm, *refs):
-    mixed_hbm = refs[2] if len(refs) == 10 else None
     first_ref, second_ref = refs[:2]
-    q_ref, g_ref, e_ref, wide_ref, q_sem, sems, out_sems = refs[-7:]
+    mixed_ref = refs[2] if len(refs) == 9 else None
+    q_ref, g_ref, e_ref, wide_ref, q_sem, sems = refs[-6:]
     m_count, pack, total_rows, width = g_ref.shape
     rank = q_ref.shape[1]
     count = place_ref.shape[0]
@@ -104,7 +104,6 @@
         turned = jnp.concatenate([q_ref[m]] * pack, axis=0).T
         for j in range(pack):
             wide_ref[m, pl.ds(j * width, width), :] = jnp.where(lane_group == j, turned, 0.0).astype(BF16)
-    outgoing = []
     for c, (where, copies) in enumerate(chunks):
         wait_all(copies)
         if c + FETCHES < count:
@@ -115,14 +114,9 @@
             mixed = [g_ref[m, j, where, :] + e_ref[m, j, where, :] for j in range(pack)]
             total = jnp.dot(jnp.concatenate(mixed, axis=1), wide_ref[m], preferred_element_type=F32)
             left_ref[at, m * LANES:(m + 1) * LANES] = total.astype(left_ref.dtype)
-            if mixed_hbm is not None:
+            if mixed_ref is not None:
                 for j in range(pack):
-                    g_ref[m, j, where, :] = mixed[j]
-        if mixed_hbm is not None:
-            copy = pltpu.make_async_copy(g_ref.at[:, :, where, :], mixed_hbm.at[:, :, where, :], out_sems.at[c])
-            copy.start()
-            outgoing.append(copy)
-    wait_all(outgoing)
+                    mixed_ref[m, j, where, :] = mixed[j]
 
 
 def mix(gradient, error_acc, q_turned, first, second, rows, kept=False):
@@ -134,8 +128,8 @@
     return pl.pallas_call(
         mix_kernel,
         in_specs=[scalar()] + [hbm] * 3,
-        out_specs=[whole()] * 2 + [hbm] * kept,
-        out_shape=[pltpu.VMEM((len(first) * rows, m_count * LANES), dtype) for dtype in (BF16, F32)] + [pltpu.HBM(shape, BF16)] * kept,
+        out_specs=[whole()] * (2 + kept),
+        out_shape=[pltpu.VMEM((len(first) * rows, m_count * LANES), dtype) for dtype in (BF16, F32)] + [pltpu.VMEM(shape, BF16)] * kept,
         scratch_shapes=[
             pltpu.VMEM(q_turned.shape, F32),
             pltpu.VMEM(shape, BF16),
@@ -143,7 +137,6 @@
             pltpu.VMEM((m_count, pack * width, LANES), BF16),
             pltpu.SemaphoreType.DMA,
             pltpu.SemaphoreType.DMA((2, count)),
-            pltpu.SemaphoreType.DMA((count,)),
         ],
         compiler_params=params(20),
         cost_estimate=cost(),
@@ -151,20 +144,15 @@
     )(places, q_turned, gradient, error_acc)
 
 
-def keep_kernel(place_ref, g_hbm, e_hbm, mixed_hbm, g_ref, e_ref, sems, out_sems):
+def keep_kernel(place_ref, g_hbm, e_hbm, mixed_ref, g_ref, e_ref, sems):
     count = place_ref.shape[0]
     rows = g_ref.shape[2] // count
-    outgoing = []
     chunks = load([place_ref[c] * rows for c in range(count)], rows, g_hbm, e_hbm, g_ref, e_ref, sems)
     for _, copies in chunks:
         start_all(copies)
-    for c, (where, copies) in enumerate(chunks):
+    for where, copies in chunks:
         wait_all(copies)
-        g_ref[:, :, where, :] = g_ref[:, :, where, :] + e_ref[:, :, where, :]
-        copy = pltpu.make_async_copy(g_ref.at[:, :, where, :], mixed_hbm.at[:, :, where, :], out_sems.at[c])
-        copy.start()
-        outgoing.append(copy)
-    wait_all(outgoing)
+        mixed_ref[:, :, where, :] = g_ref[:, :, where, :] + e_ref[:, :, where, :]
 
 
 def keep(gradient, error_acc, places, rows):
@@ -174,14 +162,9 @@
     return pl.pallas_call(
         keep_kernel,
         in_specs=[scalar()] + [pl.BlockSpec(memory_space=pltpu.HBM)] * 2,
-        out_specs=pl.BlockSpec(memory_space=pltpu.HBM),
-        out_shape=pltpu.HBM(shape, BF16),
-        scratch_shapes=[
-            pltpu.VMEM(shape, BF16),
-            pltpu.VMEM(shape, BF16),
-            pltpu.SemaphoreType.DMA((2, count)),
-            pltpu.SemaphoreType.DMA((count,)),
-        ],
+        out_specs=whole(),
+        out_shape=pltpu.VMEM(shape, BF16),
+        scratch_shapes=[pltpu.VMEM(shape, BF16), pltpu.VMEM(shape, BF16), pltpu.SemaphoreType.DMA((2, count))],
         compiler_params=params(16),
         cost_estimate=cost(),
         name="keep",
@@ -335,7 +318,7 @@
     rank = right.shape[1]
     for b in range(bits(hst)):
         right = right + exchange(right, lambda o, h, t, b=b: (o, h ^ (1 << b), t))
-    early = rank * 3 // 8
+    early = rank // 4
     right, inverse = after(right, invert(range(early), *grams))
     parts = [right] + [exchange(right, lambda o, h, t, k=k: (o ^ k, h, t)) for k in range(1, outer)]
     inverse = invert(range(early, rank), inverse)
@@ -381,7 +364,7 @@
         sent = pick(left, 1 - bit).astype(BF16)
         left = pick(left, bit) + exchange(sent, lambda o, h, t, b=b: (o, h ^ (1 << b), t)).astype(F32)
     others = near[1:] + far[1:]
-    early, late = len(others) // 6, len(others) * 2 // 3
+    early, late = len(others) // 3, len(others) // 2
     waiting, mixed = [others[:early], others[early:late]], []
     for b in range(bits(tp)):
         sent = left.astype(BF16)
@@ -389,7 +372,7 @@
         if places:
             sent, places = after_all(sent, places)
             kept = keep(gradient, error_acc, places, chunk)
-        got = exchange(sent, lambda o, h, t, b=b: (o, h, t ^ (1 << b)))
+        got = exchange(sent, lambda o, h, t, b=b: (o, h, t ^ (1 << (b if h % 2 == 0 else bits(tp) - 1 - b))))
         if places:
             got, kept = after(got, kept)
             mixed.append(kept)

time: 58.7 us -> 56.8 us (0.968)
  Pallas kernels: 32.5 us -> 28.1 us
  waiting for transfers between devices: 7.54 us -> 9.53 us
    pallas_call x3, Pallas kernels: 11.7 us -> 8.11 us  [keep(): pl.pallas_call(keep_kernel, in_specs=[scalar()] + [pl.BlockSpec(memory_sp...]
    ppermute x18, waiting for transfers between devices: 7.54 us -> 9.53 us  [exchange(): return lax.ppermute(x, AXES, pairs)]
    pallas_call x2, Pallas kernels: 10 us -> 9.15 us  [mix(): pl.pallas_call(mix_kernel, in_specs=[scalar()] + [hbm] * 3, out_specs=[wh...]
  transfers between devices with their start and end apart: 18 -> 18, of which waited for: 8 -> 8; matrix products, arithmetic and copies ran while one was open for 1% -> 1% of each run, Pallas kernels for 36% -> 29%
where the time goes in v5:
time: 56.8 us; the launch traced here: 56.4 us
  Pallas kernels  28.1 us (49%)
  starting transfers between devices  17.8 us (31%)
  waiting for transfers between devices  9.53 us (17%)
    ppermute x18, starting transfers between devices, exchange(): return lax.ppermute(x, AXES, pairs)  17.8 us
    ppermute x18, waiting for transfers between devices, exchange(): return lax.ppermute(x, AXES, pairs)  9.53 us
    pallas_call x2, Pallas kernels, mix(): pl.pallas_call(mix_kernel, in_specs=[scalar()] + [hbm] * 3, out_specs=[wh...  9.15 us
    pallas_call x3, Pallas kernels, keep(): pl.pallas_call(keep_kernel, in_specs=[scalar()] + [pl.BlockSpec(memory_sp...  8.11 us
    pallas_call x1, Pallas kernels, expand(): pl.pallas_call(lambda *refs: expand_kernel(scale, *refs), in_specs=[scala...  4.77 us
    pallas_call x2, Pallas kernels, invert(): pl.pallas_call(lambda *refs: invert_kernel(steps, *refs), in_specs=[whole...  3.96 us
    pallas_call x3, Pallas kernels, project(): pl.pallas_call(lambda *refs: project_kernel(chunks, *refs), in_specs=[who...  2.08 us
  transfers between devices with their start and end apart: 18, of which 8 were waited for; matrix products, arithmetic and copies ran while one was open for 1% of the time, Pallas kernels for 29%

profile of v5, /device:TPU:0, one launch (start us, length us, event | category | flops | bytes accessed | tf_op | source)
XLA Modules:
  0.0 56.4 jit_solution(14678617470817923028)
XLA Ops:
  0.1 5.9 %mix.2 = (bf16[768,256]{1,0:T(8,128)(2,1)S(1)}, f32[768,256]{1,0:T(8,128)S(1)}) custom-call(s32[6]{0:T(128)S(1)} %stack.105.place_ref, f32[2,32,256]{2,1,0:T(8,128)} %bitcast.46, bf16[2,4,2048,256]{3,2,1,0:T(8,128)(2,1)} %bitcast.36, bf16[2,4,2048,256]{3,2,1,0:T(8,128)(2,1)} %bitcast.41), custom_call_target="tpu_custom_call" | custom-call | flops 1000000 | tf_op jit(solution)/shard_map/mix/pallas_call | solution.py:128
  6.0 0.5 collective-permute-start
  6.5 1.3 %collective-permute-done = bf16[768,256]{1,0:T(8,128)(2,1)S(1)} collective-permute-done((bf16[768,256]{1,0:T(8,128)(2,1)S(1)}, bf16[768,256]{1,0:T(8,128)(2,1)S(1)}, u32[]{:S(2)}, u32[]{:S(2)}) %collective-permute-start) | collective-permute-done | bytes 393248 | tf_op jit(solution)/shard_map/ppermute | solution.py:34
  8.0 2.9 %collective-permute-start.2 = (bf16[256,256]{1,0:T(8,128)(2,1)S(1)}, bf16[256,256]{1,0:T(8,128)(2,1)S(1)}, u32[]{:S(2)}, u32[]{:S(2)}) collective-permute-start(bf16[256,256]{1,0:T(8,128)(2,1)S(1)} %get-tuple-element.69), channel_id=1, source_target_pairs={{0,8},{1,9},{2,10},{3,11},{4,12},{5,13},{6,14},{7,15},{8,0},{9,1},... | collective-permute-start | bytes 393224 | tf_op jit(solution)/shard_map/ppermute | solution.py:34
  11.0 1.5 %collective-permute-start.4 = (bf16[256,256]{1,0:T(8,128)(2,1)S(1)}, bf16[256,256]{1,0:T(8,128)(2,1)S(1)}, u32[]{:S(2)}, u32[]{:S(2)}) collective-permute-start(bf16[256,256]{1,0:T(8,128)(2,1)S(1)} %get-tuple-element.70), channel_id=1, source_target_pairs={{0,24},{1,25},{2,26},{3,27},{4,28},{5,29},{6,30},{7,31},{8,16},{9,... | collective-permute-start | bytes 393224 | tf_op jit(solution)/shard_map/ppermute | solution.py:34
  12.6 3.2 %mix.3 = (bf16[256,256]{1,0:T(8,128)(2,1)S(1)}, f32[256,256]{1,0:T(8,128)S(1)}, bf16[2,4,512,256]{3,2,1,0:T(8,128)(2,1)S(1)}) custom-call(s32[2]{0:T(128)S(1)} %pad_add_fusion.place_ref, f32[2,32,256]{2,1,0:T(8,128)} %bitcast.47, bf16[2,4,2048,256]{3,2,1,0:T(8,128)(2,1)} %bitcast.37, bf16[2,4,2048,256]{3,2,1,0:T(8,128)(2,1)} %bitcast.42), custom_call_target="tpu_custom_call" | custom-call | flops 1000000 | tf_op jit(solution)/shard_map/mix/pallas_call | solution.py:128
  15.9 3.0 %collective-permute-done.4 = bf16[256,256]{1,0:T(8,128)(2,1)S(1)} collective-permute-done((bf16[256,256]{1,0:T(8,128)(2,1)S(1)}, bf16[256,256]{1,0:T(8,128)(2,1)S(1)}, u32[]{:S(2)}, u32[]{:S(2)}) %collective-permute-start.4) | collective-permute-done | bytes 131104 | tf_op jit(solution)/shard_map/ppermute | solution.py:34
  18.9 1.4 %collective-permute-done.3 = bf16[256,256]{1,0:T(8,128)(2,1)S(1)} collective-permute-done((bf16[256,256]{1,0:T(8,128)(2,1)S(1)}, bf16[256,256]{1,0:T(8,128)(2,1)S(1)}, u32[]{:S(2)}, u32[]{:S(2)}) %collective-permute-start.3) | collective-permute-done | bytes 131104 | tf_op jit(solution)/shard_map/ppermute | solution.py:34
  20.3 1.6 %collective-permute-start.5 = (bf16[256,256]{1,0:T(8,128)(2,1)S(1)}, bf16[256,256]{1,0:T(8,128)(2,1)S(1)}, u32[]{:S(2)}, u32[]{:S(2)}) collective-permute-start(bf16[256,256]{1,0:T(8,128)(2,1)S(1)} %add_convert_fusion.3), channel_id=1, source_target_pairs={{0,1},{1,0},{2,3},{3,2},{4,6},{5,7},{6,4},{7,5},{8,9},{9,8},{10,11... | collective-permute-start | bytes 393224 | tf_op jit(solution)/shard_map/ppermute | solution.py:34
  22.0 2.9 %keep.3.refs_3_ = bf16[2,4,512,256]{3,2,1,0:T(8,128)(2,1)S(1)} custom-call(s32[2]{0:T(128)S(1)} %pad_add_fusion.1.place_ref, bf16[2,4,2048,256]{3,2,1,0:T(8,128)(2,1)} %bitcast.38, bf16[2,4,2048,256]{3,2,1,0:T(8,128)(2,1)} %bitcast.43), custom_call_target="tpu_custom_call" | custom-call | flops 1000000 | tf_op jit(solution)/shard_map/keep/pallas_call | solution.py:162
  24.9 0.6 %collective-permute-done.5 = bf16[256,256]{1,0:T(8,128)(2,1)S(1)} collective-permute-done((bf16[256,256]{1,0:T(8,128)(2,1)S(1)}, bf16[256,256]{1,0:T(8,128)(2,1)S(1)}, u32[]{:S(2)}, u32[]{:S(2)}) %collective-permute-start.5) | collective-permute-done | bytes 131104 | tf_op jit(solution)/shard_map/ppermute | solution.py:34
  25.5 2.9 %collective-permute-start.6 = (bf16[256,256]{1,0:T(8,128)(2,1)S(1)}, bf16[256,256]{1,0:T(8,128)(2,1)S(1)}, u32[]{:S(2)}, u32[]{:S(2)}) collective-permute-start(bf16[256,256]{1,0:T(8,128)(2,1)S(1)} %add_convert_fusion.2), channel_id=1, source_target_pairs={{0,2},{1,3},{2,0},{3,1},{4,5},{5,4},{6,7},{7,6},{8,10},{9,11},{10,... | collective-permute-start | bytes 393224 | tf_op jit(solution)/shard_map/ppermute | solution.py:34
  28.5 1.7 %keep.4.refs_4_ = bf16[2,4,256,256]{3,2,1,0:T(8,128)(2,1)S(1)} custom-call(s32[1]{0:T(128)} %bitcast.15.place_ref, bf16[2,4,2048,256]{3,2,1,0:T(8,128)(2,1)} %bitcast.39, bf16[2,4,2048,256]{3,2,1,0:T(8,128)(2,1)} %bitcast.44), custom_call_target="tpu_custom_call" | custom-call | flops 1000000 | tf_op jit(solution)/shard_map/keep/pallas_call | solution.py:162
  30.2 1.3 %collective-permute-done.6 = bf16[256,256]{1,0:T(8,128)(2,1)S(1)} collective-permute-done((bf16[256,256]{1,0:T(8,128)(2,1)S(1)}, bf16[256,256]{1,0:T(8,128)(2,1)S(1)}, u32[]{:S(2)}, u32[]{:S(2)}) %collective-permute-start.6) | collective-permute-done | bytes 131104 | tf_op jit(solution)/shard_map/ppermute | solution.py:34
  31.6 1.5 %collective-permute-start.9 = (bf16[256,256]{1,0:T(8,128)(2,1)S(1)}, bf16[256,256]{1,0:T(8,128)(2,1)S(1)}, u32[]{:S(2)}, u32[]{:S(2)}) collective-permute-start(bf16[256,256]{1,0:T(8,128)(2,1)S(1)} %add_convert_fusion.1.refs_0_), channel_id=1, source_target_pairs={{0,24},{1,25},{2,26},{3,27},{4,28},{5,29},{6,30},{7,31},{8,16},{9,... | collective-permute-start | bytes 393224 | tf_op jit(solution)/shard_map/ppermute | solution.py:34
  33.1 1.5 %collective-permute-start.8 = (bf16[256,256]{1,0:T(8,128)(2,1)S(1)}, bf16[256,256]{1,0:T(8,128)(2,1)S(1)}, u32[]{:S(2)}, u32[]{:S(2)}) collective-permute-start(bf16[256,256]{1,0:T(8,128)(2,1)S(1)} %add_convert_fusion.1.refs_0_), channel_id=1, source_target_pairs={{0,16},{1,17},{2,18},{3,19},{4,20},{5,21},{6,22},{7,23},{8,24},{9,... | collective-permute-start | bytes 393224 | tf_op jit(solution)/shard_map/ppermute | solution.py:34
  34.6 0.5 collective-permute-start.7
  35.2 3.6 %keep.5.refs_3_ = bf16[2,4,768,256]{3,2,1,0:T(8,128)(2,1)S(1)} custom-call(s32[3]{0:T(128)S(1)} %pad_add_fusion.2.place_ref, bf16[2,4,2048,256]{3,2,1,0:T(8,128)(2,1)} %bitcast.40, bf16[2,4,2048,256]{3,2,1,0:T(8,128)(2,1)} %bitcast.45), custom_call_target="tpu_custom_call" | custom-call | flops 1000000 | tf_op jit(solution)/shard_map/keep/pallas_call | solution.py:162
  38.8 0.5 project.3
  39.5 0.7 %collective-permute-done.7.refs_0_ = bf16[256,256]{1,0:T(8,128)(2,1)S(1)} collective-permute-done((bf16[256,256]{1,0:T(8,128)(2,1)S(1)}, bf16[256,256]{1,0:T(8,128)(2,1)S(1)}, u32[]{:S(2)}, u32[]{:S(2)}) %collective-permute-start.7) | collective-permute-done | bytes 131104 | tf_op jit(solution)/shard_map/ppermute | solution.py:34
  40.2 1.0 %collective-permute-done.8.refs_1_ = bf16[256,256]{1,0:T(8,128)(2,1)S(1)} collective-permute-done((bf16[256,256]{1,0:T(8,128)(2,1)S(1)}, bf16[256,256]{1,0:T(8,128)(2,1)S(1)}, u32[]{:S(2)}, u32[]{:S(2)}) %collective-permute-start.8) | collective-permute-done | bytes 131104 | tf_op jit(solution)/shard_map/ppermute | solution.py:34
  41.3 0.5 collective-permute-start.11
  41.8 0.8 %project.4 = (f32[2,32,256]{2,1,0:T(8,128)S(1)}, f32[3,2,32,32]{3,2,1,0:T(8,128)S(1)}) custom-call(bf16[256,256]{1,0:T(8,128)(2,1)S(1)} %collective-permute-done.7.refs_0_, bf16[256,256]{1,0:T(8,128)(2,1)S(1)} %collective-permute-done.8.refs_1_, bf16[256,256]{1,0:T(8,128)(2,1)S(1)} %collective-permute-done.9.refs_2_, ...), custom_call_target="tpu_custom_call" | custom-call | flops 1000000 | tf_op jit(solution)/shard_map/project/pallas_call | solution.py:204
  42.6 0.2 collective-permute-done.11.refs_0_
  42.8 0.8 %project.5 = (f32[2,32,256]{2,1,0:T(8,128)S(1)}, f32[3,2,32,32]{3,2,1,0:T(8,128)S(1)}) custom-call(bf16[256,256]{1,0:T(8,128)(2,1)S(1)} %collective-permute-done.11.refs_0_, bf16[256,256]{1,0:T(8,128)(2,1)S(1)} %collective-permute-done.12.refs_1_, bf16[256,256]{1,0:T(8,128)(2,1)S(1)} %collective-permute-done.13.refs_2_, ...), custom_call_target="tpu_custom_call" | custom-call | flops 1000000 | tf_op jit(solution)/shard_map/project/pallas_call | solution.py:204
  43.6 0.4 collective-permute-start.14
  44.0 1.0 %invert.2.refs_0_ = f32[2,32,32]{2,1,0:T(8,128)S(1)} custom-call(f32[2,2,32,32]{3,2,1,0:T(8,128)S(1)} %get-tuple-element.64.refs_0_, f32[3,2,32,32]{3,2,1,0:T(8,128)S(1)} %get-tuple-element.65.refs_1_, f32[3,2,32,32]{3,2,1,0:T(8,128)S(1)} %get-tuple-element.66.refs_2_), custom_call_target="tpu_custom_call" | custom-call | flops 1000000 | tf_op jit(solution)/shard_map/invert/pallas_call | solution.py:245
  45.0 1.6 %collective-permute-start.17 = (f32[2,32,256]{2,1,0:T(8,128)S(1)}, f32[2,32,256]{2,1,0:T(8,128)S(1)}, u32[]{:S(2)}, u32[]{:S(2)}) collective-permute-start(f32[2,32,256]{2,1,0:T(8,128)S(1)} %add.72), channel_id=1, source_target_pairs={{0,24},{1,25},{2,26},{3,27},{4,28},{5,29},{6,30},{7,31},{8,16},{9,... | collective-permute-start | bytes 196616 | tf_op jit(solution)/shard_map/ppermute | solution.py:34
  46.6 0.6 %collective-permute-start.16 = (f32[2,32,256]{2,1,0:T(8,128)S(1)}, f32[2,32,256]{2,1,0:T(8,128)S(1)}, u32[]{:S(2)}, u32[]{:S(2)}) collective-permute-start(f32[2,32,256]{2,1,0:T(8,128)S(1)} %add.72), channel_id=1, source_target_pairs={{0,16},{1,17},{2,18},{3,19},{4,20},{5,21},{6,22},{7,23},{8,24},{9,... | collective-permute-start | bytes 196616 | tf_op jit(solution)/shard_map/ppermute | solution.py:34
  47.3 1.3 %collective-permute-start.15 = (f32[2,32,256]{2,1,0:T(8,128)S(1)}, f32[2,32,256]{2,1,0:T(8,128)S(1)}, u32[]{:S(2)}, u32[]{:S(2)}) collective-permute-start(f32[2,32,256]{2,1,0:T(8,128)S(1)} %add.72), channel_id=1, source_target_pairs={{0,8},{1,9},{2,10},{3,11},{4,12},{5,13},{6,14},{7,15},{8,0},{9,1},... | collective-permute-start | bytes 196616 | tf_op jit(solution)/shard_map/ppermute | solution.py:34
  48.6 3.0 %invert.3.refs_2_ = f32[2,32,32]{2,1,0:T(8,128)S(1)} custom-call(f32[2,32,32]{2,1,0:T(8,128)S(1)} %invert.2.refs_0_), custom_call_target="tpu_custom_call" | custom-call | flops 1000000 | tf_op jit(solution)/shard_map/invert/pallas_call | solution.py:245
  51.6 4.8 %expand.1 = bf16[2,4,2048,256]{3,2,1,0:T(8,128)(2,1)} custom-call(s32[8]{0:T(128)S(1)} %stack.104.refs_0_, bf16[8,256,256]{2,1,0:T(8,128)(2,1)S(1)} %bitcast_dynamic-update-slice_fusion.refs_1_, f32[2,32,32]{2,1,0:T(8,128)S(1)} %invert.3.refs_2_, f32[2,32,256]{2,1,0:T(8,128)S(1)} %add_add_fusion.refs_3_), custom_call_target="tpu_custom_call" | custom-call | tf_op jit(solution)/shard_map/expand/pallas_call | solution.py:300
  (39 shorter events, 1.3 us)
Async XLA Ops:
  6.0 1.9 %collective-permute-start = (bf16[768,256]{1,0:T(8,128)(2,1)S(1)}, bf16[768,256]{1,0:T(8,128)(2,1)S(1)}, u32[]{:S(2)}, u32[]{:S(2)}) collective-permute-start(bf16[768,256]{1,0:T(8,128)(2,1)S(1)} %get-tuple-element.38), channel_id=1, source_target_pairs={{0,4},{1,5},{2,6},{3,7},{4,0},{5,1},{6,2},{7,3},{8,12},{9,13},{10,... | collective-permute-start | bytes 1179656 | tf_op jit(solution)/shard_map/ppermute | solution.py:34
  8.0 7.9 %collective-permute-start.2 = (bf16[256,256]{1,0:T(8,128)(2,1)S(1)}, bf16[256,256]{1,0:T(8,128)(2,1)S(1)}, u32[]{:S(2)}, u32[]{:S(2)}) collective-permute-start(bf16[256,256]{1,0:T(8,128)(2,1)S(1)} %get-tuple-element.69), channel_id=1, source_target_pairs={{0,8},{1,9},{2,10},{3,11},{4,12},{5,13},{6,14},{7,15},{8,0},{9,1},... | collective-permute-start | bytes 393224 | tf_op jit(solution)/shard_map/ppermute | solution.py:34
  11.0 7.9 %collective-permute-start.4 = (bf16[256,256]{1,0:T(8,128)(2,1)S(1)}, bf16[256,256]{1,0:T(8,128)(2,1)S(1)}, u32[]{:S(2)}, u32[]{:S(2)}) collective-permute-start(bf16[256,256]{1,0:T(8,128)(2,1)S(1)} %get-tuple-element.70), channel_id=1, source_target_pairs={{0,24},{1,25},{2,26},{3,27},{4,28},{5,29},{6,30},{7,31},{8,16},{9,... | collective-permute-start | bytes 393224 | tf_op jit(solution)/shard_map/ppermute | solution.py:34
  12.5 7.8 %collective-permute-start.3 = (bf16[256,256]{1,0:T(8,128)(2,1)S(1)}, bf16[256,256]{1,0:T(8,128)(2,1)S(1)}, u32[]{:S(2)}, u32[]{:S(2)}) collective-permute-start(bf16[256,256]{1,0:T(8,128)(2,1)S(1)} %get-tuple-element.71), channel_id=1, source_target_pairs={{0,16},{1,17},{2,18},{3,19},{4,20},{5,21},{6,22},{7,23},{8,24},{9,... | collective-permute-start | bytes 393224 | tf_op jit(solution)/shard_map/ppermute | solution.py:34
  15.8 9.1 %copy-start = (bf16[2,4,512,256]{3,2,1,0:T(8,128)(2,1)}, bf16[2,4,512,256]{3,2,1,0:T(8,128)(2,1)S(1)}, u32[]{:S(2)}) copy-start(bf16[2,4,512,256]{3,2,1,0:T(8,128)(2,1)S(1)} %get-tuple-element.52.refs_2_) | copy-start | bytes 6291460
  15.8 4.4 %collective-permute-start.1 = (bf16[256,256]{1,0:T(8,128)(2,1)S(1)}, bf16[256,256]{1,0:T(8,128)(2,1)S(1)}, u32[]{:S(2)}, u32[]{:S(2)}) collective-permute-start(bf16[256,256]{1,0:T(8,128)(2,1)S(1)} %get-tuple-element.42), channel_id=1, source_target_pairs={{0,4},{1,5},{2,6},{3,7},{4,0},{5,1},{6,2},{7,3},{8,12},{9,13},{10,... | collective-permute-start | bytes 393224 | tf_op jit(solution)/shard_map/ppermute | solution.py:34
  20.3 5.2 %collective-permute-start.5 = (bf16[256,256]{1,0:T(8,128)(2,1)S(1)}, bf16[256,256]{1,0:T(8,128)(2,1)S(1)}, u32[]{:S(2)}, u32[]{:S(2)}) collective-permute-start(bf16[256,256]{1,0:T(8,128)(2,1)S(1)} %add_convert_fusion.3), channel_id=1, source_target_pairs={{0,1},{1,0},{2,3},{3,2},{4,6},{5,7},{6,4},{7,5},{8,9},{9,8},{10,11... | collective-permute-start | bytes 393224 | tf_op jit(solution)/shard_map/ppermute | solution.py:34
  25.5 5.9 %collective-permute-start.6 = (bf16[256,256]{1,0:T(8,128)(2,1)S(1)}, bf16[256,256]{1,0:T(8,128)(2,1)S(1)}, u32[]{:S(2)}, u32[]{:S(2)}) collective-permute-start(bf16[256,256]{1,0:T(8,128)(2,1)S(1)} %add_convert_fusion.2), channel_id=1, source_target_pairs={{0,2},{1,3},{2,0},{3,1},{4,5},{5,4},{6,7},{7,6},{8,10},{9,11},{10,... | collective-permute-start | bytes 393224 | tf_op jit(solution)/shard_map/ppermute | solution.py:34
  31.5 7.3 %collective-permute-start.10 = (bf16[256,256]{1,0:T(8,128)(2,1)S(1)}, bf16[256,256]{1,0:T(8,128)(2,1)S(1)}, u32[]{:S(2)}, u32[]{:S(2)}) collective-permute-start(bf16[256,256]{1,0:T(8,128)(2,1)S(1)} %add_convert_fusion.1.refs_0_), channel_id=1, source_target_pairs={{0,4},{1,5},{2,6},{3,7},{4,0},{5,1},{6,2},{7,3},{8,12},{9,13},{10,... | collective-permute-start | bytes 393224 | tf_op jit(solution)/shard_map/ppermute | solution.py:34
  31.6 7.8 %collective-permute-start.9 = (bf16[256,256]{1,0:T(8,128)(2,1)S(1)}, bf16[256,256]{1,0:T(8,128)(2,1)S(1)}, u32[]{:S(2)}, u32[]{:S(2)}) collective-permute-start(bf16[256,256]{1,0:T(8,128)(2,1)S(1)} %add_convert_fusion.1.refs_0_), channel_id=1, source_target_pairs={{0,24},{1,25},{2,26},{3,27},{4,28},{5,29},{6,30},{7,31},{8,16},{9,... | collective-permute-start | bytes 393224 | tf_op jit(solution)/shard_map/ppermute | solution.py:34
  33.1 8.1 %collective-permute-start.8 = (bf16[256,256]{1,0:T(8,128)(2,1)S(1)}, bf16[256,256]{1,0:T(8,128)(2,1)S(1)}, u32[]{:S(2)}, u32[]{:S(2)}) collective-permute-start(bf16[256,256]{1,0:T(8,128)(2,1)S(1)} %add_convert_fusion.1.refs_0_), channel_id=1, source_target_pairs={{0,16},{1,17},{2,18},{3,19},{4,20},{5,21},{6,22},{7,23},{8,24},{9,... | collective-permute-start | bytes 393224 | tf_op jit(solution)/shard_map/ppermute | solution.py:34
  34.6 5.6 %collective-permute-start.7 = (bf16[256,256]{1,0:T(8,128)(2,1)S(1)}, bf16[256,256]{1,0:T(8,128)(2,1)S(1)}, u32[]{:S(2)}, u32[]{:S(2)}) collective-permute-start(bf16[256,256]{1,0:T(8,128)(2,1)S(1)} %add_convert_fusion.1.refs_0_), channel_id=1, source_target_pairs={{0,8},{1,9},{2,10},{3,11},{4,12},{5,13},{6,14},{7,15},{8,0},{9,1},... | collective-permute-start | bytes 393224 | tf_op jit(solution)/shard_map/ppermute | solution.py:34
  35.2 3.6 %copy-start.1 = (bf16[2,4,512,256]{3,2,1,0:T(8,128)(2,1)S(1)}, bf16[2,4,512,256]{3,2,1,0:T(8,128)(2,1)}, u32[]{:S(2)}) copy-start(bf16[2,4,512,256]{3,2,1,0:T(8,128)(2,1)} %copy-done) | copy-start | bytes 6291460
  39.4 3.5 %collective-permute-start.13 = (bf16[256,256]{1,0:T(8,128)(2,1)S(1)}, bf16[256,256]{1,0:T(8,128)(2,1)S(1)}, u32[]{:S(2)}, u32[]{:S(2)}) collective-permute-start(bf16[256,256]{1,0:T(8,128)(2,1)S(1)} %collective-permute-done.9.refs_2_), channel_id=1, source_target_pairs={{0,4},{1,5},{2,6},{3,7},{4,0},{5,1},{6,2},{7,3},{8,12},{9,13},{10,... | collective-permute-start | bytes 393224 | tf_op jit(solution)/shard_map/ppermute | solution.py:34
  41.2 1.4 %collective-permute-start.12 = (bf16[256,256]{1,0:T(8,128)(2,1)S(1)}, bf16[256,256]{1,0:T(8,128)(2,1)S(1)}, u32[]{:S(2)}, u32[]{:S(2)}) collective-permute-start(bf16[256,256]{1,0:T(8,128)(2,1)S(1)} %collective-permute-done.8.refs_1_), channel_id=1, source_target_pairs={{0,4},{1,5},{2,6},{3,7},{4,0},{5,1},{6,2},{7,3},{8,12},{9,13},{10,... | collective-permute-start | bytes 393224 | tf_op jit(solution)/shard_map/ppermute | solution.py:34
  41.3 1.5 %collective-permute-start.11 = (bf16[256,256]{1,0:T(8,128)(2,1)S(1)}, bf16[256,256]{1,0:T(8,128)(2,1)S(1)}, u32[]{:S(2)}, u32[]{:S(2)}) collective-permute-start(bf16[256,256]{1,0:T(8,128)(2,1)S(1)} %collective-permute-done.7.refs_0_), channel_id=1, source_target_pairs={{0,4},{1,5},{2,6},{3,7},{4,0},{5,1},{6,2},{7,3},{8,12},{9,13},{10,... | collective-permute-start | bytes 393224 | tf_op jit(solution)/shard_map/ppermute | solution.py:34
  43.6 1.4 %collective-permute-start.14 = (f32[2,32,256]{2,1,0:T(8,128)S(1)}, f32[2,32,256]{2,1,0:T(8,128)S(1)}, u32[]{:S(2)}, u32[]{:S(2)}) collective-permute-start(f32[2,32,256]{2,1,0:T(8,128)S(1)} %get-tuple-element.63), channel_id=1, source_target_pairs={{0,4},{1,5},{2,6},{3,7},{4,0},{5,1},{6,2},{7,3},{8,12},{9,13},{10,... | collective-permute-start | bytes 196616 | tf_op jit(solution)/shard_map/ppermute | solution.py:34
  45.0 6.6 %collective-permute-start.17 = (f32[2,32,256]{2,1,0:T(8,128)S(1)}, f32[2,32,256]{2,1,0:T(8,128)S(1)}, u32[]{:S(2)}, u32[]{:S(2)}) collective-permute-start(f32[2,32,256]{2,1,0:T(8,128)S(1)} %add.72), channel_id=1, source_target_pairs={{0,24},{1,25},{2,26},{3,27},{4,28},{5,29},{6,30},{7,31},{8,16},{9,... | collective-permute-start | bytes 196616 | tf_op jit(solution)/shard_map/ppermute | solution.py:34
  46.6 5.0 %collective-permute-start.16 = (f32[2,32,256]{2,1,0:T(8,128)S(1)}, f32[2,32,256]{2,1,0:T(8,128)S(1)}, u32[]{:S(2)}, u32[]{:S(2)}) collective-permute-start(f32[2,32,256]{2,1,0:T(8,128)S(1)} %add.72), channel_id=1, source_target_pairs={{0,16},{1,17},{2,18},{3,19},{4,20},{5,21},{6,22},{7,23},{8,24},{9,... | collective-permute-start | bytes 196616 | tf_op jit(solution)/shard_map/ppermute | solution.py:34
  47.3 4.4 %collective-permute-start.15 = (f32[2,32,256]{2,1,0:T(8,128)S(1)}, f32[2,32,256]{2,1,0:T(8,128)S(1)}, u32[]{:S(2)}, u32[]{:S(2)}) collective-permute-start(f32[2,32,256]{2,1,0:T(8,128)S(1)} %add.72), channel_id=1, source_target_pairs={{0,8},{1,9},{2,10},{3,11},{4,12},{5,13},{6,14},{7,15},{8,0},{9,1},... | collective-permute-start | bytes 196616 | tf_op jit(solution)/shard_map/ppermute | solution.py:34

commit v6 on v5

--- a/solution.py
+++ b/solution.py
@@ -223,6 +223,7 @@
     m_count, rank, _ = held_ref.shape
     row_at = lax.broadcasted_iota(jnp.int32, (rank, rank), 0)
     col_at = lax.broadcasted_iota(jnp.int32, (rank, rank), 1)
+    lane = lax.broadcasted_iota(jnp.int32, (1, rank), 1)
     held = [grams[0][m] for m in range(m_count)] if len(grams) == 1 else [
         tree_sum([grams[0][0, m]] + [grams[1][c, m] for c in range(grams[1].shape[0])])
         + tree_sum([grams[0][1, m]] + [grams[2][c, m] for c in range(grams[2].shape[0])])
@@ -232,11 +233,8 @@
         for m in range(m_count):
             a = held[m]
             row, col = a[k:k + 1, :], a[:, k:k + 1]
-            inv = 1.0 / a[k:k + 1, k:k + 1]
-            scaled = row * inv
-            rest = a - col * scaled
-            rest = jnp.where(row_at == k, scaled, rest)
-            held[m] = jnp.where(col_at == k, jnp.where(row_at == k, inv, -col * inv), rest)
+            scaled = jnp.where(lane == k, 1.0, row) * (1.0 / a[k:k + 1, k:k + 1])
+            held[m] = jnp.where(row_at == k, scaled, jnp.where(col_at == k, 0.0, a) - col * scaled)
     for m in range(m_count):
         held_ref[m] = held[m]
 
@@ -268,49 +266,51 @@
     return jnp.dot(wide, tall, preferred_element_type=F32)
 
 
-def expand_kernel(scale, place_ref, left_ref, inverse_ref, right_ref, update_ref, wide_ref, held_ref, sems):
+EXPAND_ROWS = 512
+
+
+def expand_kernel(scale, left_ref, inverse_ref, right_ref, update_ref, wide_ref, held_ref, sems):
     m_count, rank, width = right_ref.shape
     pack = LANES // rank
-    count, block, _ = left_ref.shape
-    wide_ref[...] = jnp.zeros_like(wide_ref)
     copies = []
     for m in range(m_count):
         z = small_dot(inverse_ref[m], right_ref[m]) * scale
         high = z.astype(BF16)
         low = (z - high.astype(F32)).astype(BF16)
+        wide_ref[m] = jnp.zeros(wide_ref.shape[1:], BF16)
         for j in range(pack):
             wide_ref[m, j, pl.ds(j * rank, rank), :] = high
             wide_ref[m, j, pl.ds(LANES + j * rank, rank), :] = low
-            for p in range(count):
-                left = left_ref[p, :, m * LANES:(m + 1) * LANES]
+            for p in range(left_ref.shape[0] // EXPAND_ROWS):
+                where = pl.ds(p * EXPAND_ROWS, EXPAND_ROWS)
+                left = left_ref[where, m * LANES:(m + 1) * LANES]
                 rows = jnp.dot(jnp.concatenate([left, left], axis=1), wide_ref[m, j], preferred_element_type=F32)
-                held_ref[m, j, p] = rows.astype(BF16)
-                where = pl.ds(pl.multiple_of(place_ref[p] * block, block), block)
-                copy = pltpu.make_async_copy(held_ref.at[m, j, p], update_ref.at[m, j, where, :], sems.at[m, j, p])
+                held_ref[m, j, where, :] = rows.astype(BF16)
+                copy = pltpu.make_async_copy(held_ref.at[m, j, where, :], update_ref.at[m, j, where, :], sems.at[m, j, p])
                 copy.start(priority=p % 2)
                 copies.append(copy)
-    for copy in copies:
-        copy.wait()
-
-
-def expand(pieces, places, inverse, right, scale):
+    wait_all(copies)
+
+
+def expand(left, inverse, right, scale):
     m_count, rank, width = right.shape
     pack = LANES // rank
-    count, block, _ = pieces.shape
+    rows = left.shape[0]
+    shape = (m_count, pack, rows, width)
     out = pl.pallas_call(
         lambda *refs: expand_kernel(scale, *refs),
-        in_specs=[scalar(), whole(), whole(), whole()],
+        in_specs=[whole()] * 3,
         out_specs=pl.BlockSpec(memory_space=pl.ANY),
-        out_shape=jax.ShapeDtypeStruct((m_count, pack, count * block, width), BF16),
+        out_shape=jax.ShapeDtypeStruct(shape, BF16),
         scratch_shapes=[
             pltpu.VMEM((m_count, pack, 2 * LANES, width), BF16),
-            pltpu.VMEM((m_count, pack, count, block, width), BF16),
-            pltpu.SemaphoreType.DMA((m_count, pack, count)),
+            pltpu.VMEM(shape, BF16),
+            pltpu.SemaphoreType.DMA((m_count, pack, rows // EXPAND_ROWS)),
         ],
         compiler_params=params(20),
         name="expand",
-    )(places, pieces, inverse, right)
-    return out.reshape(m_count, pack * count * block, width)
+    )(left, inverse, right)
+    return out.reshape(m_count, pack * rows, width)
 
 
 def sum_right(right, grams):
@@ -404,9 +404,10 @@
     right, gram_far = project_others(far_left[1:], where[n:], right)
 
     right, inverse = sum_right(right, (gram_own, gram_near, gram_far))
-    pieces = jnp.stack(near_left + far_left)
-    places = jnp.stack(near + far).astype(jnp.int32)
-    return expand(pieces, places, inverse, right, 1.0 / (outer * hst))
+    left = jnp.zeros((rows, own.shape[1]), BF16)
+    for place, part in zip(near + far, near_left + far_left):
+        left = lax.dynamic_update_slice(left, part, (place * chunk, 0))
+    return expand(left, inverse, right, 1.0 / (outer * hst))
 
 
 def solution(mesh):

time: 56.8 us -> 56 us (0.986)
  Pallas kernels: 28.1 us -> 26.1 us
  waiting for transfers between devices: 9.53 us -> 10.7 us
    pallas_call x2, Pallas kernels: 3.96 us -> 2.68 us  [invert(): pl.pallas_call(lambda *refs: invert_kernel(steps, *refs), in_specs=[whole...]
    ppermute x18, waiting for transfers between devices: 9.53 us -> 10.7 us  [exchange(): return lax.ppermute(x, AXES, pairs)]
    pallas_call x1, Pallas kernels: 4.77 us -> 4.06 us  [expand(): pl.pallas_call(lambda *refs: expand_kernel(scale, *refs), in_specs=[whole...]
  transfers between devices with their start and end apart: 18 -> 18, of which waited for: 8 -> 9; matrix products, arithmetic and copies ran while one was open for 1% -> 1% of each run, Pallas kernels for 29% -> 28%
where the time goes in v6:
time: 56 us; the launch traced here: 55.6 us
  Pallas kernels  26.1 us (47%)
  starting transfers between devices  17.7 us (32%)
  waiting for transfers between devices  10.7 us (19%)
    ppermute x18, starting transfers between devices, exchange(): return lax.ppermute(x, AXES, pairs)  17.7 us
    ppermute x18, waiting for transfers between devices, exchange(): return lax.ppermute(x, AXES, pairs)  10.7 us
    pallas_call x2, Pallas kernels, mix(): pl.pallas_call(mix_kernel, in_specs=[scalar()] + [hbm] * 3, out_specs=[wh...  9.15 us
    pallas_call x3, Pallas kernels, keep(): pl.pallas_call(keep_kernel, in_specs=[scalar()] + [pl.BlockSpec(memory_sp...  8.1 us
    pallas_call x1, Pallas kernels, expand(): pl.pallas_call(lambda *refs: expand_kernel(scale, *refs), in_specs=[whole...  4.06 us
    pallas_call x2, Pallas kernels, invert(): pl.pallas_call(lambda *refs: invert_kernel(steps, *refs), in_specs=[whole...  2.68 us
    pallas_call x3, Pallas kernels, project(): pl.pallas_call(lambda *refs: project_kernel(chunks, *refs), in_specs=[who...  2.09 us
  transfers between devices with their start and end apart: 18, of which 9 were waited for; matrix products, arithmetic and copies ran while one was open for 1% of the time, Pallas kernels for 28%

profile of v6, /device:TPU:0, one launch (start us, length us, event | category | flops | bytes accessed | tf_op | source)
XLA Modules:
  0.0 55.6 jit_solution(6467225657098140717)
XLA Ops:
  0.1 5.9 %mix.2 = (bf16[768,256]{1,0:T(8,128)(2,1)S(1)}, f32[768,256]{1,0:T(8,128)S(1)}) custom-call(s32[6]{0:T(128)S(1)} %stack.60.place_ref, f32[2,32,256]{2,1,0:T(8,128)} %bitcast.28, bf16[2,4,2048,256]{3,2,1,0:T(8,128)(2,1)} %bitcast.18, bf16[2,4,2048,256]{3,2,1,0:T(8,128)(2,1)} %bitcast.23), custom_call_target="tpu_custom_call" | custom-call | flops 1000000 | tf_op jit(solution)/shard_map/mix/pallas_call | solution.py:128
  6.0 0.5 collective-permute-start
  6.5 1.3 %collective-permute-done = bf16[768,256]{1,0:T(8,128)(2,1)S(1)} collective-permute-done((bf16[768,256]{1,0:T(8,128)(2,1)S(1)}, bf16[768,256]{1,0:T(8,128)(2,1)S(1)}, u32[]{:S(2)}, u32[]{:S(2)}) %collective-permute-start) | collective-permute-done | bytes 393248 | tf_op jit(solution)/shard_map/ppermute | solution.py:34
  8.0 2.9 %collective-permute-start.2 = (bf16[256,256]{1,0:T(8,128)(2,1)S(1)}, bf16[256,256]{1,0:T(8,128)(2,1)S(1)}, u32[]{:S(2)}, u32[]{:S(2)}) collective-permute-start(bf16[256,256]{1,0:T(8,128)(2,1)S(1)} %get-tuple-element.69), channel_id=1, source_target_pairs={{0,8},{1,9},{2,10},{3,11},{4,12},{5,13},{6,14},{7,15},{8,0},{9,1},... | collective-permute-start | bytes 393224 | tf_op jit(solution)/shard_map/ppermute | solution.py:34
  11.0 1.5 %collective-permute-start.4 = (bf16[256,256]{1,0:T(8,128)(2,1)S(1)}, bf16[256,256]{1,0:T(8,128)(2,1)S(1)}, u32[]{:S(2)}, u32[]{:S(2)}) collective-permute-start(bf16[256,256]{1,0:T(8,128)(2,1)S(1)} %get-tuple-element.70), channel_id=1, source_target_pairs={{0,24},{1,25},{2,26},{3,27},{4,28},{5,29},{6,30},{7,31},{8,16},{9,... | collective-permute-start | bytes 393224 | tf_op jit(solution)/shard_map/ppermute | solution.py:34
  12.6 3.2 %mix.3 = (bf16[256,256]{1,0:T(8,128)(2,1)S(1)}, f32[256,256]{1,0:T(8,128)S(1)}, bf16[2,4,512,256]{3,2,1,0:T(8,128)(2,1)S(1)}) custom-call(s32[2]{0:T(128)S(1)} %pad_add_fusion.place_ref, f32[2,32,256]{2,1,0:T(8,128)} %bitcast.29, bf16[2,4,2048,256]{3,2,1,0:T(8,128)(2,1)} %bitcast.19, bf16[2,4,2048,256]{3,2,1,0:T(8,128)(2,1)} %bitcast.24), custom_call_target="tpu_custom_call" | custom-call | flops 1000000 | tf_op jit(solution)/shard_map/mix/pallas_call | solution.py:128
  15.9 3.0 %collective-permute-done.4 = bf16[256,256]{1,0:T(8,128)(2,1)S(1)} collective-permute-done((bf16[256,256]{1,0:T(8,128)(2,1)S(1)}, bf16[256,256]{1,0:T(8,128)(2,1)S(1)}, u32[]{:S(2)}, u32[]{:S(2)}) %collective-permute-start.4) | collective-permute-done | bytes 131104 | tf_op jit(solution)/shard_map/ppermute | solution.py:34
  18.9 1.4 %collective-permute-done.3 = bf16[256,256]{1,0:T(8,128)(2,1)S(1)} collective-permute-done((bf16[256,256]{1,0:T(8,128)(2,1)S(1)}, bf16[256,256]{1,0:T(8,128)(2,1)S(1)}, u32[]{:S(2)}, u32[]{:S(2)}) %collective-permute-start.3) | collective-permute-done | bytes 131104 | tf_op jit(solution)/shard_map/ppermute | solution.py:34
  20.3 1.6 %collective-permute-start.5 = (bf16[256,256]{1,0:T(8,128)(2,1)S(1)}, bf16[256,256]{1,0:T(8,128)(2,1)S(1)}, u32[]{:S(2)}, u32[]{:S(2)}) collective-permute-start(bf16[256,256]{1,0:T(8,128)(2,1)S(1)} %add_convert_fusion.3), channel_id=1, source_target_pairs={{0,1},{1,0},{2,3},{3,2},{4,6},{5,7},{6,4},{7,5},{8,9},{9,8},{10,11... | collective-permute-start | bytes 393224 | tf_op jit(solution)/shard_map/ppermute | solution.py:34
  22.0 2.9 %keep.3.refs_3_ = bf16[2,4,512,256]{3,2,1,0:T(8,128)(2,1)S(1)} custom-call(s32[2]{0:T(128)S(1)} %pad_add_fusion.1.place_ref, bf16[2,4,2048,256]{3,2,1,0:T(8,128)(2,1)} %bitcast.20, bf16[2,4,2048,256]{3,2,1,0:T(8,128)(2,1)} %bitcast.25), custom_call_target="tpu_custom_call" | custom-call | flops 1000000 | tf_op jit(solution)/shard_map/keep/pallas_call | solution.py:162
  24.9 0.6 %collective-permute-done.5 = bf16[256,256]{1,0:T(8,128)(2,1)S(1)} collective-permute-done((bf16[256,256]{1,0:T(8,128)(2,1)S(1)}, bf16[256,256]{1,0:T(8,128)(2,1)S(1)}, u32[]{:S(2)}, u32[]{:S(2)}) %collective-permute-start.5) | collective-permute-done | bytes 131104 | tf_op jit(solution)/shard_map/ppermute | solution.py:34
  25.5 2.9 %collective-permute-start.6 = (bf16[256,256]{1,0:T(8,128)(2,1)S(1)}, bf16[256,256]{1,0:T(8,128)(2,1)S(1)}, u32[]{:S(2)}, u32[]{:S(2)}) collective-permute-start(bf16[256,256]{1,0:T(8,128)(2,1)S(1)} %add_convert_fusion.2), channel_id=1, source_target_pairs={{0,2},{1,3},{2,0},{3,1},{4,5},{5,4},{6,7},{7,6},{8,10},{9,11},{10,... | collective-permute-start | bytes 393224 | tf_op jit(solution)/shard_map/ppermute | solution.py:34
  28.4 1.7 %keep.4.refs_4_ = bf16[2,4,256,256]{3,2,1,0:T(8,128)(2,1)S(1)} custom-call(s32[1]{0:T(128)} %bitcast.13.place_ref, bf16[2,4,2048,256]{3,2,1,0:T(8,128)(2,1)} %bitcast.21, bf16[2,4,2048,256]{3,2,1,0:T(8,128)(2,1)} %bitcast.26), custom_call_target="tpu_custom_call" | custom-call | flops 1000000 | tf_op jit(solution)/shard_map/keep/pallas_call | solution.py:162
  30.1 1.4 %collective-permute-done.6 = bf16[256,256]{1,0:T(8,128)(2,1)S(1)} collective-permute-done((bf16[256,256]{1,0:T(8,128)(2,1)S(1)}, bf16[256,256]{1,0:T(8,128)(2,1)S(1)}, u32[]{:S(2)}, u32[]{:S(2)}) %collective-permute-start.6) | collective-permute-done | bytes 131104 | tf_op jit(solution)/shard_map/ppermute | solution.py:34
  31.6 1.5 %collective-permute-start.9 = (bf16[256,256]{1,0:T(8,128)(2,1)S(1)}, bf16[256,256]{1,0:T(8,128)(2,1)S(1)}, u32[]{:S(2)}, u32[]{:S(2)}) collective-permute-start(bf16[256,256]{1,0:T(8,128)(2,1)S(1)} %add_convert_fusion.1.refs_0_), channel_id=1, source_target_pairs={{0,24},{1,25},{2,26},{3,27},{4,28},{5,29},{6,30},{7,31},{8,16},{9,... | collective-permute-start | bytes 393224 | tf_op jit(solution)/shard_map/ppermute | solution.py:34
  33.1 1.5 %collective-permute-start.8 = (bf16[256,256]{1,0:T(8,128)(2,1)S(1)}, bf16[256,256]{1,0:T(8,128)(2,1)S(1)}, u32[]{:S(2)}, u32[]{:S(2)}) collective-permute-start(bf16[256,256]{1,0:T(8,128)(2,1)S(1)} %add_convert_fusion.1.refs_0_), channel_id=1, source_target_pairs={{0,16},{1,17},{2,18},{3,19},{4,20},{5,21},{6,22},{7,23},{8,24},{9,... | collective-permute-start | bytes 393224 | tf_op jit(solution)/shard_map/ppermute | solution.py:34
  34.6 0.5 collective-permute-start.7
  35.2 3.6 %keep.5.refs_3_ = bf16[2,4,768,256]{3,2,1,0:T(8,128)(2,1)S(1)} custom-call(s32[3]{0:T(128)S(1)} %pad_add_fusion.2.place_ref, bf16[2,4,2048,256]{3,2,1,0:T(8,128)(2,1)} %bitcast.22, bf16[2,4,2048,256]{3,2,1,0:T(8,128)(2,1)} %bitcast.27), custom_call_target="tpu_custom_call" | custom-call | flops 1000000 | tf_op jit(solution)/shard_map/keep/pallas_call | solution.py:162
  38.9 0.5 project.3
  39.6 1.6 %collective-permute-done.8.refs_1_ = bf16[256,256]{1,0:T(8,128)(2,1)S(1)} collective-permute-done((bf16[256,256]{1,0:T(8,128)(2,1)S(1)}, bf16[256,256]{1,0:T(8,128)(2,1)S(1)}, u32[]{:S(2)}, u32[]{:S(2)}) %collective-permute-start.8) | collective-permute-done | bytes 131104 | tf_op jit(solution)/shard_map/ppermute | solution.py:34
  41.2 0.5 collective-permute-start.11
  41.8 0.8 %project.4 = (f32[2,32,256]{2,1,0:T(8,128)S(1)}, f32[3,2,32,32]{3,2,1,0:T(8,128)S(1)}) custom-call(bf16[256,256]{1,0:T(8,128)(2,1)S(1)} %collective-permute-done.7.refs_0_, bf16[256,256]{1,0:T(8,128)(2,1)S(1)} %collective-permute-done.8.refs_1_, bf16[256,256]{1,0:T(8,128)(2,1)S(1)} %collective-permute-done.9.refs_2_, ...), custom_call_target="tpu_custom_call" | custom-call | flops 1000000 | tf_op jit(solution)/shard_map/project/pallas_call | solution.py:204
  42.7 0.8 %project.5 = (f32[2,32,256]{2,1,0:T(8,128)S(1)}, f32[3,2,32,32]{3,2,1,0:T(8,128)S(1)}) custom-call(bf16[256,256]{1,0:T(8,128)(2,1)S(1)} %collective-permute-done.11.refs_0_, bf16[256,256]{1,0:T(8,128)(2,1)S(1)} %collective-permute-done.12.refs_1_, bf16[256,256]{1,0:T(8,128)(2,1)S(1)} %collective-permute-done.13.refs_2_, ...), custom_call_target="tpu_custom_call" | custom-call | flops 1000000 | tf_op jit(solution)/shard_map/project/pallas_call | solution.py:204
  43.5 0.4 collective-permute-start.14
  43.9 0.7 %invert.2.refs_0_ = f32[2,32,32]{2,1,0:T(8,128)S(1)} custom-call(f32[2,2,32,32]{3,2,1,0:T(8,128)S(1)} %get-tuple-element.64.refs_0_, f32[3,2,32,32]{3,2,1,0:T(8,128)S(1)} %get-tuple-element.65.refs_1_, f32[3,2,32,32]{3,2,1,0:T(8,128)S(1)} %get-tuple-element.66.refs_2_), custom_call_target="tpu_custom_call" | custom-call | flops 1000000 | tf_op jit(solution)/shard_map/invert/pallas_call | solution.py:243
  44.6 0.2 collective-permute-done.14
  44.8 1.5 %collective-permute-start.17 = (f32[2,32,256]{2,1,0:T(8,128)S(1)}, f32[2,32,256]{2,1,0:T(8,128)S(1)}, u32[]{:S(2)}, u32[]{:S(2)}) collective-permute-start(f32[2,32,256]{2,1,0:T(8,128)S(1)} %add.104), channel_id=1, source_target_pairs={{0,24},{1,25},{2,26},{3,27},{4,28},{5,29},{6,30},{7,31},{8,16},{9,... | collective-permute-start | bytes 196616 | tf_op jit(solution)/shard_map/ppermute | solution.py:34
  46.3 0.7 %collective-permute-start.16 = (f32[2,32,256]{2,1,0:T(8,128)S(1)}, f32[2,32,256]{2,1,0:T(8,128)S(1)}, u32[]{:S(2)}, u32[]{:S(2)}) collective-permute-start(f32[2,32,256]{2,1,0:T(8,128)S(1)} %add.104), channel_id=1, source_target_pairs={{0,16},{1,17},{2,18},{3,19},{4,20},{5,21},{6,22},{7,23},{8,24},{9,... | collective-permute-start | bytes 196616 | tf_op jit(solution)/shard_map/ppermute | solution.py:34
  47.1 1.3 %collective-permute-start.15 = (f32[2,32,256]{2,1,0:T(8,128)S(1)}, f32[2,32,256]{2,1,0:T(8,128)S(1)}, u32[]{:S(2)}, u32[]{:S(2)}) collective-permute-start(f32[2,32,256]{2,1,0:T(8,128)S(1)} %add.104), channel_id=1, source_target_pairs={{0,8},{1,9},{2,10},{3,11},{4,12},{5,13},{6,14},{7,15},{8,0},{9,1},... | collective-permute-start | bytes 196616 | tf_op jit(solution)/shard_map/ppermute | solution.py:34
  48.4 2.0 %invert.3.refs_1_ = f32[2,32,32]{2,1,0:T(8,128)S(1)} custom-call(f32[2,32,32]{2,1,0:T(8,128)S(1)} %invert.2.refs_0_), custom_call_target="tpu_custom_call" | custom-call | flops 1000000 | tf_op jit(solution)/shard_map/invert/pallas_call | solution.py:243
  50.4 1.1 %collective-permute-done.16 = f32[2,32,256]{2,1,0:T(8,128)S(1)} collective-permute-done((f32[2,32,256]{2,1,0:T(8,128)S(1)}, f32[2,32,256]{2,1,0:T(8,128)S(1)}, u32[]{:S(2)}, u32[]{:S(2)}) %collective-permute-start.16) | collective-permute-done | bytes 65568 | tf_op jit(solution)/shard_map/ppermute | solution.py:34
  51.5 4.1 %expand.1 = bf16[2,4,2048,256]{3,2,1,0:T(8,128)(2,1)} custom-call(bf16[2048,256]{1,0:T(8,128)(2,1)S(1)} %constant_dynamic-update-slice_fusion.refs_0_, f32[2,32,32]{2,1,0:T(8,128)S(1)} %invert.3.refs_1_, f32[2,32,256]{2,1,0:T(8,128)S(1)} %add_add_fusion.refs_2_), custom_call_target="tpu_custom_call" | custom-call | tf_op jit(solution)/shard_map/expand/pallas_call | solution.py:300
  (39 shorter events, 1.3 us)
Async XLA Ops:
  6.0 1.9 %collective-permute-start = (bf16[768,256]{1,0:T(8,128)(2,1)S(1)}, bf16[768,256]{1,0:T(8,128)(2,1)S(1)}, u32[]{:S(2)}, u32[]{:S(2)}) collective-permute-start(bf16[768,256]{1,0:T(8,128)(2,1)S(1)} %get-tuple-element.38), channel_id=1, source_target_pairs={{0,4},{1,5},{2,6},{3,7},{4,0},{5,1},{6,2},{7,3},{8,12},{9,13},{10,... | collective-permute-start | bytes 1179656 | tf_op jit(solution)/shard_map/ppermute | solution.py:34
  8.0 7.9 %collective-permute-start.2 = (bf16[256,256]{1,0:T(8,128)(2,1)S(1)}, bf16[256,256]{1,0:T(8,128)(2,1)S(1)}, u32[]{:S(2)}, u32[]{:S(2)}) collective-permute-start(bf16[256,256]{1,0:T(8,128)(2,1)S(1)} %get-tuple-element.69), channel_id=1, source_target_pairs={{0,8},{1,9},{2,10},{3,11},{4,12},{5,13},{6,14},{7,15},{8,0},{9,1},... | collective-permute-start | bytes 393224 | tf_op jit(solution)/shard_map/ppermute | solution.py:34
  11.0 7.9 %collective-permute-start.4 = (bf16[256,256]{1,0:T(8,128)(2,1)S(1)}, bf16[256,256]{1,0:T(8,128)(2,1)S(1)}, u32[]{:S(2)}, u32[]{:S(2)}) collective-permute-start(bf16[256,256]{1,0:T(8,128)(2,1)S(1)} %get-tuple-element.70), channel_id=1, source_target_pairs={{0,24},{1,25},{2,26},{3,27},{4,28},{5,29},{6,30},{7,31},{8,16},{9,... | collective-permute-start | bytes 393224 | tf_op jit(solution)/shard_map/ppermute | solution.py:34
  12.5 7.8 %collective-permute-start.3 = (bf16[256,256]{1,0:T(8,128)(2,1)S(1)}, bf16[256,256]{1,0:T(8,128)(2,1)S(1)}, u32[]{:S(2)}, u32[]{:S(2)}) collective-permute-start(bf16[256,256]{1,0:T(8,128)(2,1)S(1)} %get-tuple-element.71), channel_id=1, source_target_pairs={{0,16},{1,17},{2,18},{3,19},{4,20},{5,21},{6,22},{7,23},{8,24},{9,... | collective-permute-start | bytes 393224 | tf_op jit(solution)/shard_map/ppermute | solution.py:34
  15.8 9.1 %copy-start = (bf16[2,4,512,256]{3,2,1,0:T(8,128)(2,1)}, bf16[2,4,512,256]{3,2,1,0:T(8,128)(2,1)S(1)}, u32[]{:S(2)}) copy-start(bf16[2,4,512,256]{3,2,1,0:T(8,128)(2,1)S(1)} %get-tuple-element.52.refs_2_) | copy-start | bytes 6291460
  15.8 4.4 %collective-permute-start.1 = (bf16[256,256]{1,0:T(8,128)(2,1)S(1)}, bf16[256,256]{1,0:T(8,128)(2,1)S(1)}, u32[]{:S(2)}, u32[]{:S(2)}) collective-permute-start(bf16[256,256]{1,0:T(8,128)(2,1)S(1)} %get-tuple-element.42), channel_id=1, source_target_pairs={{0,4},{1,5},{2,6},{3,7},{4,0},{5,1},{6,2},{7,3},{8,12},{9,13},{10,... | collective-permute-start | bytes 393224 | tf_op jit(solution)/shard_map/ppermute | solution.py:34
  20.3 5.2 %collective-permute-start.5 = (bf16[256,256]{1,0:T(8,128)(2,1)S(1)}, bf16[256,256]{1,0:T(8,128)(2,1)S(1)}, u32[]{:S(2)}, u32[]{:S(2)}) collective-permute-start(bf16[256,256]{1,0:T(8,128)(2,1)S(1)} %add_convert_fusion.3), channel_id=1, source_target_pairs={{0,1},{1,0},{2,3},{3,2},{4,6},{5,7},{6,4},{7,5},{8,9},{9,8},{10,11... | collective-permute-start | bytes 393224 | tf_op jit(solution)/shard_map/ppermute | solution.py:34
  25.5 5.9 %collective-permute-start.6 = (bf16[256,256]{1,0:T(8,128)(2,1)S(1)}, bf16[256,256]{1,0:T(8,128)(2,1)S(1)}, u32[]{:S(2)}, u32[]{:S(2)}) collective-permute-start(bf16[256,256]{1,0:T(8,128)(2,1)S(1)} %add_convert_fusion.2), channel_id=1, source_target_pairs={{0,2},{1,3},{2,0},{3,1},{4,5},{5,4},{6,7},{7,6},{8,10},{9,11},{10,... | collective-permute-start | bytes 393224 | tf_op jit(solution)/shard_map/ppermute | solution.py:34
  31.5 7.4 %collective-permute-start.10 = (bf16[256,256]{1,0:T(8,128)(2,1)S(1)}, bf16[256,256]{1,0:T(8,128)(2,1)S(1)}, u32[]{:S(2)}, u32[]{:S(2)}) collective-permute-start(bf16[256,256]{1,0:T(8,128)(2,1)S(1)} %add_convert_fusion.1.refs_0_), channel_id=1, source_target_pairs={{0,4},{1,5},{2,6},{3,7},{4,0},{5,1},{6,2},{7,3},{8,12},{9,13},{10,... | collective-permute-start | bytes 393224 | tf_op jit(solution)/shard_map/ppermute | solution.py:34
  31.6 7.9 %collective-permute-start.9 = (bf16[256,256]{1,0:T(8,128)(2,1)S(1)}, bf16[256,256]{1,0:T(8,128)(2,1)S(1)}, u32[]{:S(2)}, u32[]{:S(2)}) collective-permute-start(bf16[256,256]{1,0:T(8,128)(2,1)S(1)} %add_convert_fusion.1.refs_0_), channel_id=1, source_target_pairs={{0,24},{1,25},{2,26},{3,27},{4,28},{5,29},{6,30},{7,31},{8,16},{9,... | collective-permute-start | bytes 393224 | tf_op jit(solution)/shard_map/ppermute | solution.py:34
  33.1 8.1 %collective-permute-start.8 = (bf16[256,256]{1,0:T(8,128)(2,1)S(1)}, bf16[256,256]{1,0:T(8,128)(2,1)S(1)}, u32[]{:S(2)}, u32[]{:S(2)}) collective-permute-start(bf16[256,256]{1,0:T(8,128)(2,1)S(1)} %add_convert_fusion.1.refs_0_), channel_id=1, source_target_pairs={{0,16},{1,17},{2,18},{3,19},{4,20},{5,21},{6,22},{7,23},{8,24},{9,... | collective-permute-start | bytes 393224 | tf_op jit(solution)/shard_map/ppermute | solution.py:34
  34.6 6.6 %collective-permute-start.7 = (bf16[256,256]{1,0:T(8,128)(2,1)S(1)}, bf16[256,256]{1,0:T(8,128)(2,1)S(1)}, u32[]{:S(2)}, u32[]{:S(2)}) collective-permute-start(bf16[256,256]{1,0:T(8,128)(2,1)S(1)} %add_convert_fusion.1.refs_0_), channel_id=1, source_target_pairs={{0,8},{1,9},{2,10},{3,11},{4,12},{5,13},{6,14},{7,15},{8,0},{9,1},... | collective-permute-start | bytes 393224 | tf_op jit(solution)/shard_map/ppermute | solution.py:34
  35.2 3.7 %copy-start.1 = (bf16[2,4,512,256]{3,2,1,0:T(8,128)(2,1)S(1)}, bf16[2,4,512,256]{3,2,1,0:T(8,128)(2,1)}, u32[]{:S(2)}) copy-start(bf16[2,4,512,256]{3,2,1,0:T(8,128)(2,1)} %copy-done) | copy-start | bytes 6291460
  39.5 3.3 %collective-permute-start.13 = (bf16[256,256]{1,0:T(8,128)(2,1)S(1)}, bf16[256,256]{1,0:T(8,128)(2,1)S(1)}, u32[]{:S(2)}, u32[]{:S(2)}) collective-permute-start(bf16[256,256]{1,0:T(8,128)(2,1)S(1)} %collective-permute-done.9.refs_2_), channel_id=1, source_target_pairs={{0,4},{1,5},{2,6},{3,7},{4,0},{5,1},{6,2},{7,3},{8,12},{9,13},{10,... | collective-permute-start | bytes 393224 | tf_op jit(solution)/shard_map/ppermute | solution.py:34
  41.2 1.4 %collective-permute-start.12 = (bf16[256,256]{1,0:T(8,128)(2,1)S(1)}, bf16[256,256]{1,0:T(8,128)(2,1)S(1)}, u32[]{:S(2)}, u32[]{:S(2)}) collective-permute-start(bf16[256,256]{1,0:T(8,128)(2,1)S(1)} %collective-permute-done.8.refs_1_), channel_id=1, source_target_pairs={{0,4},{1,5},{2,6},{3,7},{4,0},{5,1},{6,2},{7,3},{8,12},{9,13},{10,... | collective-permute-start | bytes 393224 | tf_op jit(solution)/shard_map/ppermute | solution.py:34
  41.2 1.5 %collective-permute-start.11 = (bf16[256,256]{1,0:T(8,128)(2,1)S(1)}, bf16[256,256]{1,0:T(8,128)(2,1)S(1)}, u32[]{:S(2)}, u32[]{:S(2)}) collective-permute-start(bf16[256,256]{1,0:T(8,128)(2,1)S(1)} %collective-permute-done.7.refs_0_), channel_id=1, source_target_pairs={{0,4},{1,5},{2,6},{3,7},{4,0},{5,1},{6,2},{7,3},{8,12},{9,13},{10,... | collective-permute-start | bytes 393224 | tf_op jit(solution)/shard_map/ppermute | solution.py:34
  43.5 1.3 %collective-permute-start.14 = (f32[2,32,256]{2,1,0:T(8,128)S(1)}, f32[2,32,256]{2,1,0:T(8,128)S(1)}, u32[]{:S(2)}, u32[]{:S(2)}) collective-permute-start(f32[2,32,256]{2,1,0:T(8,128)S(1)} %get-tuple-element.63), channel_id=1, source_target_pairs={{0,4},{1,5},{2,6},{3,7},{4,0},{5,1},{6,2},{7,3},{8,12},{9,13},{10,... | collective-permute-start | bytes 196616 | tf_op jit(solution)/shard_map/ppermute | solution.py:34
  44.8 5.6 %collective-permute-start.17 = (f32[2,32,256]{2,1,0:T(8,128)S(1)}, f32[2,32,256]{2,1,0:T(8,128)S(1)}, u32[]{:S(2)}, u32[]{:S(2)}) collective-permute-start(f32[2,32,256]{2,1,0:T(8,128)S(1)} %add.104), channel_id=1, source_target_pairs={{0,24},{1,25},{2,26},{3,27},{4,28},{5,29},{6,30},{7,31},{8,16},{9,... | collective-permute-start | bytes 196616 | tf_op jit(solution)/shard_map/ppermute | solution.py:34
  46.3 5.2 %collective-permute-start.16 = (f32[2,32,256]{2,1,0:T(8,128)S(1)}, f32[2,32,256]{2,1,0:T(8,128)S(1)}, u32[]{:S(2)}, u32[]{:S(2)}) collective-permute-start(f32[2,32,256]{2,1,0:T(8,128)S(1)} %add.104), channel_id=1, source_target_pairs={{0,16},{1,17},{2,18},{3,19},{4,20},{5,21},{6,22},{7,23},{8,24},{9,... | collective-permute-start | bytes 196616 | tf_op jit(solution)/shard_map/ppermute | solution.py:34
  47.1 4.5 %collective-permute-start.15 = (f32[2,32,256]{2,1,0:T(8,128)S(1)}, f32[2,32,256]{2,1,0:T(8,128)S(1)}, u32[]{:S(2)}, u32[]{:S(2)}) collective-permute-start(f32[2,32,256]{2,1,0:T(8,128)S(1)} %add.104), channel_id=1, source_target_pairs={{0,8},{1,9},{2,10},{3,11},{4,12},{5,13},{6,14},{7,15},{8,0},{9,1},... | collective-permute-start | bytes 196616 | tf_op jit(solution)/shard_map/ppermute | solution.py:34

commit v7 on v6

--- a/solution.py
+++ b/solution.py
@@ -320,9 +320,15 @@
         right = right + exchange(right, lambda o, h, t, b=b: (o, h ^ (1 << b), t))
     early = rank // 4
     right, inverse = after(right, invert(range(early), *grams))
+    right = right.astype(BF16)
     parts = [right] + [exchange(right, lambda o, h, t, k=k: (o ^ k, h, t)) for k in range(1, outer)]
     inverse = invert(range(early, rank), inverse)
-    return tree_sum(parts), inverse
+    return tree_sum([part.astype(F32) for part in parts]), inverse
+
+
+def turned(k):
+    n = bits(lax.axis_size("outer"))
+    return sum(((k >> b) & 1) << (n - 1 - b) for b in range(n))
 
 
 def after(value, *others):
@@ -338,14 +344,14 @@
     gradient, error_acc = in_hbm(gradient.reshape(shape)), in_hbm(error_acc.reshape(shape))
     q_turned = in_hbm(jnp.swapaxes(q_start, 1, 2))
     o, h = lax.axis_index("outer"), lax.axis_index("hst")
-    near = [(h & 1) * outer + (o ^ k) for k in range(outer)]
-    far = [(1 - (h & 1)) * outer + (o ^ k) for k in range(outer)]
+    near = [(h & 1) * outer + (o ^ jnp.where(h & 1 == 1, turned(k), k)) for k in range(outer)]
+    far = [(1 - (h & 1)) * outer + (o ^ jnp.where(h & 1 == 1, k, turned(k))) for k in range(outer)]
 
     def core(x):
         return exchange(x, lambda o, h, t: (o, h ^ 1, t))
 
     def chip(x, k):
-        return exchange(x, lambda o, h, t: (o ^ k, h, t))
+        return exchange(x, lambda o, h, t: (o ^ (turned(k) if h % 2 else k), h, t))
 
     def after_all(value, places):
         value, *places = after(value, *places)

time: 56 us -> 56.2 us (level)
  waiting for transfers between devices: 10.7 us -> 11.4 us
    ppermute x18, waiting for transfers between devices: 10.7 us -> 11.4 us  [exchange(): return lax.ppermute(x, AXES, pairs)]
  transfers between devices with their start and end apart: 18 -> 18, of which waited for: 9 -> 8; matrix products, arithmetic and copies ran while one was open for 1% -> 1% of each run, Pallas kernels for 28% -> 27%
where the time goes in v7:
time: 56.2 us; the launch traced here: 56 us
  Pallas kernels  26.1 us (46%)
  starting transfers between devices  17.4 us (31%)
  waiting for transfers between devices  11.4 us (20%)
    ppermute x18, starting transfers between devices, exchange(): return lax.ppermute(x, AXES, pairs)  17.4 us
    ppermute x18, waiting for transfers between devices, exchange(): return lax.ppermute(x, AXES, pairs)  11.4 us
    pallas_call x2, Pallas kernels, mix(): pl.pallas_call(mix_kernel, in_specs=[scalar()] + [hbm] * 3, out_specs=[wh...  9.15 us
    pallas_call x3, Pallas kernels, keep(): pl.pallas_call(keep_kernel, in_specs=[scalar()] + [pl.BlockSpec(memory_sp...  8.1 us
    pallas_call x1, Pallas kernels, expand(): pl.pallas_call(lambda *refs: expand_kernel(scale, *refs), in_specs=[whole...  4.05 us
    pallas_call x2, Pallas kernels, invert(): pl.pallas_call(lambda *refs: invert_kernel(steps, *refs), in_specs=[whole...  2.68 us
    pallas_call x3, Pallas kernels, project(): pl.pallas_call(lambda *refs: project_kernel(chunks, *refs), in_specs=[who...  2.08 us
  transfers between devices with their start and end apart: 18, of which 8 were waited for; matrix products, arithmetic and copies ran while one was open for 1% of the time, Pallas kernels for 27%

profile of v7, /device:TPU:0, one launch (start us, length us, event | category | flops | bytes accessed | tf_op | source)
XLA Modules:
  0.0 56.0 jit_solution(14575041842101540082)
XLA Ops:
  0.1 5.9 %mix.2 = (bf16[768,256]{1,0:T(8,128)(2,1)S(1)}, f32[768,256]{1,0:T(8,128)S(1)}) custom-call(s32[6]{0:T(128)S(1)} %stack.60.place_ref, f32[2,32,256]{2,1,0:T(8,128)} %bitcast.28, bf16[2,4,2048,256]{3,2,1,0:T(8,128)(2,1)} %bitcast.18, bf16[2,4,2048,256]{3,2,1,0:T(8,128)(2,1)} %bitcast.23), custom_call_target="tpu_custom_call" | custom-call | flops 1000000 | tf_op jit(solution)/shard_map/mix/pallas_call | solution.py:128
  6.0 0.5 collective-permute-start
  6.5 1.3 %collective-permute-done = bf16[768,256]{1,0:T(8,128)(2,1)S(1)} collective-permute-done((bf16[768,256]{1,0:T(8,128)(2,1)S(1)}, bf16[768,256]{1,0:T(8,128)(2,1)S(1)}, u32[]{:S(2)}, u32[]{:S(2)}) %collective-permute-start) | collective-permute-done | bytes 393248 | tf_op jit(solution)/shard_map/ppermute | solution.py:34
  7.9 0.1 add_convert_fusion
  8.0 2.9 %collective-permute-start.2 = (bf16[256,256]{1,0:T(8,128)(2,1)S(1)}, bf16[256,256]{1,0:T(8,128)(2,1)S(1)}, u32[]{:S(2)}, u32[]{:S(2)}) collective-permute-start(bf16[256,256]{1,0:T(8,128)(2,1)S(1)} %get-tuple-element.69), channel_id=1, source_target_pairs={{0,8},{1,9},{2,10},{3,11},{4,20},{5,21},{6,22},{7,23},{8,0},{9,1},... | collective-permute-start | bytes 393224 | tf_op jit(solution)/shard_map/ppermute | solution.py:34
  11.0 1.5 %collective-permute-start.4 = (bf16[256,256]{1,0:T(8,128)(2,1)S(1)}, bf16[256,256]{1,0:T(8,128)(2,1)S(1)}, u32[]{:S(2)}, u32[]{:S(2)}) collective-permute-start(bf16[256,256]{1,0:T(8,128)(2,1)S(1)} %get-tuple-element.70), channel_id=1, source_target_pairs={{0,24},{1,25},{2,26},{3,27},{4,28},{5,29},{6,30},{7,31},{8,16},{9,... | collective-permute-start | bytes 393224 | tf_op jit(solution)/shard_map/ppermute | solution.py:34
  12.6 3.2 %mix.3 = (bf16[256,256]{1,0:T(8,128)(2,1)S(1)}, f32[256,256]{1,0:T(8,128)S(1)}, bf16[2,4,512,256]{3,2,1,0:T(8,128)(2,1)S(1)}) custom-call(s32[2]{0:T(128)S(1)} %pad_add_fusion.place_ref, f32[2,32,256]{2,1,0:T(8,128)} %bitcast.29, bf16[2,4,2048,256]{3,2,1,0:T(8,128)(2,1)} %bitcast.19, bf16[2,4,2048,256]{3,2,1,0:T(8,128)(2,1)} %bitcast.24), custom_call_target="tpu_custom_call" | custom-call | flops 1000000 | tf_op jit(solution)/shard_map/mix/pallas_call | solution.py:128
  15.9 3.4 %collective-permute-done.4 = bf16[256,256]{1,0:T(8,128)(2,1)S(1)} collective-permute-done((bf16[256,256]{1,0:T(8,128)(2,1)S(1)}, bf16[256,256]{1,0:T(8,128)(2,1)S(1)}, u32[]{:S(2)}, u32[]{:S(2)}) %collective-permute-start.4) | collective-permute-done | bytes 131104 | tf_op jit(solution)/shard_map/ppermute | solution.py:34
  19.4 1.6 %collective-permute-start.5 = (bf16[256,256]{1,0:T(8,128)(2,1)S(1)}, bf16[256,256]{1,0:T(8,128)(2,1)S(1)}, u32[]{:S(2)}, u32[]{:S(2)}) collective-permute-start(bf16[256,256]{1,0:T(8,128)(2,1)S(1)} %add_convert_fusion.3), channel_id=1, source_target_pairs={{0,1},{1,0},{2,3},{3,2},{4,6},{5,7},{6,4},{7,5},{8,9},{9,8},{10,11... | collective-permute-start | bytes 393224 | tf_op jit(solution)/shard_map/ppermute | solution.py:34
  21.2 2.9 %keep.3.refs_3_ = bf16[2,4,512,256]{3,2,1,0:T(8,128)(2,1)S(1)} custom-call(s32[2]{0:T(128)S(1)} %pad_add_fusion.1.place_ref, bf16[2,4,2048,256]{3,2,1,0:T(8,128)(2,1)} %bitcast.20, bf16[2,4,2048,256]{3,2,1,0:T(8,128)(2,1)} %bitcast.25), custom_call_target="tpu_custom_call" | custom-call | flops 1000000 | tf_op jit(solution)/shard_map/keep/pallas_call | solution.py:162
  24.0 0.9 %collective-permute-done.5 = bf16[256,256]{1,0:T(8,128)(2,1)S(1)} collective-permute-done((bf16[256,256]{1,0:T(8,128)(2,1)S(1)}, bf16[256,256]{1,0:T(8,128)(2,1)S(1)}, u32[]{:S(2)}, u32[]{:S(2)}) %collective-permute-start.5) | collective-permute-done | bytes 131104 | tf_op jit(solution)/shard_map/ppermute | solution.py:34
  25.0 2.6 %collective-permute-start.6 = (bf16[256,256]{1,0:T(8,128)(2,1)S(1)}, bf16[256,256]{1,0:T(8,128)(2,1)S(1)}, u32[]{:S(2)}, u32[]{:S(2)}) collective-permute-start(bf16[256,256]{1,0:T(8,128)(2,1)S(1)} %add_convert_fusion.2), channel_id=1, source_target_pairs={{0,2},{1,3},{2,0},{3,1},{4,5},{5,4},{6,7},{7,6},{8,10},{9,11},{10,... | collective-permute-start | bytes 393224 | tf_op jit(solution)/shard_map/ppermute | solution.py:34
  27.6 1.7 %keep.4.refs_4_ = bf16[2,4,256,256]{3,2,1,0:T(8,128)(2,1)S(1)} custom-call(s32[1]{0:T(128)} %bitcast.13.place_ref, bf16[2,4,2048,256]{3,2,1,0:T(8,128)(2,1)} %bitcast.21, bf16[2,4,2048,256]{3,2,1,0:T(8,128)(2,1)} %bitcast.26), custom_call_target="tpu_custom_call" | custom-call | flops 1000000 | tf_op jit(solution)/shard_map/keep/pallas_call | solution.py:162
  29.2 1.7 %collective-permute-done.6 = bf16[256,256]{1,0:T(8,128)(2,1)S(1)} collective-permute-done((bf16[256,256]{1,0:T(8,128)(2,1)S(1)}, bf16[256,256]{1,0:T(8,128)(2,1)S(1)}, u32[]{:S(2)}, u32[]{:S(2)}) %collective-permute-start.6) | collective-permute-done | bytes 131104 | tf_op jit(solution)/shard_map/ppermute | solution.py:34
  31.0 2.9 %collective-permute-start.9 = (bf16[256,256]{1,0:T(8,128)(2,1)S(1)}, bf16[256,256]{1,0:T(8,128)(2,1)S(1)}, u32[]{:S(2)}, u32[]{:S(2)}) collective-permute-start(bf16[256,256]{1,0:T(8,128)(2,1)S(1)} %add_convert_fusion.1.refs_0_), channel_id=1, source_target_pairs={{0,24},{1,25},{2,26},{3,27},{4,28},{5,29},{6,30},{7,31},{8,16},{9,... | collective-permute-start | bytes 393224 | tf_op jit(solution)/shard_map/ppermute | solution.py:34
  34.0 0.5 collective-permute-start.7
  34.6 3.6 %keep.5.refs_3_ = bf16[2,4,768,256]{3,2,1,0:T(8,128)(2,1)S(1)} custom-call(s32[3]{0:T(128)S(1)} %pad_add_fusion.2.place_ref, bf16[2,4,2048,256]{3,2,1,0:T(8,128)(2,1)} %bitcast.22, bf16[2,4,2048,256]{3,2,1,0:T(8,128)(2,1)} %bitcast.27), custom_call_target="tpu_custom_call" | custom-call | flops 1000000 | tf_op jit(solution)/shard_map/keep/pallas_call | solution.py:162
  38.4 0.5 project.3
  39.0 1.8 %collective-permute-done.8.refs_1_ = bf16[256,256]{1,0:T(8,128)(2,1)S(1)} collective-permute-done((bf16[256,256]{1,0:T(8,128)(2,1)S(1)}, bf16[256,256]{1,0:T(8,128)(2,1)S(1)}, u32[]{:S(2)}, u32[]{:S(2)}) %collective-permute-start.8) | collective-permute-done | bytes 131104 | tf_op jit(solution)/shard_map/ppermute | solution.py:34
  40.8 0.5 collective-permute-start.11
  41.4 0.8 %project.4 = (f32[2,32,256]{2,1,0:T(8,128)S(1)}, f32[3,2,32,32]{3,2,1,0:T(8,128)S(1)}) custom-call(bf16[256,256]{1,0:T(8,128)(2,1)S(1)} %collective-permute-done.7.refs_0_, bf16[256,256]{1,0:T(8,128)(2,1)S(1)} %collective-permute-done.8.refs_1_, bf16[256,256]{1,0:T(8,128)(2,1)S(1)} %collective-permute-done.9.refs_2_, ...), custom_call_target="tpu_custom_call" | custom-call | flops 1000000 | tf_op jit(solution)/shard_map/project/pallas_call | solution.py:204
  42.2 0.1 collective-permute-done.11.refs_0_
  42.4 0.8 %project.5 = (f32[2,32,256]{2,1,0:T(8,128)S(1)}, f32[3,2,32,32]{3,2,1,0:T(8,128)S(1)}) custom-call(bf16[256,256]{1,0:T(8,128)(2,1)S(1)} %collective-permute-done.11.refs_0_, bf16[256,256]{1,0:T(8,128)(2,1)S(1)} %collective-permute-done.12.refs_1_, bf16[256,256]{1,0:T(8,128)(2,1)S(1)} %collective-permute-done.13.refs_2_, ...), custom_call_target="tpu_custom_call" | custom-call | flops 1000000 | tf_op jit(solution)/shard_map/project/pallas_call | solution.py:204
  43.1 0.4 collective-permute-start.14
  43.5 0.7 %invert.2.refs_0_ = f32[2,32,32]{2,1,0:T(8,128)S(1)} custom-call(f32[2,2,32,32]{3,2,1,0:T(8,128)S(1)} %get-tuple-element.64.refs_0_, f32[3,2,32,32]{3,2,1,0:T(8,128)S(1)} %get-tuple-element.65.refs_1_, f32[3,2,32,32]{3,2,1,0:T(8,128)S(1)} %get-tuple-element.66.refs_2_), custom_call_target="tpu_custom_call" | custom-call | flops 1000000 | tf_op jit(solution)/shard_map/invert/pallas_call | solution.py:243
  44.2 0.2 collective-permute-done.14
  44.5 0.7 %collective-permute-start.16 = (bf16[2,32,256]{2,1,0:T(8,128)(2,1)S(1)}, bf16[2,32,256]{2,1,0:T(8,128)(2,1)S(1)}, u32[]{:S(2)}, u32[]{:S(2)}) collective-permute-start(bf16[2,32,256]{2,1,0:T(8,128)(2,1)S(1)} %add.104), channel_id=1, source_target_pairs={{0,16},{1,17},{2,18},{3,19},{4,20},{5,21},{6,22},{7,23},{8,24},{9,... | collective-permute-start | bytes 98312 | tf_op jit(solution)/shard_map/ppermute | solution.py:34
  45.2 1.9 %collective-permute-start.15 = (bf16[2,32,256]{2,1,0:T(8,128)(2,1)S(1)}, bf16[2,32,256]{2,1,0:T(8,128)(2,1)S(1)}, u32[]{:S(2)}, u32[]{:S(2)}) collective-permute-start(bf16[2,32,256]{2,1,0:T(8,128)(2,1)S(1)} %add.104), channel_id=1, source_target_pairs={{0,8},{1,9},{2,10},{3,11},{4,12},{5,13},{6,14},{7,15},{8,0},{9,1},... | collective-permute-start | bytes 98312 | tf_op jit(solution)/shard_map/ppermute | solution.py:34
  47.1 0.9 %collective-permute-start.17 = (bf16[2,32,256]{2,1,0:T(8,128)(2,1)S(1)}, bf16[2,32,256]{2,1,0:T(8,128)(2,1)S(1)}, u32[]{:S(2)}, u32[]{:S(2)}) collective-permute-start(bf16[2,32,256]{2,1,0:T(8,128)(2,1)S(1)} %add.104), channel_id=1, source_target_pairs={{0,24},{1,25},{2,26},{3,27},{4,28},{5,29},{6,30},{7,31},{8,16},{9,... | collective-permute-start | bytes 98312 | tf_op jit(solution)/shard_map/ppermute | solution.py:34
  48.0 2.0 %invert.3.refs_1_ = f32[2,32,32]{2,1,0:T(8,128)S(1)} custom-call(f32[2,32,32]{2,1,0:T(8,128)S(1)} %invert.2.refs_0_), custom_call_target="tpu_custom_call" | custom-call | flops 1000000 | tf_op jit(solution)/shard_map/invert/pallas_call | solution.py:243
  50.1 1.9 %collective-permute-done.17 = bf16[2,32,256]{2,1,0:T(8,128)(2,1)S(1)} collective-permute-done((bf16[2,32,256]{2,1,0:T(8,128)(2,1)S(1)}, bf16[2,32,256]{2,1,0:T(8,128)(2,1)S(1)}, u32[]{:S(2)}, u32[]{:S(2)}) %collective-permute-start.17) | collective-permute-done | bytes 32800 | tf_op jit(solution)/shard_map/ppermute | solution.py:34
  51.9 4.1 %expand.1 = bf16[2,4,2048,256]{3,2,1,0:T(8,128)(2,1)} custom-call(bf16[2048,256]{1,0:T(8,128)(2,1)S(1)} %constant_dynamic-update-slice_fusion.refs_0_, f32[2,32,32]{2,1,0:T(8,128)S(1)} %invert.3.refs_1_, f32[2,32,256]{2,1,0:T(8,128)S(1)} %add_add_fusion.refs_2_), custom_call_target="tpu_custom_call" | custom-call | tf_op jit(solution)/shard_map/expand/pallas_call | solution.py:300
  (39 shorter events, 1.1 us)
Async XLA Ops:
  6.0 1.9 %collective-permute-start = (bf16[768,256]{1,0:T(8,128)(2,1)S(1)}, bf16[768,256]{1,0:T(8,128)(2,1)S(1)}, u32[]{:S(2)}, u32[]{:S(2)}) collective-permute-start(bf16[768,256]{1,0:T(8,128)(2,1)S(1)} %get-tuple-element.38), channel_id=1, source_target_pairs={{0,4},{1,5},{2,6},{3,7},{4,0},{5,1},{6,2},{7,3},{8,12},{9,13},{10,... | collective-permute-start | bytes 1179656 | tf_op jit(solution)/shard_map/ppermute | solution.py:34
  8.0 7.9 %collective-permute-start.2 = (bf16[256,256]{1,0:T(8,128)(2,1)S(1)}, bf16[256,256]{1,0:T(8,128)(2,1)S(1)}, u32[]{:S(2)}, u32[]{:S(2)}) collective-permute-start(bf16[256,256]{1,0:T(8,128)(2,1)S(1)} %get-tuple-element.69), channel_id=1, source_target_pairs={{0,8},{1,9},{2,10},{3,11},{4,20},{5,21},{6,22},{7,23},{8,0},{9,1},... | collective-permute-start | bytes 393224 | tf_op jit(solution)/shard_map/ppermute | solution.py:34
  11.0 8.4 %collective-permute-start.4 = (bf16[256,256]{1,0:T(8,128)(2,1)S(1)}, bf16[256,256]{1,0:T(8,128)(2,1)S(1)}, u32[]{:S(2)}, u32[]{:S(2)}) collective-permute-start(bf16[256,256]{1,0:T(8,128)(2,1)S(1)} %get-tuple-element.70), channel_id=1, source_target_pairs={{0,24},{1,25},{2,26},{3,27},{4,28},{5,29},{6,30},{7,31},{8,16},{9,... | collective-permute-start | bytes 393224 | tf_op jit(solution)/shard_map/ppermute | solution.py:34
  12.5 6.9 %collective-permute-start.3 = (bf16[256,256]{1,0:T(8,128)(2,1)S(1)}, bf16[256,256]{1,0:T(8,128)(2,1)S(1)}, u32[]{:S(2)}, u32[]{:S(2)}) collective-permute-start(bf16[256,256]{1,0:T(8,128)(2,1)S(1)} %get-tuple-element.71), channel_id=1, source_target_pairs={{0,16},{1,17},{2,18},{3,19},{4,12},{5,13},{6,14},{7,15},{8,24},{9,... | collective-permute-start | bytes 393224 | tf_op jit(solution)/shard_map/ppermute | solution.py:34
  15.8 8.2 %copy-start = (bf16[2,4,512,256]{3,2,1,0:T(8,128)(2,1)}, bf16[2,4,512,256]{3,2,1,0:T(8,128)(2,1)S(1)}, u32[]{:S(2)}) copy-start(bf16[2,4,512,256]{3,2,1,0:T(8,128)(2,1)S(1)} %get-tuple-element.52.refs_2_) | copy-start | bytes 6291460
  15.8 3.5 %collective-permute-start.1 = (bf16[256,256]{1,0:T(8,128)(2,1)S(1)}, bf16[256,256]{1,0:T(8,128)(2,1)S(1)}, u32[]{:S(2)}, u32[]{:S(2)}) collective-permute-start(bf16[256,256]{1,0:T(8,128)(2,1)S(1)} %get-tuple-element.42), channel_id=1, source_target_pairs={{0,4},{1,5},{2,6},{3,7},{4,0},{5,1},{6,2},{7,3},{8,12},{9,13},{10,... | collective-permute-start | bytes 393224 | tf_op jit(solution)/shard_map/ppermute | solution.py:34
  19.4 5.5 %collective-permute-start.5 = (bf16[256,256]{1,0:T(8,128)(2,1)S(1)}, bf16[256,256]{1,0:T(8,128)(2,1)S(1)}, u32[]{:S(2)}, u32[]{:S(2)}) collective-permute-start(bf16[256,256]{1,0:T(8,128)(2,1)S(1)} %add_convert_fusion.3), channel_id=1, source_target_pairs={{0,1},{1,0},{2,3},{3,2},{4,6},{5,7},{6,4},{7,5},{8,9},{9,8},{10,11... | collective-permute-start | bytes 393224 | tf_op jit(solution)/shard_map/ppermute | solution.py:34
  25.0 5.9 %collective-permute-start.6 = (bf16[256,256]{1,0:T(8,128)(2,1)S(1)}, bf16[256,256]{1,0:T(8,128)(2,1)S(1)}, u32[]{:S(2)}, u32[]{:S(2)}) collective-permute-start(bf16[256,256]{1,0:T(8,128)(2,1)S(1)} %add_convert_fusion.2), channel_id=1, source_target_pairs={{0,2},{1,3},{2,0},{3,1},{4,5},{5,4},{6,7},{7,6},{8,10},{9,11},{10,... | collective-permute-start | bytes 393224 | tf_op jit(solution)/shard_map/ppermute | solution.py:34
  30.9 7.4 %collective-permute-start.10 = (bf16[256,256]{1,0:T(8,128)(2,1)S(1)}, bf16[256,256]{1,0:T(8,128)(2,1)S(1)}, u32[]{:S(2)}, u32[]{:S(2)}) collective-permute-start(bf16[256,256]{1,0:T(8,128)(2,1)S(1)} %add_convert_fusion.1.refs_0_), channel_id=1, source_target_pairs={{0,4},{1,5},{2,6},{3,7},{4,0},{5,1},{6,2},{7,3},{8,12},{9,13},{10,... | collective-permute-start | bytes 393224 | tf_op jit(solution)/shard_map/ppermute | solution.py:34
  31.0 7.9 %collective-permute-start.9 = (bf16[256,256]{1,0:T(8,128)(2,1)S(1)}, bf16[256,256]{1,0:T(8,128)(2,1)S(1)}, u32[]{:S(2)}, u32[]{:S(2)}) collective-permute-start(bf16[256,256]{1,0:T(8,128)(2,1)S(1)} %add_convert_fusion.1.refs_0_), channel_id=1, source_target_pairs={{0,24},{1,25},{2,26},{3,27},{4,28},{5,29},{6,30},{7,31},{8,16},{9,... | collective-permute-start | bytes 393224 | tf_op jit(solution)/shard_map/ppermute | solution.py:34
  33.9 6.9 %collective-permute-start.8 = (bf16[256,256]{1,0:T(8,128)(2,1)S(1)}, bf16[256,256]{1,0:T(8,128)(2,1)S(1)}, u32[]{:S(2)}, u32[]{:S(2)}) collective-permute-start(bf16[256,256]{1,0:T(8,128)(2,1)S(1)} %add_convert_fusion.1.refs_0_), channel_id=1, source_target_pairs={{0,16},{1,17},{2,18},{3,19},{4,12},{5,13},{6,14},{7,15},{8,24},{9,... | collective-permute-start | bytes 393224 | tf_op jit(solution)/shard_map/ppermute | solution.py:34
  34.0 6.8 %collective-permute-start.7 = (bf16[256,256]{1,0:T(8,128)(2,1)S(1)}, bf16[256,256]{1,0:T(8,128)(2,1)S(1)}, u32[]{:S(2)}, u32[]{:S(2)}) collective-permute-start(bf16[256,256]{1,0:T(8,128)(2,1)S(1)} %add_convert_fusion.1.refs_0_), channel_id=1, source_target_pairs={{0,8},{1,9},{2,10},{3,11},{4,20},{5,21},{6,22},{7,23},{8,0},{9,1},... | collective-permute-start | bytes 393224 | tf_op jit(solution)/shard_map/ppermute | solution.py:34
  34.6 3.7 %copy-start.1 = (bf16[2,4,512,256]{3,2,1,0:T(8,128)(2,1)S(1)}, bf16[2,4,512,256]{3,2,1,0:T(8,128)(2,1)}, u32[]{:S(2)}) copy-start(bf16[2,4,512,256]{3,2,1,0:T(8,128)(2,1)} %copy-done) | copy-start | bytes 6291460
  38.9 3.5 %collective-permute-start.13 = (bf16[256,256]{1,0:T(8,128)(2,1)S(1)}, bf16[256,256]{1,0:T(8,128)(2,1)S(1)}, u32[]{:S(2)}, u32[]{:S(2)}) collective-permute-start(bf16[256,256]{1,0:T(8,128)(2,1)S(1)} %collective-permute-done.9.refs_2_), channel_id=1, source_target_pairs={{0,4},{1,5},{2,6},{3,7},{4,0},{5,1},{6,2},{7,3},{8,12},{9,13},{10,... | collective-permute-start | bytes 393224 | tf_op jit(solution)/shard_map/ppermute | solution.py:34
  40.8 1.4 %collective-permute-start.12 = (bf16[256,256]{1,0:T(8,128)(2,1)S(1)}, bf16[256,256]{1,0:T(8,128)(2,1)S(1)}, u32[]{:S(2)}, u32[]{:S(2)}) collective-permute-start(bf16[256,256]{1,0:T(8,128)(2,1)S(1)} %collective-permute-done.8.refs_1_), channel_id=1, source_target_pairs={{0,4},{1,5},{2,6},{3,7},{4,0},{5,1},{6,2},{7,3},{8,12},{9,13},{10,... | collective-permute-start | bytes 393224 | tf_op jit(solution)/shard_map/ppermute | solution.py:34
  40.8 1.5 %collective-permute-start.11 = (bf16[256,256]{1,0:T(8,128)(2,1)S(1)}, bf16[256,256]{1,0:T(8,128)(2,1)S(1)}, u32[]{:S(2)}, u32[]{:S(2)}) collective-permute-start(bf16[256,256]{1,0:T(8,128)(2,1)S(1)} %collective-permute-done.7.refs_0_), channel_id=1, source_target_pairs={{0,4},{1,5},{2,6},{3,7},{4,0},{5,1},{6,2},{7,3},{8,12},{9,13},{10,... | collective-permute-start | bytes 393224 | tf_op jit(solution)/shard_map/ppermute | solution.py:34
  43.1 1.3 %collective-permute-start.14 = (f32[2,32,256]{2,1,0:T(8,128)S(1)}, f32[2,32,256]{2,1,0:T(8,128)S(1)}, u32[]{:S(2)}, u32[]{:S(2)}) collective-permute-start(f32[2,32,256]{2,1,0:T(8,128)S(1)} %get-tuple-element.63), channel_id=1, source_target_pairs={{0,4},{1,5},{2,6},{3,7},{4,0},{5,1},{6,2},{7,3},{8,12},{9,13},{10,... | collective-permute-start | bytes 196616 | tf_op jit(solution)/shard_map/ppermute | solution.py:34
  44.5 5.6 %collective-permute-start.16 = (bf16[2,32,256]{2,1,0:T(8,128)(2,1)S(1)}, bf16[2,32,256]{2,1,0:T(8,128)(2,1)S(1)}, u32[]{:S(2)}, u32[]{:S(2)}) collective-permute-start(bf16[2,32,256]{2,1,0:T(8,128)(2,1)S(1)} %add.104), channel_id=1, source_target_pairs={{0,16},{1,17},{2,18},{3,19},{4,20},{5,21},{6,22},{7,23},{8,24},{9,... | collective-permute-start | bytes 98312 | tf_op jit(solution)/shard_map/ppermute | solution.py:34
  45.2 4.9 %collective-permute-start.15 = (bf16[2,32,256]{2,1,0:T(8,128)(2,1)S(1)}, bf16[2,32,256]{2,1,0:T(8,128)(2,1)S(1)}, u32[]{:S(2)}, u32[]{:S(2)}) collective-permute-start(bf16[2,32,256]{2,1,0:T(8,128)(2,1)S(1)} %add.104), channel_id=1, source_target_pairs={{0,8},{1,9},{2,10},{3,11},{4,12},{5,13},{6,14},{7,15},{8,0},{9,1},... | collective-permute-start | bytes 98312 | tf_op jit(solution)/shard_map/ppermute | solution.py:34
  47.1 4.8 %collective-permute-start.17 = (bf16[2,32,256]{2,1,0:T(8,128)(2,1)S(1)}, bf16[2,32,256]{2,1,0:T(8,128)(2,1)S(1)}, u32[]{:S(2)}, u32[]{:S(2)}) collective-permute-start(bf16[2,32,256]{2,1,0:T(8,128)(2,1)S(1)} %add.104), channel_id=1, source_target_pairs={{0,24},{1,25},{2,26},{3,27},{4,28},{5,29},{6,30},{7,31},{8,16},{9,... | collective-permute-start | bytes 98312 | tf_op jit(solution)/shard_map/ppermute | solution.py:34

commit v8 on v6

--- a/solution.py
+++ b/solution.py
@@ -364,7 +364,7 @@
         sent = pick(left, 1 - bit).astype(BF16)
         left = pick(left, bit) + exchange(sent, lambda o, h, t, b=b: (o, h ^ (1 << b), t)).astype(F32)
     others = near[1:] + far[1:]
-    early, late = len(others) // 3, len(others) // 2
+    early, late = len(others) // 6, len(others) // 2
     waiting, mixed = [others[:early], others[early:late]], []
     for b in range(bits(tp)):
         sent = left.astype(BF16)

time: 56 us -> 56 us (level)
  transfers between devices with their start and end apart: 18 -> 18, of which waited for: 9 -> 9; matrix products, arithmetic and copies ran while one was open for 1% -> 1% of each run, Pallas kernels for 28% -> 27%
where the time goes in v8:
time: 56 us; the launch traced here: 55.6 us
  Pallas kernels  26 us (46%)
  starting transfers between devices  17.7 us (32%)
  waiting for transfers between devices  10.9 us (19%)
    ppermute x18, starting transfers between devices, exchange(): return lax.ppermute(x, AXES, pairs)  17.7 us
    ppermute x18, waiting for transfers between devices, exchange(): return lax.ppermute(x, AXES, pairs)  10.9 us
    pallas_call x2, Pallas kernels, mix(): pl.pallas_call(mix_kernel, in_specs=[scalar()] + [hbm] * 3, out_specs=[wh...  9.15 us
    pallas_call x3, Pallas kernels, keep(): pl.pallas_call(keep_kernel, in_specs=[scalar()] + [pl.BlockSpec(memory_sp...  8.02 us
    pallas_call x1, Pallas kernels, expand(): pl.pallas_call(lambda *refs: expand_kernel(scale, *refs), in_specs=[whole...  4.06 us
    pallas_call x2, Pallas kernels, invert(): pl.pallas_call(lambda *refs: invert_kernel(steps, *refs), in_specs=[whole...  2.68 us
    pallas_call x3, Pallas kernels, project(): pl.pallas_call(lambda *refs: project_kernel(chunks, *refs), in_specs=[who...  2.07 us
  transfers between devices with their start and end apart: 18, of which 9 were waited for; matrix products, arithmetic and copies ran while one was open for 1% of the time, Pallas kernels for 27%

profile of v8, /device:TPU:0, one launch (start us, length us, event | category | flops | bytes accessed | tf_op | source)
XLA Modules:
  0.0 55.6 jit_solution(5293004866715694153)
XLA Ops:
  0.1 5.9 %mix.2 = (bf16[768,256]{1,0:T(8,128)(2,1)S(1)}, f32[768,256]{1,0:T(8,128)S(1)}) custom-call(s32[6]{0:T(128)S(1)} %stack.60.place_ref, f32[2,32,256]{2,1,0:T(8,128)} %bitcast.28, bf16[2,4,2048,256]{3,2,1,0:T(8,128)(2,1)} %bitcast.18, bf16[2,4,2048,256]{3,2,1,0:T(8,128)(2,1)} %bitcast.23), custom_call_target="tpu_custom_call" | custom-call | flops 1000000 | tf_op jit(solution)/shard_map/mix/pallas_call | solution.py:128
  6.0 0.5 collective-permute-start
  6.5 1.3 %collective-permute-done = bf16[768,256]{1,0:T(8,128)(2,1)S(1)} collective-permute-done((bf16[768,256]{1,0:T(8,128)(2,1)S(1)}, bf16[768,256]{1,0:T(8,128)(2,1)S(1)}, u32[]{:S(2)}, u32[]{:S(2)}) %collective-permute-start) | collective-permute-done | bytes 393248 | tf_op jit(solution)/shard_map/ppermute | solution.py:34
  8.0 2.9 %collective-permute-start.2 = (bf16[256,256]{1,0:T(8,128)(2,1)S(1)}, bf16[256,256]{1,0:T(8,128)(2,1)S(1)}, u32[]{:S(2)}, u32[]{:S(2)}) collective-permute-start(bf16[256,256]{1,0:T(8,128)(2,1)S(1)} %get-tuple-element.69), channel_id=1, source_target_pairs={{0,8},{1,9},{2,10},{3,11},{4,12},{5,13},{6,14},{7,15},{8,0},{9,1},... | collective-permute-start | bytes 393224 | tf_op jit(solution)/shard_map/ppermute | solution.py:34
  11.0 1.5 %collective-permute-start.4 = (bf16[256,256]{1,0:T(8,128)(2,1)S(1)}, bf16[256,256]{1,0:T(8,128)(2,1)S(1)}, u32[]{:S(2)}, u32[]{:S(2)}) collective-permute-start(bf16[256,256]{1,0:T(8,128)(2,1)S(1)} %get-tuple-element.70), channel_id=1, source_target_pairs={{0,24},{1,25},{2,26},{3,27},{4,28},{5,29},{6,30},{7,31},{8,16},{9,... | collective-permute-start | bytes 393224 | tf_op jit(solution)/shard_map/ppermute | solution.py:34
  12.6 3.2 %mix.3 = (bf16[256,256]{1,0:T(8,128)(2,1)S(1)}, f32[256,256]{1,0:T(8,128)S(1)}, bf16[2,4,512,256]{3,2,1,0:T(8,128)(2,1)S(1)}) custom-call(s32[2]{0:T(128)S(1)} %pad_add_fusion.place_ref, f32[2,32,256]{2,1,0:T(8,128)} %bitcast.29, bf16[2,4,2048,256]{3,2,1,0:T(8,128)(2,1)} %bitcast.19, bf16[2,4,2048,256]{3,2,1,0:T(8,128)(2,1)} %bitcast.24), custom_call_target="tpu_custom_call" | custom-call | flops 1000000 | tf_op jit(solution)/shard_map/mix/pallas_call | solution.py:128
  15.9 3.0 %collective-permute-done.4 = bf16[256,256]{1,0:T(8,128)(2,1)S(1)} collective-permute-done((bf16[256,256]{1,0:T(8,128)(2,1)S(1)}, bf16[256,256]{1,0:T(8,128)(2,1)S(1)}, u32[]{:S(2)}, u32[]{:S(2)}) %collective-permute-start.4) | collective-permute-done | bytes 131104 | tf_op jit(solution)/shard_map/ppermute | solution.py:34
  18.9 1.4 %collective-permute-done.3 = bf16[256,256]{1,0:T(8,128)(2,1)S(1)} collective-permute-done((bf16[256,256]{1,0:T(8,128)(2,1)S(1)}, bf16[256,256]{1,0:T(8,128)(2,1)S(1)}, u32[]{:S(2)}, u32[]{:S(2)}) %collective-permute-start.3) | collective-permute-done | bytes 131104 | tf_op jit(solution)/shard_map/ppermute | solution.py:34
  20.3 1.6 %collective-permute-start.5 = (bf16[256,256]{1,0:T(8,128)(2,1)S(1)}, bf16[256,256]{1,0:T(8,128)(2,1)S(1)}, u32[]{:S(2)}, u32[]{:S(2)}) collective-permute-start(bf16[256,256]{1,0:T(8,128)(2,1)S(1)} %add_convert_fusion.3), channel_id=1, source_target_pairs={{0,1},{1,0},{2,3},{3,2},{4,6},{5,7},{6,4},{7,5},{8,9},{9,8},{10,11... | collective-permute-start | bytes 393224 | tf_op jit(solution)/shard_map/ppermute | solution.py:34
  22.0 1.7 %keep.3.refs_3_ = bf16[2,4,256,256]{3,2,1,0:T(8,128)(2,1)S(1)} custom-call(s32[1]{0:T(128)} %bitcast.11.place_ref, bf16[2,4,2048,256]{3,2,1,0:T(8,128)(2,1)} %bitcast.20, bf16[2,4,2048,256]{3,2,1,0:T(8,128)(2,1)} %bitcast.25), custom_call_target="tpu_custom_call" | custom-call | flops 1000000 | tf_op jit(solution)/shard_map/keep/pallas_call | solution.py:162
  23.6 1.9 %collective-permute-done.5 = bf16[256,256]{1,0:T(8,128)(2,1)S(1)} collective-permute-done((bf16[256,256]{1,0:T(8,128)(2,1)S(1)}, bf16[256,256]{1,0:T(8,128)(2,1)S(1)}, u32[]{:S(2)}, u32[]{:S(2)}) %collective-permute-start.5) | collective-permute-done | bytes 131104 | tf_op jit(solution)/shard_map/ppermute | solution.py:34
  25.5 2.9 %collective-permute-start.6 = (bf16[256,256]{1,0:T(8,128)(2,1)S(1)}, bf16[256,256]{1,0:T(8,128)(2,1)S(1)}, u32[]{:S(2)}, u32[]{:S(2)}) collective-permute-start(bf16[256,256]{1,0:T(8,128)(2,1)S(1)} %add_convert_fusion.2), channel_id=1, source_target_pairs={{0,2},{1,3},{2,0},{3,1},{4,5},{5,4},{6,7},{7,6},{8,10},{9,11},{10,... | collective-permute-start | bytes 393224 | tf_op jit(solution)/shard_map/ppermute | solution.py:34
  28.5 2.9 %keep.4.refs_4_ = bf16[2,4,512,256]{3,2,1,0:T(8,128)(2,1)S(1)} custom-call(s32[2]{0:T(128)S(1)} %pad_add_fusion.1.place_ref, bf16[2,4,2048,256]{3,2,1,0:T(8,128)(2,1)} %bitcast.21, bf16[2,4,2048,256]{3,2,1,0:T(8,128)(2,1)} %bitcast.26), custom_call_target="tpu_custom_call" | custom-call | flops 1000000 | tf_op jit(solution)/shard_map/keep/pallas_call | solution.py:162
  31.6 1.5 %collective-permute-start.9 = (bf16[256,256]{1,0:T(8,128)(2,1)S(1)}, bf16[256,256]{1,0:T(8,128)(2,1)S(1)}, u32[]{:S(2)}, u32[]{:S(2)}) collective-permute-start(bf16[256,256]{1,0:T(8,128)(2,1)S(1)} %add_convert_fusion.1.refs_0_), channel_id=1, source_target_pairs={{0,24},{1,25},{2,26},{3,27},{4,28},{5,29},{6,30},{7,31},{8,16},{9,... | collective-permute-start | bytes 393224 | tf_op jit(solution)/shard_map/ppermute | solution.py:34
  33.1 1.5 %collective-permute-start.8 = (bf16[256,256]{1,0:T(8,128)(2,1)S(1)}, bf16[256,256]{1,0:T(8,128)(2,1)S(1)}, u32[]{:S(2)}, u32[]{:S(2)}) collective-permute-start(bf16[256,256]{1,0:T(8,128)(2,1)S(1)} %add_convert_fusion.1.refs_0_), channel_id=1, source_target_pairs={{0,16},{1,17},{2,18},{3,19},{4,20},{5,21},{6,22},{7,23},{8,24},{9,... | collective-permute-start | bytes 393224 | tf_op jit(solution)/shard_map/ppermute | solution.py:34
  34.6 0.5 collective-permute-start.7
  35.2 3.5 %keep.5.refs_3_ = bf16[2,4,768,256]{3,2,1,0:T(8,128)(2,1)S(1)} custom-call(s32[3]{0:T(128)S(1)} %pad_add_fusion.2.place_ref, bf16[2,4,2048,256]{3,2,1,0:T(8,128)(2,1)} %bitcast.22, bf16[2,4,2048,256]{3,2,1,0:T(8,128)(2,1)} %bitcast.27), custom_call_target="tpu_custom_call" | custom-call | flops 1000000 | tf_op jit(solution)/shard_map/keep/pallas_call | solution.py:162
  38.8 0.5 project.3
  39.5 1.7 %collective-permute-done.8.refs_1_ = bf16[256,256]{1,0:T(8,128)(2,1)S(1)} collective-permute-done((bf16[256,256]{1,0:T(8,128)(2,1)S(1)}, bf16[256,256]{1,0:T(8,128)(2,1)S(1)}, u32[]{:S(2)}, u32[]{:S(2)}) %collective-permute-start.8) | collective-permute-done | bytes 131104 | tf_op jit(solution)/shard_map/ppermute | solution.py:34
  41.2 0.5 collective-permute-start.11
  41.8 0.8 %project.4 = (f32[2,32,256]{2,1,0:T(8,128)S(1)}, f32[3,2,32,32]{3,2,1,0:T(8,128)S(1)}) custom-call(bf16[256,256]{1,0:T(8,128)(2,1)S(1)} %collective-permute-done.7.refs_0_, bf16[256,256]{1,0:T(8,128)(2,1)S(1)} %collective-permute-done.8.refs_1_, bf16[256,256]{1,0:T(8,128)(2,1)S(1)} %collective-permute-done.9.refs_2_, ...), custom_call_target="tpu_custom_call" | custom-call | flops 1000000 | tf_op jit(solution)/shard_map/project/pallas_call | solution.py:204
  42.6 0.2 collective-permute-done.11.refs_0_
  42.7 0.8 %project.5 = (f32[2,32,256]{2,1,0:T(8,128)S(1)}, f32[3,2,32,32]{3,2,1,0:T(8,128)S(1)}) custom-call(bf16[256,256]{1,0:T(8,128)(2,1)S(1)} %collective-permute-done.11.refs_0_, bf16[256,256]{1,0:T(8,128)(2,1)S(1)} %collective-permute-done.12.refs_1_, bf16[256,256]{1,0:T(8,128)(2,1)S(1)} %collective-permute-done.13.refs_2_, ...), custom_call_target="tpu_custom_call" | custom-call | flops 1000000 | tf_op jit(solution)/shard_map/project/pallas_call | solution.py:204
  43.5 0.4 collective-permute-start.14
  43.9 0.7 %invert.2.refs_0_ = f32[2,32,32]{2,1,0:T(8,128)S(1)} custom-call(f32[2,2,32,32]{3,2,1,0:T(8,128)S(1)} %get-tuple-element.64.refs_0_, f32[3,2,32,32]{3,2,1,0:T(8,128)S(1)} %get-tuple-element.65.refs_1_, f32[3,2,32,32]{3,2,1,0:T(8,128)S(1)} %get-tuple-element.66.refs_2_), custom_call_target="tpu_custom_call" | custom-call | flops 1000000 | tf_op jit(solution)/shard_map/invert/pallas_call | solution.py:243
  44.6 0.2 collective-permute-done.14
  44.8 1.5 %collective-permute-start.17 = (f32[2,32,256]{2,1,0:T(8,128)S(1)}, f32[2,32,256]{2,1,0:T(8,128)S(1)}, u32[]{:S(2)}, u32[]{:S(2)}) collective-permute-start(f32[2,32,256]{2,1,0:T(8,128)S(1)} %add.104), channel_id=1, source_target_pairs={{0,24},{1,25},{2,26},{3,27},{4,28},{5,29},{6,30},{7,31},{8,16},{9,... | collective-permute-start | bytes 196616 | tf_op jit(solution)/shard_map/ppermute | solution.py:34
  46.3 0.7 %collective-permute-start.16 = (f32[2,32,256]{2,1,0:T(8,128)S(1)}, f32[2,32,256]{2,1,0:T(8,128)S(1)}, u32[]{:S(2)}, u32[]{:S(2)}) collective-permute-start(f32[2,32,256]{2,1,0:T(8,128)S(1)} %add.104), channel_id=1, source_target_pairs={{0,16},{1,17},{2,18},{3,19},{4,20},{5,21},{6,22},{7,23},{8,24},{9,... | collective-permute-start | bytes 196616 | tf_op jit(solution)/shard_map/ppermute | solution.py:34
  47.1 1.3 %collective-permute-start.15 = (f32[2,32,256]{2,1,0:T(8,128)S(1)}, f32[2,32,256]{2,1,0:T(8,128)S(1)}, u32[]{:S(2)}, u32[]{:S(2)}) collective-permute-start(f32[2,32,256]{2,1,0:T(8,128)S(1)} %add.104), channel_id=1, source_target_pairs={{0,8},{1,9},{2,10},{3,11},{4,12},{5,13},{6,14},{7,15},{8,0},{9,1},... | collective-permute-start | bytes 196616 | tf_op jit(solution)/shard_map/ppermute | solution.py:34
  48.4 2.0 %invert.3.refs_1_ = f32[2,32,32]{2,1,0:T(8,128)S(1)} custom-call(f32[2,32,32]{2,1,0:T(8,128)S(1)} %invert.2.refs_0_), custom_call_target="tpu_custom_call" | custom-call | flops 1000000 | tf_op jit(solution)/shard_map/invert/pallas_call | solution.py:243
  50.4 1.1 %collective-permute-done.16 = f32[2,32,256]{2,1,0:T(8,128)S(1)} collective-permute-done((f32[2,32,256]{2,1,0:T(8,128)S(1)}, f32[2,32,256]{2,1,0:T(8,128)S(1)}, u32[]{:S(2)}, u32[]{:S(2)}) %collective-permute-start.16) | collective-permute-done | bytes 65568 | tf_op jit(solution)/shard_map/ppermute | solution.py:34
  51.5 4.1 %expand.1 = bf16[2,4,2048,256]{3,2,1,0:T(8,128)(2,1)} custom-call(bf16[2048,256]{1,0:T(8,128)(2,1)S(1)} %constant_dynamic-update-slice_fusion.refs_0_, f32[2,32,32]{2,1,0:T(8,128)S(1)} %invert.3.refs_1_, f32[2,32,256]{2,1,0:T(8,128)S(1)} %add_add_fusion.refs_2_), custom_call_target="tpu_custom_call" | custom-call | tf_op jit(solution)/shard_map/expand/pallas_call | solution.py:300
  (35 shorter events, 1.2 us)
Async XLA Ops:
  6.0 1.9 %collective-permute-start = (bf16[768,256]{1,0:T(8,128)(2,1)S(1)}, bf16[768,256]{1,0:T(8,128)(2,1)S(1)}, u32[]{:S(2)}, u32[]{:S(2)}) collective-permute-start(bf16[768,256]{1,0:T(8,128)(2,1)S(1)} %get-tuple-element.38), channel_id=1, source_target_pairs={{0,4},{1,5},{2,6},{3,7},{4,0},{5,1},{6,2},{7,3},{8,12},{9,13},{10,... | collective-permute-start | bytes 1179656 | tf_op jit(solution)/shard_map/ppermute | solution.py:34
  8.0 7.9 %collective-permute-start.2 = (bf16[256,256]{1,0:T(8,128)(2,1)S(1)}, bf16[256,256]{1,0:T(8,128)(2,1)S(1)}, u32[]{:S(2)}, u32[]{:S(2)}) collective-permute-start(bf16[256,256]{1,0:T(8,128)(2,1)S(1)} %get-tuple-element.69), channel_id=1, source_target_pairs={{0,8},{1,9},{2,10},{3,11},{4,12},{5,13},{6,14},{7,15},{8,0},{9,1},... | collective-permute-start | bytes 393224 | tf_op jit(solution)/shard_map/ppermute | solution.py:34
  11.0 7.9 %collective-permute-start.4 = (bf16[256,256]{1,0:T(8,128)(2,1)S(1)}, bf16[256,256]{1,0:T(8,128)(2,1)S(1)}, u32[]{:S(2)}, u32[]{:S(2)}) collective-permute-start(bf16[256,256]{1,0:T(8,128)(2,1)S(1)} %get-tuple-element.70), channel_id=1, source_target_pairs={{0,24},{1,25},{2,26},{3,27},{4,28},{5,29},{6,30},{7,31},{8,16},{9,... | collective-permute-start | bytes 393224 | tf_op jit(solution)/shard_map/ppermute | solution.py:34
  12.5 7.8 %collective-permute-start.3 = (bf16[256,256]{1,0:T(8,128)(2,1)S(1)}, bf16[256,256]{1,0:T(8,128)(2,1)S(1)}, u32[]{:S(2)}, u32[]{:S(2)}) collective-permute-start(bf16[256,256]{1,0:T(8,128)(2,1)S(1)} %get-tuple-element.71), channel_id=1, source_target_pairs={{0,16},{1,17},{2,18},{3,19},{4,20},{5,21},{6,22},{7,23},{8,24},{9,... | collective-permute-start | bytes 393224 | tf_op jit(solution)/shard_map/ppermute | solution.py:34
  15.8 4.4 %collective-permute-start.1 = (bf16[256,256]{1,0:T(8,128)(2,1)S(1)}, bf16[256,256]{1,0:T(8,128)(2,1)S(1)}, u32[]{:S(2)}, u32[]{:S(2)}) collective-permute-start(bf16[256,256]{1,0:T(8,128)(2,1)S(1)} %get-tuple-element.42), channel_id=1, source_target_pairs={{0,4},{1,5},{2,6},{3,7},{4,0},{5,1},{6,2},{7,3},{8,12},{9,13},{10,... | collective-permute-start | bytes 393224 | tf_op jit(solution)/shard_map/ppermute | solution.py:34
  20.3 5.2 %collective-permute-start.5 = (bf16[256,256]{1,0:T(8,128)(2,1)S(1)}, bf16[256,256]{1,0:T(8,128)(2,1)S(1)}, u32[]{:S(2)}, u32[]{:S(2)}) collective-permute-start(bf16[256,256]{1,0:T(8,128)(2,1)S(1)} %add_convert_fusion.3), channel_id=1, source_target_pairs={{0,1},{1,0},{2,3},{3,2},{4,6},{5,7},{6,4},{7,5},{8,9},{9,8},{10,11... | collective-permute-start | bytes 393224 | tf_op jit(solution)/shard_map/ppermute | solution.py:34
  25.5 5.9 %collective-permute-start.6 = (bf16[256,256]{1,0:T(8,128)(2,1)S(1)}, bf16[256,256]{1,0:T(8,128)(2,1)S(1)}, u32[]{:S(2)}, u32[]{:S(2)}) collective-permute-start(bf16[256,256]{1,0:T(8,128)(2,1)S(1)} %add_convert_fusion.2), channel_id=1, source_target_pairs={{0,2},{1,3},{2,0},{3,1},{4,5},{5,4},{6,7},{7,6},{8,10},{9,11},{10,... | collective-permute-start | bytes 393224 | tf_op jit(solution)/shard_map/ppermute | solution.py:34
  31.5 7.3 %collective-permute-start.10 = (bf16[256,256]{1,0:T(8,128)(2,1)S(1)}, bf16[256,256]{1,0:T(8,128)(2,1)S(1)}, u32[]{:S(2)}, u32[]{:S(2)}) collective-permute-start(bf16[256,256]{1,0:T(8,128)(2,1)S(1)} %add_convert_fusion.1.refs_0_), channel_id=1, source_target_pairs={{0,4},{1,5},{2,6},{3,7},{4,0},{5,1},{6,2},{7,3},{8,12},{9,13},{10,... | collective-permute-start | bytes 393224 | tf_op jit(solution)/shard_map/ppermute | solution.py:34
  31.6 7.8 %collective-permute-start.9 = (bf16[256,256]{1,0:T(8,128)(2,1)S(1)}, bf16[256,256]{1,0:T(8,128)(2,1)S(1)}, u32[]{:S(2)}, u32[]{:S(2)}) collective-permute-start(bf16[256,256]{1,0:T(8,128)(2,1)S(1)} %add_convert_fusion.1.refs_0_), channel_id=1, source_target_pairs={{0,24},{1,25},{2,26},{3,27},{4,28},{5,29},{6,30},{7,31},{8,16},{9,... | collective-permute-start | bytes 393224 | tf_op jit(solution)/shard_map/ppermute | solution.py:34
  33.1 8.1 %collective-permute-start.8 = (bf16[256,256]{1,0:T(8,128)(2,1)S(1)}, bf16[256,256]{1,0:T(8,128)(2,1)S(1)}, u32[]{:S(2)}, u32[]{:S(2)}) collective-permute-start(bf16[256,256]{1,0:T(8,128)(2,1)S(1)} %add_convert_fusion.1.refs_0_), channel_id=1, source_target_pairs={{0,16},{1,17},{2,18},{3,19},{4,20},{5,21},{6,22},{7,23},{8,24},{9,... | collective-permute-start | bytes 393224 | tf_op jit(solution)/shard_map/ppermute | solution.py:34
  34.6 6.6 %collective-permute-start.7 = (bf16[256,256]{1,0:T(8,128)(2,1)S(1)}, bf16[256,256]{1,0:T(8,128)(2,1)S(1)}, u32[]{:S(2)}, u32[]{:S(2)}) collective-permute-start(bf16[256,256]{1,0:T(8,128)(2,1)S(1)} %add_convert_fusion.1.refs_0_), channel_id=1, source_target_pairs={{0,8},{1,9},{2,10},{3,11},{4,12},{5,13},{6,14},{7,15},{8,0},{9,1},... | collective-permute-start | bytes 393224 | tf_op jit(solution)/shard_map/ppermute | solution.py:34
  39.4 3.4 %collective-permute-start.13 = (bf16[256,256]{1,0:T(8,128)(2,1)S(1)}, bf16[256,256]{1,0:T(8,128)(2,1)S(1)}, u32[]{:S(2)}, u32[]{:S(2)}) collective-permute-start(bf16[256,256]{1,0:T(8,128)(2,1)S(1)} %collective-permute-done.9.refs_2_), channel_id=1, source_target_pairs={{0,4},{1,5},{2,6},{3,7},{4,0},{5,1},{6,2},{7,3},{8,12},{9,13},{10,... | collective-permute-start | bytes 393224 | tf_op jit(solution)/shard_map/ppermute | solution.py:34
  41.2 1.4 %collective-permute-start.12 = (bf16[256,256]{1,0:T(8,128)(2,1)S(1)}, bf16[256,256]{1,0:T(8,128)(2,1)S(1)}, u32[]{:S(2)}, u32[]{:S(2)}) collective-permute-start(bf16[256,256]{1,0:T(8,128)(2,1)S(1)} %collective-permute-done.8.refs_1_), channel_id=1, source_target_pairs={{0,4},{1,5},{2,6},{3,7},{4,0},{5,1},{6,2},{7,3},{8,12},{9,13},{10,... | collective-permute-start | bytes 393224 | tf_op jit(solution)/shard_map/ppermute | solution.py:34
  41.2 1.5 %collective-permute-start.11 = (bf16[256,256]{1,0:T(8,128)(2,1)S(1)}, bf16[256,256]{1,0:T(8,128)(2,1)S(1)}, u32[]{:S(2)}, u32[]{:S(2)}) collective-permute-start(bf16[256,256]{1,0:T(8,128)(2,1)S(1)} %collective-permute-done.7.refs_0_), channel_id=1, source_target_pairs={{0,4},{1,5},{2,6},{3,7},{4,0},{5,1},{6,2},{7,3},{8,12},{9,13},{10,... | collective-permute-start | bytes 393224 | tf_op jit(solution)/shard_map/ppermute | solution.py:34
  43.5 1.3 %collective-permute-start.14 = (f32[2,32,256]{2,1,0:T(8,128)S(1)}, f32[2,32,256]{2,1,0:T(8,128)S(1)}, u32[]{:S(2)}, u32[]{:S(2)}) collective-permute-start(f32[2,32,256]{2,1,0:T(8,128)S(1)} %get-tuple-element.63), channel_id=1, source_target_pairs={{0,4},{1,5},{2,6},{3,7},{4,0},{5,1},{6,2},{7,3},{8,12},{9,13},{10,... | collective-permute-start | bytes 196616 | tf_op jit(solution)/shard_map/ppermute | solution.py:34
  44.8 5.6 %collective-permute-start.17 = (f32[2,32,256]{2,1,0:T(8,128)S(1)}, f32[2,32,256]{2,1,0:T(8,128)S(1)}, u32[]{:S(2)}, u32[]{:S(2)}) collective-permute-start(f32[2,32,256]{2,1,0:T(8,128)S(1)} %add.104), channel_id=1, source_target_pairs={{0,24},{1,25},{2,26},{3,27},{4,28},{5,29},{6,30},{7,31},{8,16},{9,... | collective-permute-start | bytes 196616 | tf_op jit(solution)/shard_map/ppermute | solution.py:34
  46.3 5.2 %collective-permute-start.16 = (f32[2,32,256]{2,1,0:T(8,128)S(1)}, f32[2,32,256]{2,1,0:T(8,128)S(1)}, u32[]{:S(2)}, u32[]{:S(2)}) collective-permute-start(f32[2,32,256]{2,1,0:T(8,128)S(1)} %add.104), channel_id=1, source_target_pairs={{0,16},{1,17},{2,18},{3,19},{4,20},{5,21},{6,22},{7,23},{8,24},{9,... | collective-permute-start | bytes 196616 | tf_op jit(solution)/shard_map/ppermute | solution.py:34
  47.1 4.4 %collective-permute-start.15 = (f32[2,32,256]{2,1,0:T(8,128)S(1)}, f32[2,32,256]{2,1,0:T(8,128)S(1)}, u32[]{:S(2)}, u32[]{:S(2)}) collective-permute-start(f32[2,32,256]{2,1,0:T(8,128)S(1)} %add.104), channel_id=1, source_target_pairs={{0,8},{1,9},{2,10},{3,11},{4,12},{5,13},{6,14},{7,15},{8,0},{9,1},... | collective-permute-start | bytes 196616 | tf_op jit(solution)/shard_map/ppermute | solution.py:34
